TPU v7x, 512 devices: a whole 4x4x16 slice. The times are simulated.
512 devices in a mesh: src: 16 (over x, z_hi), shard: 32 (over y, z_lo, core).
Axes of the slice: x: 4, y: 4, z: 16 (z_hi: 4, z_lo: 4; z = z_hi * 4 + z_lo), core: 2. Of those that a mesh axis runs over, the one named last changes fastest.
Arguments:
- weights: bfloat16 [16, 4096, 14848], P('src', None, 'shard'), may hold values from -0.09375 to 0.09375
- calib_pool: bfloat16 [512, 4096], P(('src', 'shard')), may hold values from -6 to 6
- cand_index: int32 [4, 16], replicated, may hold values from 0 to 15
- coef_table: float32 [16], replicated, may hold values from 0.05 to 0.6
- row_ids: int32 [512], replicated, may hold values from 0 to 511
Outputs:
- acts: bfloat16 [512, 4, 14848], P('src', None, 'shard')
All inputs are finite; a program needn't handle non-finite values.
Results may differ from a plain program's by a relative error of at most 0.001.
Values may be sent and summed in bfloat16 or wider, within the bound.
No kernel may reach another device: no remote copies, remote signals or barrier semaphores. Data moves between devices by JAX's collectives and lax.ppermute only.
A program may use at most 128 MiB of HBM per device.

v0:
```python
import jax
import jax.numpy as jnp
from jax import lax
from jax.sharding import PartitionSpec as P


def on_device(weights, calib_pool, cand_index, coef_table, row_ids):
    gathered = lax.all_gather(calib_pool, ("src", "shard"), axis=0, tiled=True)
    calib_rows = jnp.take(gathered, row_ids, axis=0)
    entries = jnp.arange(coef_table.shape[0], dtype=jnp.int32)
    onehot = (cand_index[:, :, None] == entries[None, None, :]).astype(jnp.float32)
    coefficient = jnp.sum(onehot * coef_table[None, None, :], axis=2)
    w_piece = weights[0]
    own_coefs = lax.dynamic_index_in_dim(coefficient, lax.axis_index("src"), 1, keepdims=False)
    partial_value = jnp.dot(calib_rows, w_piece, preferred_element_type=jnp.float32)
    summed = lax.psum_scatter(
        partial_value[:, None, :] * own_coefs[None, :, None], "src", scatter_dimension=0, tiled=True
    )
    return summed.astype(jnp.bfloat16)


def solution(mesh):
    placed = (P("src", None, "shard"), P(("src", "shard"), None), P(), P(), P())
    return jax.shard_map(
        on_device, mesh=mesh, in_specs=placed, out_specs=P("src", None, "shard"), check_vma=False
    )
```

profile of v0, /device:TPU:30, one launch (start us, length us, event | category | flops | bytes accessed | tf_op | source)
XLA Modules:
  0.0 1251.3 jit_solution(1330472164557593438)
XLA Ops:
  6.5 0.0 all-gather.3.cloned.1.call-start
  6.5 0.7 all-gather.3.cloned.1.call-update
  7.3 0.9 select_reduce_fusion
  8.1 0.2 dynamic-slice_reduce_fusion
  8.3 1.3 dynamic-slice
  10.2 0.7 compare_select_fusion
  10.9 0.7 compare_and_fusion
  11.6 822.3 %all-gather.3.cloned.1.call-done = bf16[512,1,4096]{2,1,0:T(2,128)(2,1)} async-done(((bf16[1,1,4096]{2,1,0:T(2,128)(2,1)}), bf16[512,1,4096]{2,1,0:T(2,128)(2,1)}) %all-gather.3.cloned.1.call-update) | async-done | bytes 4194320 | tf_op jit(solution)/shard_map/all_gather | solution.py:8
  833.9 10.1 copy.14
  844.0 11.3 gather_fusion
  855.3 5.7 fusion
  861.0 2.7 broadcast_multiply_fusion
  863.7 380.0 %all-reduce.2 = bf16[512,4,464]{2,1,0:T(4,128)(2,1)S(1)} all-reduce(f32[512,4,464]{2,1,0:T(4,128)} %broadcast_multiply_fusion), channel_id=2, replica_groups=mesh['src'=16,'shard'=32] {'src'}, use_global_device_ids=true, to_apply=%region_1.2.clone | all-reduce | flops 950272 | bytes 5701632
  1243.8 0.7 dynamic-slice_convert_fusion
  (1 shorter events, 0.0 us)
Async XLA Ops:
  6.5 827.4 %all-gather.3.cloned.1.call-start = ((), (), s32[]{:S(2)}) async-start(), calls=%async_computation | async-start | bytes 8404992 | tf_op jit(solution)/shard_map/all_gather | solution.py:8
Sparse Core Ops, SparseCore 0:
  9.6 824.2 all-gather.2
where the time goes:
time: 1250 us
  waiting for transfers between devices  823 us (66%)
  blocking collectives  380 us (30%)
  local copies, waits for them, and re-layouts  23.5 us (2%)
  between operations  14.1 us (1%)
    all_gather x1, waiting for transfers between devices, on_device(): gathered = lax.all_gather(calib_pool, ('src', 'shard'), axis=0, tiled=True)  822 us
    unnamed x1, blocking collectives  380 us
  transfers between devices with their start and end apart: 1, of which 1 were waited for; matrix products, arithmetic and copies ran while one was open for 0% of the time, Pallas kernels for 0%

commit v1 on v0

v1 whole, which is shorter than its diff:
```python
import jax
import jax.numpy as jnp
from jax import lax
from jax.sharding import Mesh, PartitionSpec as P

BF16, F32, I16, I32 = jnp.bfloat16, jnp.float32, jnp.int16, jnp.int32
LANES = 512
TOP = 32767.0


def spread(block, axes, count):
    copies = jnp.broadcast_to(block[None], (count,) + block.shape)
    return lax.all_to_all(copies, axes, 0, 0)


def encode(partial):
    top = jnp.max(jnp.abs(partial), axis=1, keepdims=True)
    power = jnp.clip(jnp.floor(jnp.log2(top)), -80.0, 80.0)
    mantissa = jnp.ceil(top * jnp.exp2(-power) * 8192.0) + 1.0
    step = mantissa * jnp.exp2(power) * (1.0 / (8192.0 * TOP))
    codes = jnp.clip(jnp.round(partial / step), -TOP, TOP)
    rows, width = partial.shape
    column = lax.broadcasted_iota(I32, (rows, LANES), 1)
    codes = jnp.pad(codes, ((0, 0), (0, LANES - width)))
    codes = jnp.where(column == width, mantissa, codes)
    return jnp.where(column == width + 1, power, codes)


def on_device(weights, calib_pool, cand_index, coef_table, row_ids):
    core = lax.axis_index("c")
    own = spread(calib_pool.reshape(32, 128), ("zh", "zl"), 16).reshape(16, 4096)
    own = spread(own, ("x", "y"), 16).reshape(256, 4096)
    other = lax.ppermute(own, "c", [(0, 1), (1, 0)])
    w_piece = weights[0]
    mine = jnp.dot(own, w_piece, preferred_element_type=F32)
    others = jnp.dot(other, w_piece, preferred_element_type=F32)
    partial = jnp.concatenate([mine, others], axis=0)
    width = partial.shape[1]

    codes = encode(partial)
    high = jnp.floor(codes * (1.0 / 256.0))
    low = codes - high * 256.0
    x, zh, y, zl, c = (row_ids >> 7) & 3, (row_ids >> 5) & 3, (row_ids >> 3) & 3, (row_ids >> 1) & 3, row_ids & 1
    place = ((x * 4 + y) * 4 + zh) * 4 + zl + jnp.where(c == core, 0, 256)
    pick = (place[:, None] == lax.broadcasted_iota(I32, (512, 512), 1)).astype(BF16)
    high = jnp.dot(pick, high.astype(BF16), preferred_element_type=F32)
    low = jnp.dot(pick, low.astype(BF16), preferred_element_type=F32)
    sent = (high * 256.0 + low).astype(I32).astype(I16)
    got = lax.all_to_all(sent, ("x", "zh"), 0, 0, tiled=True).reshape(16, 32, LANES)

    entries = jnp.arange(coef_table.shape[0], dtype=I32)
    onehot = (cand_index[:, :, None] == entries[None, None, :]).astype(F32)
    coefficient = jnp.sum(onehot * coef_table[None, None, :], axis=2)
    got = got.astype(F32)
    step = got[:, :, width] * jnp.exp2(got[:, :, width + 1]) * (1.0 / (8192.0 * TOP))
    factor = coefficient.T[:, None, :] * step[:, :, None]
    acts = jnp.sum(factor[:, :, :, None] * got[:, :, None, :width], axis=0)
    return acts.astype(BF16)


def solution(mesh):
    fine = Mesh(mesh.devices.reshape(4, 4, 4, 4, 2), ("x", "zh", "y", "zl", "c"))
    src, shard = ("x", "zh"), ("y", "zl", "c")
    placed = (P(src, None, shard), P(src + shard, None), P(), P(), P())
    return jax.shard_map(on_device, mesh=fine, in_specs=placed, out_specs=P(src, None, shard), check_vma=False)
```

time: 1250 us -> 117 us (0.09)
  the two profiles are of different devices: /device:TPU:30 before, /device:TPU:32 now
where the time goes in v1:
time: 117 us
  blocking collectives  61.3 us (52%)
  waiting for transfers between devices  34.9 us (30%)
  starting transfers between devices  8.41 us (7%)
  matrix products  7.58 us (6%)
  local copies, waits for them, and re-layouts  2.3 us (2%)
  other arithmetic  2.13 us (2%)
    all_to_all x2, blocking collectives, spread(): return lax.all_to_all(copies, axes, 0, 0)  61.3 us
    all_to_all x1, waiting for transfers between devices, on_device(): lax.all_to_all(sent, ('x', 'zh'), 0, 0, tiled=True).reshape(16, 32, LANES)  34.1 us
    all_to_all x1, starting transfers between devices, on_device(): lax.all_to_all(sent, ('x', 'zh'), 0, 0, tiled=True).reshape(16, 32, LANES)  6.5 us
    dot_general x1, matrix products, on_device(): mine = jnp.dot(own, w_piece, preferred_element_type=F32)  3.41 us
    dot_general x1, matrix products, on_device(): others = jnp.dot(other, w_piece, preferred_element_type=F32)  2.77 us
  transfers between devices with their start and end apart: 2, of which 2 were waited for; matrix products, arithmetic and copies ran while one was open for 3% of the time, Pallas kernels for 0%

profile of v1, /device:TPU:32, one launch (start us, length us, event | category | flops | bytes accessed | tf_op | source)
XLA Modules:
  0.0 116.8 jit_solution(18364513846087708942)
XLA Ops:
  0.0 0.0 copy-start
  0.0 0.8 reduce
  0.8 29.2 %all_to_all.19 = bf16[16,32,128]{2,1,0:T(8,128)(2,1)S(1)} all-to-all(bf16[16,32,128]{2,1,0:T(8,128)(2,1)S(1)} %broadcast_in_dim.47), channel_id=1, replica_groups=mesh['x'=4,'zh'=4,'y'=4,'zl'=4,'c'=2] {'zh','zl'}, dimensions={0} | all-to-all | bytes 262144 | tf_op jit(solution)/shard_map/all_to_all | solution.py:13
  30.0 0.1 copy.27
  30.1 0.2 broadcast_in_dim.49
  30.3 32.1 %all_to_all.20 = bf16[16,16,4096]{2,1,0:T(8,128)(2,1)S(1)} all-to-all(bf16[16,16,4096]{2,1,0:T(8,128)(2,1)S(1)} %broadcast_in_dim.49), channel_id=1, replica_groups=mesh['x'=4,'zh'=4,'y'=4,'zl'=4,'c'=2] {'x','y'}, dimensions={0} | all-to-all | bytes 4194304 | tf_op jit(solution)/shard_map/all_to_all | solution.py:13
  62.4 1.9 %collective-permute-start = (bf16[256,4096]{1,0:T(8,128)(2,1)S(1)}, bf16[256,4096]{1,0:T(8,128)(2,1)}, u32[]{:S(2)}, u32[]{:S(2)}) collective-permute-start(bf16[256,4096]{1,0:T(8,128)(2,1)S(1)} %bitcast.17), channel_id=1, source_target_pairs={{0,1},{1,0},{2,3},{3,2},{4,5},{5,4},{6,7},{7,6},{8,9},{9,8},{10,11... | collective-permute-start | bytes 6291464 | tf_op jit(solution)/shard_map/ppermute | solution.py:33
  64.4 0.0 copy-start.3
  64.4 0.0 copy-done
  64.4 3.4 %fusion.2 = f32[256,464]{0,1:T(8,128)S(1)} fusion(bf16[256,4096]{1,0:T(8,128)(2,1)S(1)} %bitcast.18, bf16[1,4096,464]{1,2,0:T(8,128)(2,1)} %param.5), kind=kOutput, calls=%fused_computation.3 | convolution fusion | flops 973078528 | bytes 6373376 | tf_op jit(solution)/shard_map/dot_general | solution.py:35
  67.8 0.8 collective-permute-done
  68.6 0.0 copy-done.3
  68.6 2.8 %fusion = f32[256,464]{0,1:T(8,128)S(1)} fusion(bf16[256,4096]{1,0:T(8,128)(2,1)} %collective-permute-done, bf16[1,4096,464]{1,2,0:T(8,128)(2,1)S(1)} %copy-done.3), kind=kOutput, calls=%fused_computation.1 | convolution fusion | flops 973078528 | bytes 6373376 | tf_op jit(solution)/shard_map/dot_general | solution.py:36
  71.4 0.1 abs_reduce_fusion
  71.5 0.2 round-nearest-even_clamp_fusion
  71.6 0.0 copy-start.1
  71.6 0.0 copy-start.2
  71.7 0.7 convolution_multiply_fusion
  72.3 0.7 fusion.5
  73.1 1.1 copy.21
  74.2 6.5 %all-to-all-start.2 = ((s16[16,32,512]{2,1,0:T(8,128)(2,1)}), s16[16,32,512]{2,1,0:T(8,128)(2,1)S(1)}, u32[]{:S(2)}, u32[]{:S(2)}) async-start(s16[16,32,512]{2,1,0:T(8,128)(2,1)} %bitcast.3), calls=%async_computation.2 | async-start | bytes 1048576 | tf_op jit(solution)/shard_map/all_to_all | solution.py:49
  80.7 0.0 copy-done.1
  80.7 0.0 copy-done.2
  80.7 0.2 select_reduce_fusion
  80.9 0.1 copy.18
  81.0 34.1 %all-to-all-done.2 = s16[16,32,512]{2,1,0:T(8,128)(2,1)S(1)} async-done(((s16[16,32,512]{2,1,0:T(8,128)(2,1)}), s16[16,32,512]{2,1,0:T(8,128)(2,1)S(1)}, u32[]{:S(2)}, u32[]{:S(2)}) %all-to-all-start.2) | async-done | bytes 524320 | tf_op jit(solution)/shard_map/all_to_all | solution.py:49
  115.1 0.2 convert_element_type.26
  115.3 0.3 fusion.24
  115.6 0.1 broadcast_multiply_fusion
  115.7 0.4 multiply_reduce_fusion
  116.1 0.8 copy.22
  (4 shorter events, 0.1 us)
Async XLA Ops:
  0.0 64.4 %copy-start = (s32[512]{0:T(512)S(1)}, s32[512]{0:T(512)}, u32[]{:S(2)}) copy-start(s32[512]{0:T(512)} %param.9) | copy-start | bytes 6148
  62.4 6.2 %collective-permute-start = (bf16[256,4096]{1,0:T(8,128)(2,1)S(1)}, bf16[256,4096]{1,0:T(8,128)(2,1)}, u32[]{:S(2)}, u32[]{:S(2)}) collective-permute-start(bf16[256,4096]{1,0:T(8,128)(2,1)S(1)} %bitcast.17), channel_id=1, source_target_pairs={{0,1},{1,0},{2,3},{3,2},{4,5},{5,4},{6,7},{7,6},{8,9},{9,8},{10,11... | collective-permute-start | bytes 6291464 | tf_op jit(solution)/shard_map/ppermute | solution.py:33
  64.4 4.3 %copy-start.3 = (bf16[1,4096,464]{1,2,0:T(8,128)(2,1)S(1)}, bf16[1,4096,464]{1,2,0:T(8,128)(2,1)}, u32[]{:S(2)}) copy-start(bf16[1,4096,464]{1,2,0:T(8,128)(2,1)} %param.5) | copy-start | bytes 11403268
  71.6 9.1 %copy-start.1 = (s32[4,16]{1,0:T(4,128)S(1)}, s32[4,16]{1,0:T(4,128)}, u32[]{:S(2)}) copy-start(s32[4,16]{1,0:T(4,128)} %param.7) | copy-start | bytes 772
  71.6 9.1 %copy-start.2 = (f32[16]{0:T(128)S(1)}, f32[16]{0:T(128)}, u32[]{:S(2)}) copy-start(f32[16]{0:T(128)} %param.8) | copy-start | bytes 196
  74.2 40.9 %all-to-all-start.2 = ((s16[16,32,512]{2,1,0:T(8,128)(2,1)}), s16[16,32,512]{2,1,0:T(8,128)(2,1)S(1)}, u32[]{:S(2)}, u32[]{:S(2)}) async-start(s16[16,32,512]{2,1,0:T(8,128)(2,1)} %bitcast.3), calls=%async_computation.2 | async-start | bytes 1048576 | tf_op jit(solution)/shard_map/all_to_all | solution.py:49

commit v2 on v1

--- a/solution.py
+++ b/solution.py
@@ -8,9 +8,18 @@
 TOP = 32767.0
 
 
-def spread(block, axes, count):
+def spread(block, axes, count, groups=None):
     copies = jnp.broadcast_to(block[None], (count,) + block.shape)
-    return lax.all_to_all(copies, axes, 0, 0)
+    return lax.all_to_all(copies, axes, 0, 0, axis_index_groups=groups)
+
+
+def lines(along):
+    def at(x, y, role):
+        return (x * 4 + y) * 2 + (role + x + y) % 2
+
+    return [[at(i, j, along) for j in range(4)] for i in range(4)] + [
+        [at(i, j, 1 - along) for i in range(4)] for j in range(4)
+    ]
 
 
 def encode(partial):
@@ -28,8 +37,10 @@
 
 def on_device(weights, calib_pool, cand_index, coef_table, row_ids):
     core = lax.axis_index("c")
+    role = (core + lax.axis_index("x") + lax.axis_index("y")) % 2
     own = spread(calib_pool.reshape(32, 128), ("zh", "zl"), 16).reshape(16, 4096)
-    own = spread(own, ("x", "y"), 16).reshape(256, 4096)
+    own = spread(own, ("x", "y", "c"), 4, lines(0)).reshape(64, 4096)
+    own = spread(own, ("x", "y", "c"), 4, lines(1)).reshape(256, 4096)
     other = lax.ppermute(own, "c", [(0, 1), (1, 0)])
     w_piece = weights[0]
     mine = jnp.dot(own, w_piece, preferred_element_type=F32)
@@ -41,7 +52,8 @@
     high = jnp.floor(codes * (1.0 / 256.0))
     low = codes - high * 256.0
     x, zh, y, zl, c = (row_ids >> 7) & 3, (row_ids >> 5) & 3, (row_ids >> 3) & 3, (row_ids >> 1) & 3, row_ids & 1
-    place = ((x * 4 + y) * 4 + zh) * 4 + zl + jnp.where(c == core, 0, 256)
+    its_role = (c + x + y) & 1
+    place = jnp.where(its_role == 0, x * 4 + y, y * 4 + x) * 16 + zh * 4 + zl + jnp.where(its_role == role, 0, 256)
     pick = (place[:, None] == lax.broadcasted_iota(I32, (512, 512), 1)).astype(BF16)
     high = jnp.dot(pick, high.astype(BF16), preferred_element_type=F32)
     low = jnp.dot(pick, low.astype(BF16), preferred_element_type=F32)

time: 117 us -> 116 us (level)
  starting transfers between devices: 8.41 us -> 5.65 us
    all_to_all x1, starting transfers between devices: 6.5 us -> 3.74 us  [on_device(): lax.all_to_all(sent, ('x', 'zh'), 0, 0, tiled=True).reshape(16, 32, LANES)]
    all_to_all x2 -> x3, blocking collectives: 61.3 us -> 62.2 us  [spread(): return lax.all_to_all(copies, axes, 0, 0, axis_index_groups=groups)]
where the time goes in v2:
time: 116 us; the launch traced here: 115 us
  blocking collectives  62.2 us (54%)
  waiting for transfers between devices  35.3 us (30%)
  matrix products  7.58 us (7%)
  starting transfers between devices  5.65 us (5%)
  local copies, waits for them, and re-layouts  2.36 us (2%)
  other arithmetic  2.12 us (2%)
    all_to_all x3, blocking collectives, spread(): return lax.all_to_all(copies, axes, 0, 0, axis_index_groups=groups)  62.2 us
    all_to_all x1, waiting for transfers between devices, on_device(): lax.all_to_all(sent, ('x', 'zh'), 0, 0, tiled=True).reshape(16, 32, LANES)  34.6 us
    all_to_all x1, starting transfers between devices, on_device(): lax.all_to_all(sent, ('x', 'zh'), 0, 0, tiled=True).reshape(16, 32, LANES)  3.74 us
    dot_general x1, matrix products, on_device(): mine = jnp.dot(own, w_piece, preferred_element_type=F32)  3.41 us
    dot_general x1, matrix products, on_device(): others = jnp.dot(other, w_piece, preferred_element_type=F32)  2.77 us
  transfers between devices with their start and end apart: 2, of which 2 were waited for; matrix products, arithmetic and copies ran while one was open for 3% of the time, Pallas kernels for 0%

profile of v2, /device:TPU:32, one launch (start us, length us, event | category | flops | bytes accessed | tf_op | source)
XLA Modules:
  0.0 115.4 jit_solution(1641373378828186733)
XLA Ops:
  0.0 0.8 reduce
  0.8 29.2 %all_to_all.24 = bf16[16,32,128]{2,1,0:T(8,128)(2,1)S(1)} all-to-all(bf16[16,32,128]{2,1,0:T(8,128)(2,1)S(1)} %broadcast_in_dim.51), channel_id=1, replica_groups=mesh['x'=4,'zh'=4,'y'=4,'zl'=4,'c'=2] {'zh','zl'}, dimensions={0} | all-to-all | bytes 262144 | tf_op jit(solution)/shard_map/all_to_all | solution.py:13
  30.0 0.1 copy.27
  30.1 0.0 copy-start
  30.1 12.3 %all_to_all.25 = bf16[4,16,4096]{2,1,0:T(8,128)(2,1)S(1)} all-to-all(bf16[4,16,4096]{2,1,0:T(8,128)(2,1)S(1)} %broadcast_in_dim.53), channel_id=1, replica_groups={{0,9,16,25},{129,136,145,152},{256,265,272,281},{385,392,401,408},{1,12..., dimensions={0} | all-to-all | bytes 1048576 | tf_op jit(solution)/shard_map/all_to_all | solution.py:13
  42.5 0.2 broadcast_in_dim.55
  42.7 20.6 %all_to_all.26 = bf16[4,64,4096]{2,1,0:T(8,128)(2,1)S(1)} all-to-all(bf16[4,64,4096]{2,1,0:T(8,128)(2,1)S(1)} %broadcast_in_dim.55), channel_id=1, replica_groups={{1,8,17,24},{128,137,144,153},{257,264,273,280},{384,393,400,409},{0,12..., dimensions={0} | all-to-all | bytes 4194304 | tf_op jit(solution)/shard_map/all_to_all | solution.py:13
  63.3 1.9 %collective-permute-start = (bf16[256,4096]{1,0:T(8,128)(2,1)S(1)}, bf16[256,4096]{1,0:T(8,128)(2,1)}, u32[]{:S(2)}, u32[]{:S(2)}) collective-permute-start(bf16[256,4096]{1,0:T(8,128)(2,1)S(1)} %bitcast.19), channel_id=1, source_target_pairs={{0,1},{1,0},{2,3},{3,2},{4,5},{5,4},{6,7},{7,6},{8,9},{9,8},{10,11... | collective-permute-start | bytes 6291464 | tf_op jit(solution)/shard_map/ppermute | solution.py:44
  65.3 0.0 copy-start.3
  65.3 0.0 copy-done
  65.3 3.4 %fusion.2 = f32[256,464]{0,1:T(8,128)S(1)} fusion(bf16[256,4096]{1,0:T(8,128)(2,1)S(1)} %bitcast.20, bf16[1,4096,464]{1,2,0:T(8,128)(2,1)} %param.5), kind=kOutput, calls=%fused_computation.3 | convolution fusion | flops 973078528 | bytes 6373376 | tf_op jit(solution)/shard_map/dot_general | solution.py:46
  68.7 0.8 collective-permute-done
  69.5 0.0 copy-done.3
  69.5 2.8 %fusion = f32[256,464]{0,1:T(8,128)S(1)} fusion(bf16[256,4096]{1,0:T(8,128)(2,1)} %collective-permute-done, bf16[1,4096,464]{1,2,0:T(8,128)(2,1)S(1)} %copy-done.3), kind=kOutput, calls=%fused_computation.1 | convolution fusion | flops 973078528 | bytes 6373376 | tf_op jit(solution)/shard_map/dot_general | solution.py:47
  72.3 0.1 abs_reduce_fusion
  72.4 0.2 round-nearest-even_clamp_fusion
  72.5 0.0 copy-start.1
  72.5 0.0 copy-start.2
  72.5 0.7 convolution_multiply_fusion
  73.2 0.7 fusion.5
  74.0 1.1 copy.21
  75.1 3.7 %all-to-all-start.3 = ((s16[16,32,512]{2,1,0:T(8,128)(2,1)}), s16[16,32,512]{2,1,0:T(8,128)(2,1)S(1)}, u32[]{:S(2)}, u32[]{:S(2)}) async-start(s16[16,32,512]{2,1,0:T(8,128)(2,1)} %bitcast.4), calls=%async_computation.3 | async-start | bytes 1048576 | tf_op jit(solution)/shard_map/all_to_all | solution.py:61
  78.8 0.0 copy-done.1
  78.9 0.0 copy-done.2
  78.9 0.2 select_reduce_fusion
  79.0 0.1 copy.18
  79.1 34.6 %all-to-all-done.3 = s16[16,32,512]{2,1,0:T(8,128)(2,1)S(1)} async-done(((s16[16,32,512]{2,1,0:T(8,128)(2,1)}), s16[16,32,512]{2,1,0:T(8,128)(2,1)S(1)}, u32[]{:S(2)}, u32[]{:S(2)}) %all-to-all-start.3) | async-done | bytes 524320 | tf_op jit(solution)/shard_map/all_to_all | solution.py:61
  113.7 0.2 convert_element_type.26
  113.8 0.3 fusion.24
  114.2 0.1 broadcast_multiply_fusion
  114.3 0.4 multiply_reduce_fusion
  114.6 0.8 copy.22
  (5 shorter events, 0.1 us)
Async XLA Ops:
  30.1 35.2 %copy-start = (s32[512]{0:T(512)S(1)}, s32[512]{0:T(512)}, u32[]{:S(2)}) copy-start(s32[512]{0:T(512)} %param.9) | copy-start | bytes 6148
  63.3 6.2 %collective-permute-start = (bf16[256,4096]{1,0:T(8,128)(2,1)S(1)}, bf16[256,4096]{1,0:T(8,128)(2,1)}, u32[]{:S(2)}, u32[]{:S(2)}) collective-permute-start(bf16[256,4096]{1,0:T(8,128)(2,1)S(1)} %bitcast.19), channel_id=1, source_target_pairs={{0,1},{1,0},{2,3},{3,2},{4,5},{5,4},{6,7},{7,6},{8,9},{9,8},{10,11... | collective-permute-start | bytes 6291464 | tf_op jit(solution)/shard_map/ppermute | solution.py:44
  65.3 4.2 %copy-start.3 = (bf16[1,4096,464]{1,2,0:T(8,128)(2,1)S(1)}, bf16[1,4096,464]{1,2,0:T(8,128)(2,1)}, u32[]{:S(2)}) copy-start(bf16[1,4096,464]{1,2,0:T(8,128)(2,1)} %param.5) | copy-start | bytes 11403268
  72.5 6.3 %copy-start.1 = (s32[4,16]{1,0:T(4,128)S(1)}, s32[4,16]{1,0:T(4,128)}, u32[]{:S(2)}) copy-start(s32[4,16]{1,0:T(4,128)} %param.7) | copy-start | bytes 772
  72.5 6.3 %copy-start.2 = (f32[16]{0:T(128)S(1)}, f32[16]{0:T(128)}, u32[]{:S(2)}) copy-start(f32[16]{0:T(128)} %param.8) | copy-start | bytes 196
  75.1 38.6 %all-to-all-start.3 = ((s16[16,32,512]{2,1,0:T(8,128)(2,1)}), s16[16,32,512]{2,1,0:T(8,128)(2,1)S(1)}, u32[]{:S(2)}, u32[]{:S(2)}) async-start(s16[16,32,512]{2,1,0:T(8,128)(2,1)} %bitcast.4), calls=%async_computation.3 | async-start | bytes 1048576 | tf_op jit(solution)/shard_map/all_to_all | solution.py:61

commit v3 on v1

v3 whole, which is shorter than its diff:
```python
import jax
import jax.numpy as jnp
from jax import lax
from jax.experimental import pallas as pl
from jax.experimental.pallas import tpu as pltpu
from jax.sharding import Mesh, PartitionSpec as P

BF16, F32, I16, I32 = jnp.bfloat16, jnp.float32, jnp.int16, jnp.int32
LANES = 512
TOP = 32767.0
SHIFTS = (2, 1, 3)
DEPTH = 512


def spread(block, axes, count):
    copies = jnp.broadcast_to(block[None], (count,) + block.shape)
    return lax.all_to_all(copies, axes, 0, 0)


def shifted(block, along, shift):
    def at(x, y, c):
        return (x % 4 * 4 + y % 4) * 2 + c

    pairs = [
        (at(x, y, c), at(x, y + shift, c) if c == along else at(x + shift, y, c))
        for x in range(4)
        for y in range(4)
        for c in range(2)
    ]
    return lax.ppermute(block, ("x", "y", "c"), pairs)


def swapped(block):
    return lax.ppermute(block, "c", [(0, 1), (1, 0)])


def product(rows, w_ref):
    total = None
    for at in range(0, w_ref.shape[1], DEPTH):
        block = jnp.concatenate([r[:, at : at + DEPTH] for r in rows], axis=0)
        term = lax.dot_general(
            block, w_ref[:, at : at + DEPTH], (((1,), (1,)), ((), ())), preferred_element_type=F32
        )
        total = term if total is None else total + term
    return total


def first_kernel(a, b, c, d, w_ref, out_ref):
    out_ref[...] = product((a, b, c, d), w_ref)


def encode(partial):
    rows, width = partial.shape
    top = jnp.max(jnp.abs(partial), axis=1, keepdims=True)
    power = jnp.clip(jnp.floor(jnp.log2(top)), -80.0, 80.0)
    mantissa = jnp.ceil(top * jnp.exp2(-power) * 8192.0) + 1.0
    step = mantissa * jnp.exp2(power) * (1.0 / (8192.0 * TOP))
    codes = jnp.clip(jnp.round(partial * (1.0 / step)), -TOP, TOP)
    codes = jnp.concatenate([codes, jnp.zeros((rows, LANES - width), F32)], axis=1)
    column = lax.broadcasted_iota(I32, (rows, LANES), 1)
    codes = jnp.where(column == width, mantissa, codes)
    codes = jnp.where(column == width + 1, power, codes)
    high = jnp.floor(codes * (1.0 / 256.0))
    return high.astype(BF16), (codes - high * 256.0).astype(BF16)


def second_kernel(a, b, c, d, w_ref, first_ref, place_ref, out_ref, high_ref, low_ref):
    half = first_ref.shape[0]
    high_ref[:half], low_ref[:half] = encode(first_ref[...])
    high_ref[half:], low_ref[half:] = encode(product((a, b, c, d), w_ref))
    for at in range(0, 512, 256):
        column = lax.broadcasted_iota(I32, (256, 512), 1)
        pick = jnp.where(place_ref[at : at + 256] == column, 1.0, 0.0).astype(BF16)
        high = jnp.dot(pick, high_ref[...], preferred_element_type=F32)
        low = jnp.dot(pick, low_ref[...], preferred_element_type=F32)
        out_ref[at : at + 256] = (high * 256.0 + low).astype(I32).astype(I16)


def on_device(weights, calib_pool, cand_index, coef_table, row_ids):
    core, my_x, my_y = lax.axis_index("c"), lax.axis_index("x"), lax.axis_index("y")
    w_piece = weights[0].T
    start = spread(calib_pool.reshape(32, 128), ("zh", "zl"), 16).reshape(16, 4096)
    start = jnp.concatenate([start] + [shifted(start, 0, k) for k in (1, 2, 3)], axis=0)
    own = [start] + [shifted(start, 1, k) for k in SHIFTS]
    other = [swapped(piece) for piece in own]

    width = w_piece.shape[0]
    params = pltpu.CompilerParams(vmem_limit_bytes=40 * 2**20)
    cost = pl.CostEstimate(flops=2 * 256 * 4096 * width, bytes_accessed=6 * 2**20, transcendentals=0)
    first = pl.pallas_call(
        first_kernel,
        out_shape=jax.ShapeDtypeStruct((256, width), F32),
        compiler_params=params,
        cost_estimate=cost,
        name="first",
    )(own[0], own[1], other[0], other[1], w_piece)

    x, zh, y, zl, c = (row_ids >> 7) & 3, (row_ids >> 5) & 3, (row_ids >> 3) & 3, (row_ids >> 1) & 3, row_ids & 1
    back_x, back_y = (my_x - x) & 3, (my_y - y) & 3
    inner, outer = jnp.where(c == 0, back_y, back_x), jnp.where(c == 0, back_x, back_y)
    slot = jnp.where(outer == 0, 0, jnp.where(outer == 2, 1, jnp.where(outer == 1, 2, 3)))
    place = (slot >> 1) * 256 + jnp.where(c == core, 0, 128) + (slot & 1) * 64 + inner * 16 + zh * 4 + zl

    sent = pl.pallas_call(
        second_kernel,
        out_shape=jax.ShapeDtypeStruct((512, LANES), I16),
        scratch_shapes=[pltpu.VMEM((512, LANES), BF16)] * 2,
        compiler_params=params,
        cost_estimate=cost,
        name="second",
    )(own[2], own[3], other[2], other[3], w_piece, first, place[:, None])
    got = lax.all_to_all(sent, ("x", "zh"), 0, 0, tiled=True).reshape(16, 32, LANES)

    entries = jnp.arange(coef_table.shape[0], dtype=I32)
    onehot = (cand_index[:, :, None] == entries[None, None, :]).astype(F32)
    coefficient = jnp.sum(onehot * coef_table[None, None, :], axis=2)
    got = got.astype(F32)
    step = got[:, :, width] * jnp.exp2(got[:, :, width + 1]) * (1.0 / (8192.0 * TOP))
    factor = coefficient.T[:, None, :] * step[:, :, None]
    acts = jnp.sum(factor[:, :, :, None] * got[:, :, None, :width], axis=0)
    return acts.astype(BF16)


def solution(mesh):
    fine = Mesh(mesh.devices.reshape(4, 4, 4, 4, 2), ("x", "zh", "y", "zl", "c"))
    src, shard = ("x", "zh"), ("y", "zl", "c")
    placed = (P(src, None, shard), P(src + shard, None), P(), P(), P())
    return jax.shard_map(on_device, mesh=fine, in_specs=placed, out_specs=P(src, None, shard), check_vma=False)
```

time: 117 us -> 132 us (1.13)
  the two profiles are of different devices: /device:TPU:32 before, /device:TPU:2 now
where the time goes in v3:
time: 132 us; the launch traced here: 131 us
  waiting for transfers between devices  48.2 us (37%)
  starting transfers between devices  32.9 us (25%)
  blocking collectives  29.7 us (22%)
  local copies, waits for them, and re-layouts  10.7 us (8%)
  Pallas kernels  6.55 us (5%)
  other arithmetic  2.65 us (2%)
    all_to_all x1, waiting for transfers between devices, on_device(): lax.all_to_all(sent, ('x', 'zh'), 0, 0, tiled=True).reshape(16, 32, LANES)  32.9 us
    all_to_all x1, blocking collectives, spread(): return lax.all_to_all(copies, axes, 0, 0)  29.7 us
    ppermute x6, starting transfers between devices, shifted(): return lax.ppermute(block, ('x', 'y', 'c'), pairs)  20.2 us
    ppermute x6, waiting for transfers between devices, shifted(): return lax.ppermute(block, ('x', 'y', 'c'), pairs)  15.2 us
    ppermute x4, starting transfers between devices, swapped(): return lax.ppermute(block, 'c', [(0, 1), (1, 0)])  8.15 us
    slice x2, local copies, waits for them, and re-layouts, on_device(): acts = jnp.sum(factor[:, :, :, None] * got[:, :, None, :width], axis=0)  4.77 us
    all_to_all x1, starting transfers between devices, on_device(): lax.all_to_all(sent, ('x', 'zh'), 0, 0, tiled=True).reshape(16, 32, LANES)  4.59 us
    pallas_call x1, Pallas kernels, on_device(): pl.pallas_call(second_kernel, out_shape=jax.ShapeDtypeStruct((512, LANES)...  4.1 us
  transfers between devices with their start and end apart: 11, of which 4 were waited for; matrix products, arithmetic and copies ran while one was open for 1% of the time, Pallas kernels for 2%

profile of v3, /device:TPU:2, one launch (start us, length us, event | category | flops | bytes accessed | tf_op | source)
XLA Modules:
  0.0 131.0 jit_solution(16808820916098180042)
XLA Ops:
  0.0 0.8 reduce
  0.8 29.7 %all_to_all.14 = bf16[16,32,128]{2,1,0:T(8,128)(2,1)S(1)} all-to-all(bf16[16,32,128]{2,1,0:T(8,128)(2,1)S(1)} %broadcast_in_dim.29), channel_id=1, replica_groups=mesh['x'=4,'zh'=4,'y'=4,'zl'=4,'c'=2] {'zh','zl'}, dimensions={0} | all-to-all | bytes 262144 | tf_op jit(solution)/shard_map/all_to_all | solution.py:17
  30.5 0.1 copy.24
  30.5 4.9 %collective-permute-start.2 = (bf16[16,4096]{1,0:T(8,128)(2,1)S(1)}, bf16[16,4096]{1,0:T(8,128)(2,1)S(1)}, u32[]{:S(2)}, u32[]{:S(2)}) collective-permute-start(bf16[16,4096]{1,0:T(8,128)(2,1)S(1)} %bitcast.19), channel_id=1, source_target_pairs={{0,24},{1,385},{8,0},{9,393},{16,8},{17,401},{24,16},{25,409},{128... | collective-permute-start | bytes 393224 | tf_op jit(solution)/shard_map/ppermute | solution.py:30
  35.5 2.5 %collective-permute-start.1 = (bf16[16,4096]{1,0:T(8,128)(2,1)S(1)}, bf16[16,4096]{1,0:T(8,128)(2,1)S(1)}, u32[]{:S(2)}, u32[]{:S(2)}) collective-permute-start(bf16[16,4096]{1,0:T(8,128)(2,1)S(1)} %bitcast.20), channel_id=1, source_target_pairs={{0,16},{1,257},{8,24},{9,265},{16,0},{17,273},{24,8},{25,281},{128... | collective-permute-start | bytes 393224 | tf_op jit(solution)/shard_map/ppermute | solution.py:30
  38.0 2.9 %collective-permute-start = (bf16[16,4096]{1,0:T(8,128)(2,1)S(1)}, bf16[16,4096]{1,0:T(8,128)(2,1)S(1)}, u32[]{:S(2)}, u32[]{:S(2)}) collective-permute-start(bf16[16,4096]{1,0:T(8,128)(2,1)S(1)} %bitcast.21), channel_id=1, source_target_pairs={{0,8},{1,129},{8,16},{9,137},{16,24},{17,145},{24,0},{25,153},{128... | collective-permute-start | bytes 393224 | tf_op jit(solution)/shard_map/ppermute | solution.py:30
  41.0 10.8 %collective-permute-done = bf16[16,4096]{1,0:T(8,128)(2,1)S(1)} collective-permute-done((bf16[16,4096]{1,0:T(8,128)(2,1)S(1)}, bf16[16,4096]{1,0:T(8,128)(2,1)S(1)}, u32[]{:S(2)}, u32[]{:S(2)}) %collective-permute-start) | collective-permute-done | bytes 131104 | tf_op jit(solution)/shard_map/ppermute | solution.py:30
  51.7 0.0 collective-permute-done.1
  51.8 0.0 collective-permute-done.2
  51.8 4.0 %collective-permute-start.7 = (bf16[64,4096]{1,0:T(8,128)(2,1)S(1)}, bf16[64,4096]{1,0:T(8,128)(2,1)S(1)}, u32[]{:S(2)}, u32[]{:S(2)}) collective-permute-start(bf16[64,4096]{1,0:T(8,128)(2,1)S(1)} %constant_dynamic-update-slice_fusion.a), channel_id=1, source_target_pairs={{0,256},{1,17},{8,264},{9,25},{16,272},{17,1},{24,280},{25,9},{128... | collective-permute-start | bytes 1572872 | tf_op jit(solution)/shard_map/ppermute | solution.py:30
  55.8 3.3 %collective-permute-start.4 = (bf16[64,4096]{1,0:T(8,128)(2,1)S(1)}, bf16[64,4096]{1,0:T(8,128)(2,1)S(1)}, u32[]{:S(2)}, u32[]{:S(2)}) collective-permute-start(bf16[64,4096]{1,0:T(8,128)(2,1)S(1)} %constant_dynamic-update-slice_fusion.a), channel_id=1, source_target_pairs={{0,384},{1,25},{8,392},{9,1},{16,400},{17,9},{24,408},{25,17},{128... | collective-permute-start | bytes 1572872 | tf_op jit(solution)/shard_map/ppermute | solution.py:30
  59.2 2.5 %collective-permute-start.3 = (bf16[64,4096]{1,0:T(8,128)(2,1)S(1)}, bf16[64,4096]{1,0:T(8,128)(2,1)S(1)}, u32[]{:S(2)}, u32[]{:S(2)}) collective-permute-start(bf16[64,4096]{1,0:T(8,128)(2,1)S(1)} %constant_dynamic-update-slice_fusion.a), channel_id=1, source_target_pairs={{0,128},{1,9},{8,136},{9,17},{16,144},{17,25},{24,152},{25,1},{128... | collective-permute-start | bytes 1572872 | tf_op jit(solution)/shard_map/ppermute | solution.py:30
  61.7 1.9 %collective-permute-start.8 = (bf16[64,4096]{1,0:T(8,128)(2,1)S(1)}, bf16[64,4096]{1,0:T(8,128)(2,1)S(1)}, u32[]{:S(2)}, u32[]{:S(2)}) collective-permute-start(bf16[64,4096]{1,0:T(8,128)(2,1)S(1)} %constant_dynamic-update-slice_fusion.a), channel_id=1, source_target_pairs={{0,1},{1,0},{2,3},{3,2},{4,5},{5,4},{6,7},{7,6},{8,9},{9,8},{10,11... | collective-permute-start | bytes 1572872 | tf_op jit(solution)/shard_map/ppermute | solution.py:34
  63.6 0.9 collective-permute-done.7.b
  64.5 1.9 %collective-permute-start.9 = (bf16[64,4096]{1,0:T(8,128)(2,1)S(1)}, bf16[64,4096]{1,0:T(8,128)(2,1)}, u32[]{:S(2)}, u32[]{:S(2)}) collective-permute-start(bf16[64,4096]{1,0:T(8,128)(2,1)S(1)} %collective-permute-done.7.b), channel_id=1, source_target_pairs={{0,1},{1,0},{2,3},{3,2},{4,5},{5,4},{6,7},{7,6},{8,9},{9,8},{10,11... | collective-permute-start | bytes 1572872 | tf_op jit(solution)/shard_map/ppermute | solution.py:34
  66.4 3.6 %collective-permute-done.4.b = bf16[64,4096]{1,0:T(8,128)(2,1)S(1)} collective-permute-done((bf16[64,4096]{1,0:T(8,128)(2,1)S(1)}, bf16[64,4096]{1,0:T(8,128)(2,1)S(1)}, u32[]{:S(2)}, u32[]{:S(2)}) %collective-permute-start.4) | collective-permute-done | bytes 524320 | tf_op jit(solution)/shard_map/ppermute | solution.py:30
  70.0 1.9 %collective-permute-start.6 = (bf16[64,4096]{1,0:T(8,128)(2,1)S(1)}, bf16[64,4096]{1,0:T(8,128)(2,1)S(1)}, u32[]{:S(2)}, u32[]{:S(2)}) collective-permute-start(bf16[64,4096]{1,0:T(8,128)(2,1)S(1)} %collective-permute-done.4.b), channel_id=1, source_target_pairs={{0,1},{1,0},{2,3},{3,2},{4,5},{5,4},{6,7},{7,6},{8,9},{9,8},{10,11... | collective-permute-start | bytes 1572872 | tf_op jit(solution)/shard_map/ppermute | solution.py:34
  71.9 0.0 collective-permute-done.3.a
  71.9 2.4 %collective-permute-start.5 = (bf16[64,4096]{1,0:T(8,128)(2,1)S(1)}, bf16[64,4096]{1,0:T(8,128)(2,1)}, u32[]{:S(2)}, u32[]{:S(2)}) collective-permute-start(bf16[64,4096]{1,0:T(8,128)(2,1)S(1)} %collective-permute-done.3.a), channel_id=1, source_target_pairs={{0,1},{1,0},{2,3},{3,2},{4,5},{5,4},{6,7},{7,6},{8,9},{9,8},{10,11... | collective-permute-start | bytes 1572872 | tf_op jit(solution)/shard_map/ppermute | solution.py:34
  74.3 0.7 and_add_fusion
  75.0 0.1 copy.16.place_ref
  75.2 0.0 collective-permute-done.8.c
  75.2 0.0 collective-permute-done.9.d
  75.2 0.0 copy-start
  75.2 2.1 %copy-done = bf16[1,4096,464]{1,2,0:T(8,128)(2,1)S(1)} copy-done((bf16[1,4096,464]{1,2,0:T(8,128)(2,1)S(1)}, bf16[1,4096,464]{1,2,0:T(8,128)(2,1)}, u32[]{:S(2)}) %copy-start) | copy-done | bytes 3801112
  77.3 0.0 copy-start.1
  77.3 2.5 %first.1.first_ref = f32[256,464]{1,0:T(8,128)S(1)} custom-call(bf16[64,4096]{1,0:T(8,128)(2,1)S(1)} %constant_dynamic-update-slice_fusion.a, bf16[64,4096]{1,0:T(8,128)(2,1)S(1)} %collective-permute-done.7.b, bf16[64,4096]{1,0:T(8,128)(2,1)S(1)} %collective-permute-done.8.c, bf16[64,4096]{1,0:T(8,128)(2,1)} %collective-permute-done.9.d, ...), custom_call_target="tpu_custom_call" | custom-call | flops 973078528 | bytes 6291456 | tf_op jit(solution)/shard_map/first/pallas_call | solution.py:90
  79.7 0.0 copy-start.2
  79.8 0.0 copy-start.3
  79.8 0.0 collective-permute-done.6.d
  79.8 0.0 collective-permute-done.5.c
  79.8 0.0 copy-done.1
  79.8 4.1 %second.1 = s16[512,512]{1,0:T(8,128)(2,1)} custom-call(bf16[64,4096]{1,0:T(8,128)(2,1)S(1)} %collective-permute-done.3.a, bf16[64,4096]{1,0:T(8,128)(2,1)S(1)} %collective-permute-done.4.b, bf16[64,4096]{1,0:T(8,128)(2,1)} %collective-permute-done.5.c, bf16[64,4096]{1,0:T(8,128)(2,1)S(1)} %collective-permute-done.6.d, bf16[464,4096]{1,0:T(8,128)(2,1)S(1)} %bitcast.16, ...), custom_call_target="tpu_custom_call" | custom-call | flops 973078528 | bytes 6291456 | tf_op jit(solution)/shard_map/second/pallas_call | solution.py:104
  83.9 4.6 %all-to-all-start.1 = ((s16[16,32,512]{2,1,0:T(8,128)(2,1)}), s16[16,32,512]{2,1,0:T(8,128)(2,1)S(1)}, u32[]{:S(2)}, u32[]{:S(2)}) async-start(s16[16,32,512]{2,1,0:T(8,128)(2,1)} %bitcast.5), calls=%async_computation.1 | async-start | bytes 1048576 | tf_op jit(solution)/shard_map/all_to_all | solution.py:112
  88.5 0.0 copy-done.2
  88.5 0.0 copy-done.3
  88.5 0.2 select_reduce_fusion
  88.7 0.1 copy.15
  88.7 32.9 %all-to-all-done.1 = s16[16,32,512]{2,1,0:T(8,128)(2,1)S(1)} async-done(((s16[16,32,512]{2,1,0:T(8,128)(2,1)}), s16[16,32,512]{2,1,0:T(8,128)(2,1)S(1)}, u32[]{:S(2)}, u32[]{:S(2)}) %all-to-all-start.1) | async-done | bytes 524320 | tf_op jit(solution)/shard_map/all_to_all | solution.py:112
  121.7 2.7 %copy.17 = s16[16,32,512]{1,0,2:T(8,128)(2,1)S(1)} copy(s16[16,32,512]{2,1,0:T(8,128)(2,1)S(1)} %all-to-all-done.1) | data formatting | bytes 1048576 | tf_op jit(solution)/shard_map/all_to_all | solution.py:112
  124.4 0.5 convert_element_type.7
  125.0 2.1 %slice.14 = f32[16,32,464]{1,0,2:T(8,128)} slice(f32[16,32,512]{1,0,2:T(8,128)S(1)} %convert_element_type.7), slice={[0:16], [0:32], [0:464]} | slice | bytes 1900544 | tf_op jit(solution)/shard_map/slice | solution.py:120
  127.0 2.7 %copy.18 = f32[16,32,464]{2,1,0:T(8,128)S(1)} copy(f32[16,32,464]{1,0,2:T(8,128)} %slice.14) | data formatting | bytes 1900544 | tf_op jit(solution)/shard_map/slice | solution.py:120
  129.7 0.1 broadcast_multiply_fusion
  129.8 0.4 multiply_reduce_fusion
  130.2 0.8 copy.19
  (6 shorter events, 0.1 us)
Async XLA Ops:
  30.5 21.2 %collective-permute-start.2 = (bf16[16,4096]{1,0:T(8,128)(2,1)S(1)}, bf16[16,4096]{1,0:T(8,128)(2,1)S(1)}, u32[]{:S(2)}, u32[]{:S(2)}) collective-permute-start(bf16[16,4096]{1,0:T(8,128)(2,1)S(1)} %bitcast.19), channel_id=1, source_target_pairs={{0,24},{1,385},{8,0},{9,393},{16,8},{17,401},{24,16},{25,409},{128... | collective-permute-start | bytes 393224 | tf_op jit(solution)/shard_map/ppermute | solution.py:30
  35.5 16.3 %collective-permute-start.1 = (bf16[16,4096]{1,0:T(8,128)(2,1)S(1)}, bf16[16,4096]{1,0:T(8,128)(2,1)S(1)}, u32[]{:S(2)}, u32[]{:S(2)}) collective-permute-start(bf16[16,4096]{1,0:T(8,128)(2,1)S(1)} %bitcast.20), channel_id=1, source_target_pairs={{0,16},{1,257},{8,24},{9,265},{16,0},{17,273},{24,8},{25,281},{128... | collective-permute-start | bytes 393224 | tf_op jit(solution)/shard_map/ppermute | solution.py:30
  38.0 13.7 %collective-permute-start = (bf16[16,4096]{1,0:T(8,128)(2,1)S(1)}, bf16[16,4096]{1,0:T(8,128)(2,1)S(1)}, u32[]{:S(2)}, u32[]{:S(2)}) collective-permute-start(bf16[16,4096]{1,0:T(8,128)(2,1)S(1)} %bitcast.21), channel_id=1, source_target_pairs={{0,8},{1,129},{8,16},{9,137},{16,24},{17,145},{24,0},{25,153},{128... | collective-permute-start | bytes 393224 | tf_op jit(solution)/shard_map/ppermute | solution.py:30
  51.8 12.7 %collective-permute-start.7 = (bf16[64,4096]{1,0:T(8,128)(2,1)S(1)}, bf16[64,4096]{1,0:T(8,128)(2,1)S(1)}, u32[]{:S(2)}, u32[]{:S(2)}) collective-permute-start(bf16[64,4096]{1,0:T(8,128)(2,1)S(1)} %constant_dynamic-update-slice_fusion.a), channel_id=1, source_target_pairs={{0,256},{1,17},{8,264},{9,25},{16,272},{17,1},{24,280},{25,9},{128... | collective-permute-start | bytes 1572872 | tf_op jit(solution)/shard_map/ppermute | solution.py:30
  55.8 14.2 %collective-permute-start.4 = (bf16[64,4096]{1,0:T(8,128)(2,1)S(1)}, bf16[64,4096]{1,0:T(8,128)(2,1)S(1)}, u32[]{:S(2)}, u32[]{:S(2)}) collective-permute-start(bf16[64,4096]{1,0:T(8,128)(2,1)S(1)} %constant_dynamic-update-slice_fusion.a), channel_id=1, source_target_pairs={{0,384},{1,25},{8,392},{9,1},{16,400},{17,9},{24,408},{25,17},{128... | collective-permute-start | bytes 1572872 | tf_op jit(solution)/shard_map/ppermute | solution.py:30
  59.2 12.7 %collective-permute-start.3 = (bf16[64,4096]{1,0:T(8,128)(2,1)S(1)}, bf16[64,4096]{1,0:T(8,128)(2,1)S(1)}, u32[]{:S(2)}, u32[]{:S(2)}) collective-permute-start(bf16[64,4096]{1,0:T(8,128)(2,1)S(1)} %constant_dynamic-update-slice_fusion.a), channel_id=1, source_target_pairs={{0,128},{1,9},{8,136},{9,17},{16,144},{17,25},{24,152},{25,1},{128... | collective-permute-start | bytes 1572872 | tf_op jit(solution)/shard_map/ppermute | solution.py:30
  61.7 13.5 %collective-permute-start.8 = (bf16[64,4096]{1,0:T(8,128)(2,1)S(1)}, bf16[64,4096]{1,0:T(8,128)(2,1)S(1)}, u32[]{:S(2)}, u32[]{:S(2)}) collective-permute-start(bf16[64,4096]{1,0:T(8,128)(2,1)S(1)} %constant_dynamic-update-slice_fusion.a), channel_id=1, source_target_pairs={{0,1},{1,0},{2,3},{3,2},{4,5},{5,4},{6,7},{7,6},{8,9},{9,8},{10,11... | collective-permute-start | bytes 1572872 | tf_op jit(solution)/shard_map/ppermute | solution.py:34
  64.5 10.7 %collective-permute-start.9 = (bf16[64,4096]{1,0:T(8,128)(2,1)S(1)}, bf16[64,4096]{1,0:T(8,128)(2,1)}, u32[]{:S(2)}, u32[]{:S(2)}) collective-permute-start(bf16[64,4096]{1,0:T(8,128)(2,1)S(1)} %collective-permute-done.7.b), channel_id=1, source_target_pairs={{0,1},{1,0},{2,3},{3,2},{4,5},{5,4},{6,7},{7,6},{8,9},{9,8},{10,11... | collective-permute-start | bytes 1572872 | tf_op jit(solution)/shard_map/ppermute | solution.py:34
  70.0 9.8 %collective-permute-start.6 = (bf16[64,4096]{1,0:T(8,128)(2,1)S(1)}, bf16[64,4096]{1,0:T(8,128)(2,1)S(1)}, u32[]{:S(2)}, u32[]{:S(2)}) collective-permute-start(bf16[64,4096]{1,0:T(8,128)(2,1)S(1)} %collective-permute-done.4.b), channel_id=1, source_target_pairs={{0,1},{1,0},{2,3},{3,2},{4,5},{5,4},{6,7},{7,6},{8,9},{9,8},{10,11... | collective-permute-start | bytes 1572872 | tf_op jit(solution)/shard_map/ppermute | solution.py:34
  71.9 7.9 %collective-permute-start.5 = (bf16[64,4096]{1,0:T(8,128)(2,1)S(1)}, bf16[64,4096]{1,0:T(8,128)(2,1)}, u32[]{:S(2)}, u32[]{:S(2)}) collective-permute-start(bf16[64,4096]{1,0:T(8,128)(2,1)S(1)} %collective-permute-done.3.a), channel_id=1, source_target_pairs={{0,1},{1,0},{2,3},{3,2},{4,5},{5,4},{6,7},{7,6},{8,9},{9,8},{10,11... | collective-permute-start | bytes 1572872 | tf_op jit(solution)/shard_map/ppermute | solution.py:34
  75.2 2.1 %copy-start = (bf16[1,4096,464]{1,2,0:T(8,128)(2,1)S(1)}, bf16[1,4096,464]{1,2,0:T(8,128)(2,1)}, u32[]{:S(2)}) copy-start(bf16[1,4096,464]{1,2,0:T(8,128)(2,1)} %param.5) | copy-start | bytes 11403268
  77.3 2.5 %copy-start.1 = (bf16[1,4096,464]{1,2,0:T(8,128)(2,1)S(1)}, bf16[1,4096,464]{1,2,0:T(8,128)(2,1)}, u32[]{:S(2)}) copy-start(bf16[1,4096,464]{1,2,0:T(8,128)(2,1)} %param.5) | copy-start | bytes 11403268
  79.7 8.7 %copy-start.2 = (s32[4,16]{1,0:T(4,128)S(1)}, s32[4,16]{1,0:T(4,128)}, u32[]{:S(2)}) copy-start(s32[4,16]{1,0:T(4,128)} %param.7) | copy-start | bytes 772
  79.8 8.7 %copy-start.3 = (f32[16]{0:T(128)S(1)}, f32[16]{0:T(128)}, u32[]{:S(2)}) copy-start(f32[16]{0:T(128)} %param.8) | copy-start | bytes 196
  83.9 37.8 %all-to-all-start.1 = ((s16[16,32,512]{2,1,0:T(8,128)(2,1)}), s16[16,32,512]{2,1,0:T(8,128)(2,1)S(1)}, u32[]{:S(2)}, u32[]{:S(2)}) async-start(s16[16,32,512]{2,1,0:T(8,128)(2,1)} %bitcast.5), calls=%async_computation.1 | async-start | bytes 1048576 | tf_op jit(solution)/shard_map/all_to_all | solution.py:112

commit v4 on v3

v4 whole, which is shorter than its diff:
```python
import jax
import jax.numpy as jnp
from jax import lax
from jax.experimental import pallas as pl
from jax.experimental.pallas import tpu as pltpu
from jax.sharding import Mesh, PartitionSpec as P

BF16, F32, I16, I32 = jnp.bfloat16, jnp.float32, jnp.int16, jnp.int32
LANES = 512
TOP = 32767.0
AXES = ("x", "zh", "y", "zl", "c")


def spread(block, axes, groups):
    copies = jnp.broadcast_to(block[None], (len(groups[0]),) + block.shape)
    return lax.all_to_all(copies, axes, 0, 0, axis_index_groups=groups)


def columns():
    def at(x, y, z, c):
        return (((x * 4 + z // 4) * 4 + y) * 4 + z % 4) * 2 + c

    return [[at(k, j, z, 0) for j in range(4) for z in range(16)] for k in range(4)] + [
        [at(j, k, z, 1) for j in range(4) for z in range(16)] for k in range(4)
    ]


def lines():
    return [[(i * 4 + k) * 2 for i in range(4)] for k in range(4)] + [
        [(k * 4 + i) * 2 + 1 for i in range(4)] for k in range(4)
    ]


def product(rows_ref, w_ref):
    return lax.dot_general(rows_ref[...], w_ref[...], (((1,), (1,)), ((), ())), preferred_element_type=F32)


def first_kernel(rows_ref, w_ref, out_ref):
    out_ref[...] = product(rows_ref, w_ref)


def encode(partial):
    rows, width = partial.shape
    top = jnp.max(jnp.abs(partial), axis=1, keepdims=True)
    power = jnp.clip(jnp.floor(jnp.log2(top)), -80.0, 80.0)
    mantissa = jnp.ceil(top * jnp.exp2(-power) * 8192.0) + 1.0
    step = mantissa * jnp.exp2(power) * (1.0 / (8192.0 * TOP))
    codes = jnp.clip(jnp.round(partial * (1.0 / step)), -TOP, TOP)
    codes = jnp.concatenate([codes, jnp.zeros((rows, LANES - width), F32)], axis=1)
    column = lax.broadcasted_iota(I32, (rows, LANES), 1)
    codes = jnp.where(column == width, mantissa, codes)
    codes = jnp.where(column == width + 1, power, codes)
    high = jnp.floor(codes * (1.0 / 256.0))
    return high.astype(BF16), (codes - high * 256.0).astype(BF16)


def second_kernel(rows_ref, w_ref, first_ref, place_ref, out_ref, high_ref, low_ref):
    half = first_ref.shape[0]
    high_ref[:half], low_ref[:half] = encode(first_ref[...])
    high_ref[half:], low_ref[half:] = encode(product(rows_ref, w_ref))
    for at in range(0, 512, 256):
        column = lax.broadcasted_iota(I32, (256, 512), 1)
        pick = jnp.where(place_ref[at : at + 256] == column, 1.0, 0.0).astype(BF16)
        high = jnp.dot(pick, high_ref[...], preferred_element_type=F32)
        low = jnp.dot(pick, low_ref[...], preferred_element_type=F32)
        out_ref[at : at + 256] = (high * 256.0 + low).astype(I32).astype(I16)


def decode_kernel(coefficient_ref, got_ref, out_ref):
    rows, cands, width = out_ref.shape
    totals = [None] * cands
    for source in range(16):
        codes = got_ref[source * rows : (source + 1) * rows].astype(I32).astype(F32)
        step = codes[:, width : width + 1] * jnp.exp2(codes[:, width + 1 : width + 2]) * (1.0 / (8192.0 * TOP))
        values = codes * step
        for c in range(cands):
            term = coefficient_ref[c, source] * values
            totals[c] = term if source == 0 else totals[c] + term
    out_ref[...] = jnp.stack([t[:, :width] for t in totals], axis=1).astype(BF16)


def on_device(weights, calib_pool, cand_index, coef_table, row_ids):
    core = lax.axis_index("c")
    w_piece = weights[0].T
    own = spread(calib_pool.reshape(32, 128), AXES, columns()).reshape(64, 4096)
    own = spread(own, ("x", "y", "c"), lines()).reshape(256, 4096)
    other = lax.ppermute(own, "c", [(0, 1), (1, 0)])

    width = w_piece.shape[0]
    vmem = pl.BlockSpec(memory_space=pltpu.VMEM)
    params = pltpu.CompilerParams(vmem_limit_bytes=40 * 2**20)
    cost = pl.CostEstimate(flops=2 * 256 * 4096 * width, bytes_accessed=6 * 2**20, transcendentals=0)
    first = pl.pallas_call(
        first_kernel,
        out_shape=jax.ShapeDtypeStruct((256, width), F32),
        in_specs=[vmem] * 2,
        out_specs=vmem,
        compiler_params=params,
        cost_estimate=cost,
        name="first",
    )(own, w_piece)

    x, zh, y, zl, c = (row_ids >> 7) & 3, (row_ids >> 5) & 3, (row_ids >> 3) & 3, (row_ids >> 1) & 3, row_ids & 1
    place = jnp.where(c == 0, x * 4 + y, y * 4 + x) * 16 + zh * 4 + zl + jnp.where(c == core, 0, 256)

    sent = pl.pallas_call(
        second_kernel,
        out_shape=jax.ShapeDtypeStruct((512, LANES), I16),
        in_specs=[vmem] * 4,
        out_specs=vmem,
        scratch_shapes=[pltpu.VMEM((512, LANES), BF16)] * 2,
        compiler_params=params,
        cost_estimate=cost,
        name="second",
    )(other, w_piece, first, place[:, None])
    got = lax.all_to_all(sent, ("x", "zh"), 0, 0, tiled=True)

    entries = jnp.arange(coef_table.shape[0], dtype=I32)
    onehot = (cand_index[:, :, None] == entries[None, None, :]).astype(F32)
    coefficient = jnp.sum(onehot * coef_table[None, None, :], axis=2)
    return pl.pallas_call(
        decode_kernel,
        out_shape=jax.ShapeDtypeStruct((32, 4, width), BF16),
        in_specs=[pl.BlockSpec(memory_space=pltpu.SMEM), vmem],
        out_specs=vmem,
        compiler_params=params,
        name="decode",
    )(coefficient, got)


def solution(mesh):
    fine = Mesh(mesh.devices.reshape(4, 4, 4, 4, 2), AXES)
    src, shard = ("x", "zh"), ("y", "zl", "c")
    placed = (P(src, None, shard), P(src + shard, None), P(), P(), P())
    return jax.shard_map(on_device, mesh=fine, in_specs=placed, out_specs=P(src, None, shard), check_vma=False)
```

time: 132 us -> 126 us (0.955)
  the two profiles are of different devices: /device:TPU:2 before, /device:TPU:32 now
where the time goes in v4:
time: 126 us; the launch traced here: 125 us
  blocking collectives  69.7 us (55%)
  waiting for transfers between devices  35.2 us (28%)
  starting transfers between devices  8.49 us (7%)
  Pallas kernels  7.84 us (6%)
  local copies, waits for them, and re-layouts  2.85 us (2%)
    all_to_all x2, blocking collectives, spread(): return lax.all_to_all(copies, axes, 0, 0, axis_index_groups=groups)  69.7 us
    all_to_all x1, waiting for transfers between devices, on_device(): got = lax.all_to_all(sent, ('x', 'zh'), 0, 0, tiled=True)  34.6 us
    all_to_all x1, starting transfers between devices, on_device(): got = lax.all_to_all(sent, ('x', 'zh'), 0, 0, tiled=True)  6.58 us
    pallas_call x1, Pallas kernels, on_device(): pl.pallas_call(second_kernel, out_shape=jax.ShapeDtypeStruct((512, LANES)...  4.63 us
  transfers between devices with their start and end apart: 2, of which 2 were waited for; matrix products, arithmetic and copies ran while one was open for 0% of the time, Pallas kernels for 1%

profile of v4, /device:TPU:32, one launch (start us, length us, event | category | flops | bytes accessed | tf_op | source)
XLA Modules:
  0.0 125.2 jit_solution(18410112794822432312)
XLA Ops:
  0.0 0.8 reduce
  0.8 0.1 broadcast_in_dim.27
  0.8 48.9 %all_to_all.21 = bf16[64,32,128]{2,1,0:T(8,128)(2,1)S(1)} all-to-all(bf16[64,32,128]{2,1,0:T(8,128)(2,1)S(1)} %broadcast_in_dim.27), channel_id=1, replica_groups={{0,2,4,6,32,34,36,38,64,66,68,70,96,98,100,102,8,10,12,14,40,42,44,46,7..., dimensions={0} | all-to-all | bytes 1048576 | tf_op jit(solution)/shard_map/all_to_all | solution.py:16
  49.8 0.2 copy.10
  50.0 0.2 broadcast_in_dim.29
  50.2 0.0 copy-start.2
  50.3 20.8 %all_to_all.22 = bf16[4,64,4096]{2,1,0:T(8,128)(2,1)S(1)} all-to-all(bf16[4,64,4096]{2,1,0:T(8,128)(2,1)S(1)} %broadcast_in_dim.29), channel_id=1, replica_groups={{0,128,256,384},{8,136,264,392},{16,144,272,400},{24,152,280,408},{1,9,..., dimensions={0} | all-to-all | bytes 4194304 | tf_op jit(solution)/shard_map/all_to_all | solution.py:16
  71.0 1.9 %collective-permute-start = (bf16[256,4096]{1,0:T(8,128)(2,1)S(1)}, bf16[256,4096]{1,0:T(8,128)(2,1)}, u32[]{:S(2)}, u32[]{:S(2)}) collective-permute-start(bf16[256,4096]{1,0:T(8,128)(2,1)S(1)} %bitcast.14), channel_id=1, source_target_pairs={{0,1},{1,0},{2,3},{3,2},{4,5},{5,4},{6,7},{7,6},{8,9},{9,8},{10,11... | collective-permute-start | bytes 6291464 | tf_op jit(solution)/shard_map/ppermute | solution.py:87
  73.0 0.0 copy-done.2
  73.0 0.1 copy.7.place_ref
  73.1 0.0 copy-start
  73.1 2.1 %copy-done = bf16[1,4096,464]{1,2,0:T(8,128)(2,1)S(1)} copy-done((bf16[1,4096,464]{1,2,0:T(8,128)(2,1)S(1)}, bf16[1,4096,464]{1,2,0:T(8,128)(2,1)}, u32[]{:S(2)}) %copy-start) | copy-done | bytes 3801112
  75.2 0.0 copy-start.1
  75.2 1.3 %first.1.first_ref = f32[256,464]{1,0:T(8,128)S(1)} custom-call(bf16[256,4096]{1,0:T(8,128)(2,1)S(1)} %bitcast.15, bf16[464,4096]{1,0:T(8,128)(2,1)S(1)} %bitcast.12), custom_call_target="tpu_custom_call" | custom-call | flops 973078528 | bytes 6291456 | tf_op jit(solution)/shard_map/first/pallas_call | solution.py:93
  76.5 0.0 copy-start.3
  76.5 0.0 copy-start.4
  76.5 0.7 collective-permute-done.rows_ref
  77.2 0.1 copy-done.1
  77.3 4.6 %second.1 = s16[512,512]{1,0:T(8,128)(2,1)} custom-call(bf16[256,4096]{1,0:T(8,128)(2,1)} %collective-permute-done.rows_ref, bf16[464,4096]{1,0:T(8,128)(2,1)S(1)} %bitcast.13, f32[256,464]{1,0:T(8,128)S(1)} %first.1.first_ref, s32[512,1]{1,0:T(8,128)S(1)} %copy.7.place_ref), custom_call_target="tpu_custom_call" | custom-call | flops 973078528 | bytes 6291456 | tf_op jit(solution)/shard_map/second/pallas_call | solution.py:106
  81.9 6.6 %all-to-all-start.2 = ((s16[16,32,512]{2,1,0:T(8,128)(2,1)}), s16[16,32,512]{2,1,0:T(8,128)(2,1)S(1)}, u32[]{:S(2)}, u32[]{:S(2)}) async-start(s16[16,32,512]{2,1,0:T(8,128)(2,1)} %bitcast.5), calls=%async_computation.2 | async-start | bytes 1048576 | tf_op jit(solution)/shard_map/all_to_all | solution.py:116
  88.5 0.0 copy-done.3
  88.5 0.0 copy-done.4
  88.5 0.2 select_reduce_fusion.coefficient_ref
  88.7 34.6 %all-to-all-done.2 = s16[16,32,512]{2,1,0:T(8,128)(2,1)S(1)} async-done(((s16[16,32,512]{2,1,0:T(8,128)(2,1)}), s16[16,32,512]{2,1,0:T(8,128)(2,1)S(1)}, u32[]{:S(2)}, u32[]{:S(2)}) %all-to-all-start.2) | async-done | bytes 524320 | tf_op jit(solution)/shard_map/all_to_all | solution.py:116
  123.2 1.9 %decode.1 = bf16[32,4,464]{2,1,0:T(4,128)(2,1)} custom-call(f32[4,16]{1,0:T(4,128)S(1)} %select_reduce_fusion.coefficient_ref, s16[512,512]{1,0:T(8,128)(2,1)S(1)} %bitcast.16), custom_call_target="tpu_custom_call" | custom-call | tf_op jit(solution)/shard_map/decode/pallas_call | solution.py:121
  (1 shorter events, 0.0 us)
Async XLA Ops:
  50.2 22.7 %copy-start.2 = (s32[512]{0:T(512)S(1)}, s32[512]{0:T(512)}, u32[]{:S(2)}) copy-start(s32[512]{0:T(512)} %param.9) | copy-start | bytes 6148
  71.0 6.2 %collective-permute-start = (bf16[256,4096]{1,0:T(8,128)(2,1)S(1)}, bf16[256,4096]{1,0:T(8,128)(2,1)}, u32[]{:S(2)}, u32[]{:S(2)}) collective-permute-start(bf16[256,4096]{1,0:T(8,128)(2,1)S(1)} %bitcast.14), channel_id=1, source_target_pairs={{0,1},{1,0},{2,3},{3,2},{4,5},{5,4},{6,7},{7,6},{8,9},{9,8},{10,11... | collective-permute-start | bytes 6291464 | tf_op jit(solution)/shard_map/ppermute | solution.py:87
  73.1 2.1 %copy-start = (bf16[1,4096,464]{1,2,0:T(8,128)(2,1)S(1)}, bf16[1,4096,464]{1,2,0:T(8,128)(2,1)}, u32[]{:S(2)}) copy-start(bf16[1,4096,464]{1,2,0:T(8,128)(2,1)} %param.5) | copy-start | bytes 11403268
  75.2 2.1 %copy-start.1 = (bf16[1,4096,464]{1,2,0:T(8,128)(2,1)S(1)}, bf16[1,4096,464]{1,2,0:T(8,128)(2,1)}, u32[]{:S(2)}) copy-start(bf16[1,4096,464]{1,2,0:T(8,128)(2,1)} %param.5) | copy-start | bytes 11403268
  76.5 12.0 %copy-start.3 = (s32[4,16]{1,0:T(4,128)S(1)}, s32[4,16]{1,0:T(4,128)}, u32[]{:S(2)}) copy-start(s32[4,16]{1,0:T(4,128)} %param.7) | copy-start | bytes 772
  76.5 12.0 %copy-start.4 = (f32[16]{0:T(128)S(1)}, f32[16]{0:T(128)}, u32[]{:S(2)}) copy-start(f32[16]{0:T(128)} %param.8) | copy-start | bytes 196
  81.9 41.3 %all-to-all-start.2 = ((s16[16,32,512]{2,1,0:T(8,128)(2,1)}), s16[16,32,512]{2,1,0:T(8,128)(2,1)S(1)}, u32[]{:S(2)}, u32[]{:S(2)}) async-start(s16[16,32,512]{2,1,0:T(8,128)(2,1)} %bitcast.5), calls=%async_computation.2 | async-start | bytes 1048576 | tf_op jit(solution)/shard_map/all_to_all | solution.py:116

commit v5 on v4

--- a/solution.py
+++ b/solution.py
@@ -11,23 +11,14 @@
 AXES = ("x", "zh", "y", "zl", "c")
 
 
-def spread(block, axes, groups):
-    copies = jnp.broadcast_to(block[None], (len(groups[0]),) + block.shape)
+def spread(block, axes, count, groups=None):
+    copies = jnp.broadcast_to(block[None], (count,) + block.shape)
     return lax.all_to_all(copies, axes, 0, 0, axis_index_groups=groups)
 
 
-def columns():
-    def at(x, y, z, c):
-        return (((x * 4 + z // 4) * 4 + y) * 4 + z % 4) * 2 + c
-
-    return [[at(k, j, z, 0) for j in range(4) for z in range(16)] for k in range(4)] + [
-        [at(j, k, z, 1) for j in range(4) for z in range(16)] for k in range(4)
-    ]
-
-
-def lines():
-    return [[(i * 4 + k) * 2 for i in range(4)] for k in range(4)] + [
-        [(k * 4 + i) * 2 + 1 for i in range(4)] for k in range(4)
+def lines(along):
+    return [[(k * 4 + i) * 2 + along for i in range(4)] for k in range(4)] + [
+        [(i * 4 + k) * 2 + 1 - along for i in range(4)] for k in range(4)
     ]
 
 
@@ -39,31 +30,33 @@
     out_ref[...] = product(rows_ref, w_ref)
 
 
-def encode(partial):
+def encode(partial, out_ref, at):
     rows, width = partial.shape
+    main = LANES - 128
     top = jnp.max(jnp.abs(partial), axis=1, keepdims=True)
     power = jnp.clip(jnp.floor(jnp.log2(top)), -80.0, 80.0)
     mantissa = jnp.ceil(top * jnp.exp2(-power) * 8192.0) + 1.0
-    step = mantissa * jnp.exp2(power) * (1.0 / (8192.0 * TOP))
-    codes = jnp.clip(jnp.round(partial * (1.0 / step)), -TOP, TOP)
-    codes = jnp.concatenate([codes, jnp.zeros((rows, LANES - width), F32)], axis=1)
-    column = lax.broadcasted_iota(I32, (rows, LANES), 1)
-    codes = jnp.where(column == width, mantissa, codes)
-    codes = jnp.where(column == width + 1, power, codes)
-    high = jnp.floor(codes * (1.0 / 256.0))
-    return high.astype(BF16), (codes - high * 256.0).astype(BF16)
+    per_step = 1.0 / (mantissa * jnp.exp2(power) * (1.0 / (8192.0 * TOP)))
+    tail = jnp.concatenate([partial[:, main:], jnp.zeros((rows, LANES - width), F32)], axis=1)
+    tail = jnp.round(tail * per_step)
+    column = lax.broadcasted_iota(I32, (rows, 128), 1) + main
+    tail = jnp.where(column == width, mantissa, jnp.where(column == width + 1, power, tail))
+    for codes, columns in ((jnp.round(partial[:, :main] * per_step), slice(0, main)), (tail, slice(main, LANES))):
+        high = jnp.floor(codes * (1.0 / 256.0))
+        out_ref[at : at + rows, columns] = high.astype(BF16)
+        out_ref[512 + at : 512 + at + rows, columns] = (codes - high * 256.0).astype(BF16)
 
 
-def second_kernel(rows_ref, w_ref, first_ref, place_ref, out_ref, high_ref, low_ref):
+def second_kernel(rows_ref, w_ref, first_ref, place_ref, out_ref, bytes_ref):
     half = first_ref.shape[0]
-    high_ref[:half], low_ref[:half] = encode(first_ref[...])
-    high_ref[half:], low_ref[half:] = encode(product(rows_ref, w_ref))
+    encode(first_ref[...], bytes_ref, 0)
+    encode(product(rows_ref, w_ref), bytes_ref, half)
     for at in range(0, 512, 256):
         column = lax.broadcasted_iota(I32, (256, 512), 1)
-        pick = jnp.where(place_ref[at : at + 256] == column, 1.0, 0.0).astype(BF16)
-        high = jnp.dot(pick, high_ref[...], preferred_element_type=F32)
-        low = jnp.dot(pick, low_ref[...], preferred_element_type=F32)
-        out_ref[at : at + 256] = (high * 256.0 + low).astype(I32).astype(I16)
+        found = place_ref[at : at + 256] == column
+        pick = jnp.concatenate([jnp.where(found, 256.0, 0.0), jnp.where(found, 1.0, 0.0)], axis=1).astype(BF16)
+        codes = jnp.dot(pick, bytes_ref[...], preferred_element_type=F32)
+        out_ref[at : at + 256] = codes.astype(I32).astype(I16)
 
 
 def decode_kernel(coefficient_ref, got_ref, out_ref):
@@ -82,13 +75,14 @@
 def on_device(weights, calib_pool, cand_index, coef_table, row_ids):
     core = lax.axis_index("c")
     w_piece = weights[0].T
-    own = spread(calib_pool.reshape(32, 128), AXES, columns()).reshape(64, 4096)
-    own = spread(own, ("x", "y", "c"), lines()).reshape(256, 4096)
+    own = spread(calib_pool.reshape(32, 128), ("zh", "zl"), 16).reshape(16, 4096)
+    own = spread(own, ("x", "y", "c"), 4, lines(0)).reshape(64, 4096)
+    own = spread(own, ("x", "y", "c"), 4, lines(1)).reshape(256, 4096)
     other = lax.ppermute(own, "c", [(0, 1), (1, 0)])
 
     width = w_piece.shape[0]
     vmem = pl.BlockSpec(memory_space=pltpu.VMEM)
-    params = pltpu.CompilerParams(vmem_limit_bytes=40 * 2**20)
+    params = pltpu.CompilerParams(vmem_limit_bytes=16 * 2**20)
     cost = pl.CostEstimate(flops=2 * 256 * 4096 * width, bytes_accessed=6 * 2**20, transcendentals=0)
     first = pl.pallas_call(
         first_kernel,
@@ -108,7 +102,7 @@
         out_shape=jax.ShapeDtypeStruct((512, LANES), I16),
         in_specs=[vmem] * 4,
         out_specs=vmem,
-        scratch_shapes=[pltpu.VMEM((512, LANES), BF16)] * 2,
+        scratch_shapes=[pltpu.VMEM((1024, LANES), BF16)],
         compiler_params=params,
         cost_estimate=cost,
         name="second",

time: 126 us -> 116 us (0.921)
  blocking collectives: 69.7 us -> 62.2 us
  starting transfers between devices: 8.49 us -> 6.19 us
    all_to_all x2 -> x3, blocking collectives: 69.7 us -> 62.2 us  [spread(): return lax.all_to_all(copies, axes, 0, 0, axis_index_groups=groups)]
    all_to_all x1, starting transfers between devices: 6.58 us -> 4.28 us  [on_device(): got = lax.all_to_all(sent, ('x', 'zh'), 0, 0, tiled=True)]
where the time goes in v5:
time: 116 us
  blocking collectives  62.2 us (54%)
  waiting for transfers between devices  35.6 us (31%)
  Pallas kernels  7.89 us (7%)
  starting transfers between devices  6.19 us (5%)
  local copies, waits for them, and re-layouts  2.68 us (2%)
    all_to_all x3, blocking collectives, spread(): return lax.all_to_all(copies, axes, 0, 0, axis_index_groups=groups)  62.2 us
    all_to_all x1, waiting for transfers between devices, on_device(): got = lax.all_to_all(sent, ('x', 'zh'), 0, 0, tiled=True)  34.9 us
    pallas_call x1, Pallas kernels, on_device(): pl.pallas_call(second_kernel, out_shape=jax.ShapeDtypeStruct((512, LANES)...  4.68 us
    all_to_all x1, starting transfers between devices, on_device(): got = lax.all_to_all(sent, ('x', 'zh'), 0, 0, tiled=True)  4.28 us
  transfers between devices with their start and end apart: 2, of which 2 were waited for; matrix products, arithmetic and copies ran while one was open for 0% of the time, Pallas kernels for 1%

profile of v5, /device:TPU:32, one launch (start us, length us, event | category | flops | bytes accessed | tf_op | source)
XLA Modules:
  0.0 115.6 jit_solution(4469752207094547350)
XLA Ops:
  0.0 0.8 reduce
  0.8 29.2 %all_to_all.26 = bf16[16,32,128]{2,1,0:T(8,128)(2,1)S(1)} all-to-all(bf16[16,32,128]{2,1,0:T(8,128)(2,1)S(1)} %broadcast_in_dim.34), channel_id=1, replica_groups=mesh['x'=4,'zh'=4,'y'=4,'zl'=4,'c'=2] {'zh','zl'}, dimensions={0} | all-to-all | bytes 262144 | tf_op jit(solution)/shard_map/all_to_all | solution.py:16
  30.0 0.1 copy.10
  30.1 12.3 %all_to_all.27 = bf16[4,16,4096]{2,1,0:T(8,128)(2,1)S(1)} all-to-all(bf16[4,16,4096]{2,1,0:T(8,128)(2,1)S(1)} %broadcast_in_dim.36), channel_id=1, replica_groups={{0,8,16,24},{128,136,144,152},{256,264,272,280},{384,392,400,408},{1,12..., dimensions={0} | all-to-all | bytes 1048576 | tf_op jit(solution)/shard_map/all_to_all | solution.py:16
  42.5 0.2 broadcast_in_dim.38
  42.7 0.0 copy-start.2
  42.7 20.6 %all_to_all.28 = bf16[4,64,4096]{2,1,0:T(8,128)(2,1)S(1)} all-to-all(bf16[4,64,4096]{2,1,0:T(8,128)(2,1)S(1)} %broadcast_in_dim.38), channel_id=1, replica_groups={{1,9,17,25},{129,137,145,153},{257,265,273,281},{385,393,401,409},{0,12..., dimensions={0} | all-to-all | bytes 4194304 | tf_op jit(solution)/shard_map/all_to_all | solution.py:16
  63.3 1.9 %collective-permute-start = (bf16[256,4096]{1,0:T(8,128)(2,1)S(1)}, bf16[256,4096]{1,0:T(8,128)(2,1)}, u32[]{:S(2)}, u32[]{:S(2)}) collective-permute-start(bf16[256,4096]{1,0:T(8,128)(2,1)S(1)} %bitcast.15), channel_id=1, source_target_pairs={{0,1},{1,0},{2,3},{3,2},{4,5},{5,4},{6,7},{7,6},{8,9},{9,8},{10,11... | collective-permute-start | bytes 6291464 | tf_op jit(solution)/shard_map/ppermute | solution.py:81
  65.2 0.0 copy-done.2
  65.3 0.1 copy.7.place_ref
  65.4 0.0 copy-start
  65.4 2.1 %copy-done = bf16[1,4096,464]{1,2,0:T(8,128)(2,1)S(1)} copy-done((bf16[1,4096,464]{1,2,0:T(8,128)(2,1)S(1)}, bf16[1,4096,464]{1,2,0:T(8,128)(2,1)}, u32[]{:S(2)}) %copy-start) | copy-done | bytes 3801112
  67.5 0.0 copy-start.1
  67.5 1.3 %first.1.first_ref = f32[256,464]{1,0:T(8,128)S(1)} custom-call(bf16[256,4096]{1,0:T(8,128)(2,1)S(1)} %bitcast.16, bf16[464,4096]{1,0:T(8,128)(2,1)S(1)} %bitcast.13), custom_call_target="tpu_custom_call" | custom-call | flops 973078528 | bytes 6291456 | tf_op jit(solution)/shard_map/first/pallas_call | solution.py:87
  68.8 0.0 copy-start.3
  68.8 0.0 copy-start.4
  68.8 0.7 collective-permute-done.rows_ref
  69.5 0.1 copy-done.1
  69.6 4.7 %second.1 = s16[512,512]{1,0:T(8,128)(2,1)} custom-call(bf16[256,4096]{1,0:T(8,128)(2,1)} %collective-permute-done.rows_ref, bf16[464,4096]{1,0:T(8,128)(2,1)S(1)} %bitcast.14, f32[256,464]{1,0:T(8,128)S(1)} %first.1.first_ref, s32[512,1]{1,0:T(8,128)S(1)} %copy.7.place_ref), custom_call_target="tpu_custom_call" | custom-call | flops 973078528 | bytes 6291456 | tf_op jit(solution)/shard_map/second/pallas_call | solution.py:100
  74.3 4.3 %all-to-all-start.3 = ((s16[16,32,512]{2,1,0:T(8,128)(2,1)}), s16[16,32,512]{2,1,0:T(8,128)(2,1)S(1)}, u32[]{:S(2)}, u32[]{:S(2)}) async-start(s16[16,32,512]{2,1,0:T(8,128)(2,1)} %bitcast.6), calls=%async_computation.3 | async-start | bytes 1048576 | tf_op jit(solution)/shard_map/all_to_all | solution.py:110
  78.6 0.0 copy-done.3
  78.6 0.0 copy-done.4
  78.6 0.2 select_reduce_fusion.coefficient_ref
  78.7 34.9 %all-to-all-done.3 = s16[16,32,512]{2,1,0:T(8,128)(2,1)S(1)} async-done(((s16[16,32,512]{2,1,0:T(8,128)(2,1)}), s16[16,32,512]{2,1,0:T(8,128)(2,1)S(1)}, u32[]{:S(2)}, u32[]{:S(2)}) %all-to-all-start.3) | async-done | bytes 524320 | tf_op jit(solution)/shard_map/all_to_all | solution.py:110
  113.7 1.9 %decode.1 = bf16[32,4,464]{2,1,0:T(4,128)(2,1)} custom-call(f32[4,16]{1,0:T(4,128)S(1)} %select_reduce_fusion.coefficient_ref, s16[512,512]{1,0:T(8,128)(2,1)S(1)} %bitcast.17), custom_call_target="tpu_custom_call" | custom-call | tf_op jit(solution)/shard_map/decode/pallas_call | solution.py:115
  (3 shorter events, 0.1 us)
Async XLA Ops:
  42.7 22.5 %copy-start.2 = (s32[512]{0:T(512)S(1)}, s32[512]{0:T(512)}, u32[]{:S(2)}) copy-start(s32[512]{0:T(512)} %param.9) | copy-start | bytes 6148
  63.3 6.2 %collective-permute-start = (bf16[256,4096]{1,0:T(8,128)(2,1)S(1)}, bf16[256,4096]{1,0:T(8,128)(2,1)}, u32[]{:S(2)}, u32[]{:S(2)}) collective-permute-start(bf16[256,4096]{1,0:T(8,128)(2,1)S(1)} %bitcast.15), channel_id=1, source_target_pairs={{0,1},{1,0},{2,3},{3,2},{4,5},{5,4},{6,7},{7,6},{8,9},{9,8},{10,11... | collective-permute-start | bytes 6291464 | tf_op jit(solution)/shard_map/ppermute | solution.py:81
  65.4 2.1 %copy-start = (bf16[1,4096,464]{1,2,0:T(8,128)(2,1)S(1)}, bf16[1,4096,464]{1,2,0:T(8,128)(2,1)}, u32[]{:S(2)}) copy-start(bf16[1,4096,464]{1,2,0:T(8,128)(2,1)} %param.5) | copy-start | bytes 11403268
  67.5 2.1 %copy-start.1 = (bf16[1,4096,464]{1,2,0:T(8,128)(2,1)S(1)}, bf16[1,4096,464]{1,2,0:T(8,128)(2,1)}, u32[]{:S(2)}) copy-start(bf16[1,4096,464]{1,2,0:T(8,128)(2,1)} %param.5) | copy-start | bytes 11403268
  68.8 9.8 %copy-start.3 = (s32[4,16]{1,0:T(4,128)S(1)}, s32[4,16]{1,0:T(4,128)}, u32[]{:S(2)}) copy-start(s32[4,16]{1,0:T(4,128)} %param.7) | copy-start | bytes 772
  68.8 9.8 %copy-start.4 = (f32[16]{0:T(128)S(1)}, f32[16]{0:T(128)}, u32[]{:S(2)}) copy-start(f32[16]{0:T(128)} %param.8) | copy-start | bytes 196
  74.3 39.4 %all-to-all-start.3 = ((s16[16,32,512]{2,1,0:T(8,128)(2,1)}), s16[16,32,512]{2,1,0:T(8,128)(2,1)S(1)}, u32[]{:S(2)}, u32[]{:S(2)}) async-start(s16[16,32,512]{2,1,0:T(8,128)(2,1)} %bitcast.6), calls=%async_computation.3 | async-start | bytes 1048576 | tf_op jit(solution)/shard_map/all_to_all | solution.py:110

commit v6 on v5

v6 whole, which is shorter than its diff:
```python
import jax
import jax.numpy as jnp
from jax import lax
from jax.experimental import pallas as pl
from jax.experimental.pallas import tpu as pltpu
from jax.sharding import Mesh, PartitionSpec as P

BF16, F32, I16, I32 = jnp.bfloat16, jnp.float32, jnp.int16, jnp.int32
LANES = 512
TOP = 32767.0
AXES = ("x", "zh", "y", "zl", "c")


def spread(block, axes, count, groups=None):
    copies = jnp.broadcast_to(block[None], (count,) + block.shape)
    return lax.all_to_all(copies, axes, 0, 0, axis_index_groups=groups)


def lines(along):
    return [[(k * 4 + i) * 2 + along for i in range(4)] for k in range(4)] + [
        [(i * 4 + k) * 2 + 1 - along for i in range(4)] for k in range(4)
    ]


def encode(partial, out_ref):
    rows, width = partial.shape
    main = LANES - 128
    top = jnp.max(jnp.abs(partial), axis=1, keepdims=True)
    power = jnp.clip(jnp.floor(jnp.log2(top)), -80.0, 80.0)
    mantissa = jnp.ceil(top * jnp.exp2(-power) * 8192.0) + 1.0
    per_step = 1.0 / (mantissa * jnp.exp2(power) * (1.0 / (8192.0 * TOP)))
    tail = jnp.concatenate([partial[:, main:], jnp.zeros((rows, LANES - width), F32)], axis=1)
    tail = jnp.round(tail * per_step)
    column = lax.broadcasted_iota(I32, (rows, 128), 1) + main
    tail = jnp.where(column == width, mantissa, jnp.where(column == width + 1, power, tail))
    for codes, columns in ((jnp.round(partial[:, :main] * per_step), slice(0, main)), (tail, slice(main, LANES))):
        high = jnp.floor(codes * (1.0 / 256.0))
        out_ref[:rows, columns] = high.astype(BF16)
        out_ref[rows:, columns] = (codes - high * 256.0).astype(BF16)


def coded_kernel(rows_ref, w_ref, out_ref):
    encode(lax.dot_general(rows_ref[...], w_ref[...], (((1,), (1,)), ((), ())), preferred_element_type=F32), out_ref)


def pick_kernel(place_ref, own_ref, other_ref, out_ref):
    column = lax.broadcasted_iota(I32, (256, 256), 1)
    lane16, lane8 = lax.broadcasted_iota(I32, (16, 128), 1), lax.broadcasted_iota(I32, (8, 128), 1)
    for at in range(0, 512, 256):
        place = place_ref[at : at + 256]
        picks = []
        for half in (0, 256):
            found = place - half == column
            picks += [jnp.where(found, 256.0, 0.0).astype(BF16), jnp.where(found, 1.0, 0.0).astype(BF16)]
        codes = jnp.dot(jnp.concatenate(picks[:2], axis=1), own_ref[...], preferred_element_type=F32)
        codes += jnp.dot(jnp.concatenate(picks[2:], axis=1), other_ref[...], preferred_element_type=F32)
        for block in range(8):
            owner = at // 32 + block
            to = owner % 4 * 4 + owner // 4
            rows = codes[block * 32 : block * 32 + 32]
            tail = rows[:, 384:]
            fold = jnp.where(lane16 < 64, tail[:16], pltpu.roll(tail[16:], 64, 1))
            a, b, c, d = (pltpu.roll(tail[8 * i : 8 * i + 8], (64 + 32 * i) % 128, 1) for i in range(4))
            last = jnp.where(lane8 < 64, jnp.where(lane8 < 32, a, b), jnp.where(lane8 < 96, c, d))
            packed = jnp.concatenate([rows[:, :128], rows[:, 128:256], rows[:, 256:384], fold, last], axis=0)
            out_ref[to] = packed.astype(I32).astype(I16)


def decode_kernel(coefficient_ref, got_ref, out_ref):
    rows, cands, width = out_ref.shape
    lane = lax.broadcasted_iota(I32, (32, 128), 1)
    totals = [None] * cands
    for source in range(16):
        codes = got_ref[source].astype(I32).astype(F32)
        fold, last = codes[96:112], codes[112:120]
        folds = jnp.concatenate([fold, pltpu.roll(fold, 64, 1)], axis=0)
        lasts = jnp.concatenate([pltpu.roll(last, (64 - 32 * i) % 128, 1) for i in range(4)], axis=0)
        tail = jnp.where(lane < 64, folds, lasts)
        at = width % 128
        step = tail[:, at : at + 1] * jnp.exp2(tail[:, at + 1 : at + 2]) * (1.0 / (8192.0 * TOP))
        values = jnp.concatenate([codes[:32], codes[32:64], codes[64:96], tail], axis=1) * step
        for c in range(cands):
            term = coefficient_ref[c, source % 4 * 4 + source // 4] * values
            totals[c] = term if source == 0 else totals[c] + term
    out_ref[...] = jnp.stack([t[:, :width] for t in totals], axis=1).astype(BF16)


def on_device(weights, calib_pool, cand_index, coef_table, row_ids):
    core = lax.axis_index("c")
    swap = [(0, 1), (1, 0)]
    w_piece = weights[0].T
    own = spread(calib_pool.reshape(32, 128), ("zh", "zl"), 16).reshape(16, 4096)
    own = spread(own, ("x", "y", "c"), 4, lines(0)).reshape(64, 4096)
    own, w_mine = lax.optimization_barrier((own, w_piece))
    w_other = lax.ppermute(w_mine, "c", swap)
    own = spread(own, ("x", "y", "c"), 4, lines(1)).reshape(256, 4096)

    width = w_piece.shape[0]
    vmem = pl.BlockSpec(memory_space=pltpu.VMEM)
    params = pltpu.CompilerParams(vmem_limit_bytes=16 * 2**20)

    def coded(w):
        return pl.pallas_call(
            coded_kernel,
            out_shape=jax.ShapeDtypeStruct((512, LANES), BF16),
            in_specs=[vmem] * 2,
            out_specs=vmem,
            compiler_params=params,
            cost_estimate=pl.CostEstimate(flops=2 * 256 * 4096 * width, bytes_accessed=6 * 2**20, transcendentals=0),
            name="coded",
        )(own, w)

    from_other = lax.ppermute(coded(w_other), "c", swap)
    mine = coded(w_piece)

    x, zh, y, zl, c = (row_ids >> 7) & 3, (row_ids >> 5) & 3, (row_ids >> 3) & 3, (row_ids >> 1) & 3, row_ids & 1
    place = jnp.where(c == 0, x * 4 + y, y * 4 + x) * 16 + zh * 4 + zl + jnp.where(c == core, 0, 256)
    sent = pl.pallas_call(
        pick_kernel,
        out_shape=jax.ShapeDtypeStruct((16, 120, 128), I16),
        in_specs=[vmem] * 3,
        out_specs=vmem,
        compiler_params=params,
        cost_estimate=pl.CostEstimate(flops=2**29, bytes_accessed=2**21, transcendentals=0),
        name="pick",
    )(place[:, None], mine, from_other)
    got = lax.all_to_all(sent, ("zh", "x"), 0, 0)

    entries = jnp.arange(coef_table.shape[0], dtype=I32)
    onehot = (cand_index[:, :, None] == entries[None, None, :]).astype(F32)
    coefficient = jnp.sum(onehot * coef_table[None, None, :], axis=2)
    return pl.pallas_call(
        decode_kernel,
        out_shape=jax.ShapeDtypeStruct((32, 4, width), BF16),
        in_specs=[pl.BlockSpec(memory_space=pltpu.SMEM), vmem],
        out_specs=vmem,
        compiler_params=params,
        name="decode",
    )(coefficient, got)


def solution(mesh):
    fine = Mesh(mesh.devices.reshape(4, 4, 4, 4, 2), AXES)
    src, shard = ("x", "zh"), ("y", "zl", "c")
    placed = (P(src, None, shard), P(src + shard, None), P(), P(), P())
    return jax.shard_map(on_device, mesh=fine, in_specs=placed, out_specs=P(src, None, shard), check_vma=False)
```

time: 116 us -> 114 us (0.983)
  waiting for transfers between devices: 35.6 us -> 32.5 us
  starting transfers between devices: 6.19 us -> 8.11 us
    all_to_all x1, waiting for transfers between devices: 34.9 us -> 32.4 us  [on_device(): got = lax.all_to_all(sent, ('zh', 'x'), 0, 0)]
    ppermute x1 -> x2, starting transfers between devices: 1.91 us -> 3.83 us  [the longest x1 1.92 us: on_device(): from_other = lax.ppermute(coded(w_other), 'c', swap)]
    pallas_call x2 -> x3, Pallas kernels: 5.95 us -> 4.63 us  [the longest x2 3.02 us: coded(): pl.pallas_call(coded_kernel, out_shape=jax.ShapeDtypeStruct((512, LANES),...]
  transfers between devices with their start and end apart: 2 -> 3, of which waited for: 2 -> 1; matrix products, arithmetic and copies ran while one was open for 0% -> 0% of each run, Pallas kernels for 1% -> 1%
where the time goes in v6:
time: 114 us; the launch traced here: 113 us
  blocking collectives  62.2 us (55%)
  waiting for transfers between devices  32.5 us (29%)
  starting transfers between devices  8.11 us (7%)
  Pallas kernels  6.74 us (6%)
  local copies, waits for them, and re-layouts  2.59 us (2%)
    all_to_all x3, blocking collectives, spread(): return lax.all_to_all(copies, axes, 0, 0, axis_index_groups=groups)  62.2 us
    all_to_all x1, waiting for transfers between devices, on_device(): got = lax.all_to_all(sent, ('zh', 'x'), 0, 0)  32.4 us
    all_to_all x1, starting transfers between devices, on_device(): got = lax.all_to_all(sent, ('zh', 'x'), 0, 0)  4.28 us
    pallas_call x2, Pallas kernels, coded(): pl.pallas_call(coded_kernel, out_shape=jax.ShapeDtypeStruct((512, LANES),...  3.02 us
  transfers between devices with their start and end apart: 3, of which 1 were waited for; matrix products, arithmetic and copies ran while one was open for 0% of the time, Pallas kernels for 1%

profile of v6, /device:TPU:32, one launch (start us, length us, event | category | flops | bytes accessed | tf_op | source)
XLA Modules:
  0.0 113.1 jit_solution(15081200929947620453)
XLA Ops:
  0.0 0.8 reduce
  0.8 29.2 %all_to_all.20 = bf16[16,32,128]{2,1,0:T(8,128)(2,1)S(1)} all-to-all(bf16[16,32,128]{2,1,0:T(8,128)(2,1)S(1)} %broadcast_in_dim.35), channel_id=1, replica_groups=mesh['x'=4,'zh'=4,'y'=4,'zl'=4,'c'=2] {'zh','zl'}, dimensions={0} | all-to-all | bytes 262144 | tf_op jit(solution)/shard_map/all_to_all | solution.py:16
  30.0 0.1 copy.10
  30.1 12.3 %all_to_all.21 = bf16[4,16,4096]{2,1,0:T(8,128)(2,1)S(1)} all-to-all(bf16[4,16,4096]{2,1,0:T(8,128)(2,1)S(1)} %broadcast_in_dim.37), channel_id=1, replica_groups={{0,8,16,24},{128,136,144,152},{256,264,272,280},{384,392,400,408},{1,12..., dimensions={0} | all-to-all | bytes 1048576 | tf_op jit(solution)/shard_map/all_to_all | solution.py:16
  42.5 1.9 %collective-permute-start = (bf16[464,4096]{1,0:T(8,128)(2,1)}, bf16[464,4096]{1,0:T(8,128)(2,1)S(1)}, u32[]{:S(2)}, u32[]{:S(2)}) collective-permute-start(bf16[464,4096]{1,0:T(8,128)(2,1)} %bitcast.13), channel_id=1, source_target_pairs={{0,1},{1,0},{2,3},{3,2},{4,5},{5,4},{6,7},{7,6},{8,9},{9,8},{10,11... | collective-permute-start | bytes 11403272 | tf_op jit(solution)/shard_map/ppermute | solution.py:95
  44.4 0.2 broadcast_in_dim.38
  44.6 20.6 %all_to_all.22 = bf16[4,64,4096]{2,1,0:T(8,128)(2,1)S(1)} all-to-all(bf16[4,64,4096]{2,1,0:T(8,128)(2,1)S(1)} %broadcast_in_dim.38), channel_id=1, replica_groups={{1,9,17,25},{129,137,145,153},{257,265,273,281},{385,393,401,409},{0,12..., dimensions={0} | all-to-all | bytes 4194304 | tf_op jit(solution)/shard_map/all_to_all | solution.py:16
  65.2 0.0 copy-start.1
  65.2 0.0 collective-permute-done.w_ref
  65.2 1.5 %coded.3 = bf16[512,512]{1,0:T(8,128)(2,1)S(1)} custom-call(bf16[256,4096]{1,0:T(8,128)(2,1)S(1)} %bitcast.11, bf16[464,4096]{1,0:T(8,128)(2,1)S(1)} %collective-permute-done.w_ref), custom_call_target="tpu_custom_call" | custom-call | flops 973078528 | bytes 6291456 | tf_op jit(solution)/shard_map/coded/pallas_call | solution.py:103
  66.8 1.9 %collective-permute-start.1 = (bf16[512,512]{1,0:T(8,128)(2,1)S(1)}, bf16[512,512]{1,0:T(8,128)(2,1)S(1)}, u32[]{:S(2)}, u32[]{:S(2)}) collective-permute-start(bf16[512,512]{1,0:T(8,128)(2,1)S(1)} %coded.3), channel_id=1, source_target_pairs={{0,1},{1,0},{2,3},{3,2},{4,5},{5,4},{6,7},{7,6},{8,9},{9,8},{10,11... | collective-permute-start | bytes 1572872 | tf_op jit(solution)/shard_map/ppermute | solution.py:113
  68.7 0.0 copy-done.1
  68.7 0.1 copy.7.place_ref
  68.9 0.0 copy-start
  68.9 2.1 %copy-done = bf16[1,4096,464]{1,2,0:T(8,128)(2,1)S(1)} copy-done((bf16[1,4096,464]{1,2,0:T(8,128)(2,1)S(1)}, bf16[1,4096,464]{1,2,0:T(8,128)(2,1)}, u32[]{:S(2)}) %copy-start) | copy-done | bytes 3801112
  71.0 0.0 copy-start.2
  71.0 0.0 copy-start.3
  71.0 1.5 %coded.2.own_ref = bf16[512,512]{1,0:T(8,128)(2,1)S(1)} custom-call(bf16[256,4096]{1,0:T(8,128)(2,1)S(1)} %bitcast.12, bf16[464,4096]{1,0:T(8,128)(2,1)S(1)} %bitcast.14), custom_call_target="tpu_custom_call" | custom-call | flops 973078528 | bytes 6291456 | tf_op jit(solution)/shard_map/coded/pallas_call | solution.py:103
  72.5 0.0 collective-permute-done.1.other_ref
  72.5 1.6 %pick.1 = s16[16,120,128]{2,1,0:T(8,128)(2,1)} custom-call(s32[512,1]{1,0:T(8,128)S(1)} %copy.7.place_ref, bf16[512,512]{1,0:T(8,128)(2,1)S(1)} %coded.2.own_ref, bf16[512,512]{1,0:T(8,128)(2,1)S(1)} %collective-permute-done.1.other_ref), custom_call_target="tpu_custom_call" | custom-call | flops 536870912 | bytes 2097152 | tf_op jit(solution)/shard_map/pick/pallas_call | solution.py:118
  74.1 4.3 %all-to-all-start.3 = ((s16[16,120,128]{2,1,0:T(8,128)(2,1)}), s16[16,120,128]{2,1,0:T(8,128)(2,1)S(1)}, u32[]{:S(2)}, u32[]{:S(2)}) async-start(s16[16,120,128]{2,1,0:T(8,128)(2,1)} %pick.1), calls=%async_computation.3 | async-start | bytes 983040 | tf_op jit(solution)/shard_map/all_to_all | solution.py:127
  78.4 0.0 copy-done.2
  78.4 0.0 copy-done.3
  78.4 0.2 select_reduce_fusion.coefficient_ref
  78.6 32.4 %all-to-all-done.3.got_ref = s16[16,120,128]{2,1,0:T(8,128)(2,1)S(1)} async-done(((s16[16,120,128]{2,1,0:T(8,128)(2,1)}), s16[16,120,128]{2,1,0:T(8,128)(2,1)S(1)}, u32[]{:S(2)}, u32[]{:S(2)}) %all-to-all-start.3) | async-done | bytes 491552 | tf_op jit(solution)/shard_map/all_to_all | solution.py:127
  111.0 2.1 %decode.1 = bf16[32,4,464]{2,1,0:T(4,128)(2,1)} custom-call(f32[4,16]{1,0:T(4,128)S(1)} %select_reduce_fusion.coefficient_ref, s16[16,120,128]{2,1,0:T(8,128)(2,1)S(1)} %all-to-all-done.3.got_ref), custom_call_target="tpu_custom_call" | custom-call | tf_op jit(solution)/shard_map/decode/pallas_call | solution.py:132
  (3 shorter events, 0.1 us)
Async XLA Ops:
  42.5 22.8 %collective-permute-start = (bf16[464,4096]{1,0:T(8,128)(2,1)}, bf16[464,4096]{1,0:T(8,128)(2,1)S(1)}, u32[]{:S(2)}, u32[]{:S(2)}) collective-permute-start(bf16[464,4096]{1,0:T(8,128)(2,1)} %bitcast.13), channel_id=1, source_target_pairs={{0,1},{1,0},{2,3},{3,2},{4,5},{5,4},{6,7},{7,6},{8,9},{9,8},{10,11... | collective-permute-start | bytes 11403272 | tf_op jit(solution)/shard_map/ppermute | solution.py:95
  65.2 3.5 %copy-start.1 = (s32[512]{0:T(512)S(1)}, s32[512]{0:T(512)}, u32[]{:S(2)}) copy-start(s32[512]{0:T(512)} %param.9) | copy-start | bytes 6148
  66.8 5.7 %collective-permute-start.1 = (bf16[512,512]{1,0:T(8,128)(2,1)S(1)}, bf16[512,512]{1,0:T(8,128)(2,1)S(1)}, u32[]{:S(2)}, u32[]{:S(2)}) collective-permute-start(bf16[512,512]{1,0:T(8,128)(2,1)S(1)} %coded.3), channel_id=1, source_target_pairs={{0,1},{1,0},{2,3},{3,2},{4,5},{5,4},{6,7},{7,6},{8,9},{9,8},{10,11... | collective-permute-start | bytes 1572872 | tf_op jit(solution)/shard_map/ppermute | solution.py:113
  68.9 2.1 %copy-start = (bf16[1,4096,464]{1,2,0:T(8,128)(2,1)S(1)}, bf16[1,4096,464]{1,2,0:T(8,128)(2,1)}, u32[]{:S(2)}) copy-start(bf16[1,4096,464]{1,2,0:T(8,128)(2,1)} %param.5) | copy-start | bytes 11403268
  71.0 7.4 %copy-start.2 = (s32[4,16]{1,0:T(4,128)S(1)}, s32[4,16]{1,0:T(4,128)}, u32[]{:S(2)}) copy-start(s32[4,16]{1,0:T(4,128)} %param.7) | copy-start | bytes 772
  71.0 7.4 %copy-start.3 = (f32[16]{0:T(128)S(1)}, f32[16]{0:T(128)}, u32[]{:S(2)}) copy-start(f32[16]{0:T(128)} %param.8) | copy-start | bytes 196
  74.1 36.9 %all-to-all-start.3 = ((s16[16,120,128]{2,1,0:T(8,128)(2,1)}), s16[16,120,128]{2,1,0:T(8,128)(2,1)S(1)}, u32[]{:S(2)}, u32[]{:S(2)}) async-start(s16[16,120,128]{2,1,0:T(8,128)(2,1)} %pick.1), calls=%async_computation.3 | async-start | bytes 983040 | tf_op jit(solution)/shard_map/all_to_all | solution.py:127

commit v7 on v6

--- a/solution.py
+++ b/solution.py
@@ -43,6 +43,23 @@
     encode(lax.dot_general(rows_ref[...], w_ref[...], (((1,), (1,)), ((), ())), preferred_element_type=F32), out_ref)
 
 
+def streamed_kernel(rows_ref, w_ref, out_ref, w_here, arrived):
+    pieces, _, depth = w_here.shape
+    copies = [
+        pltpu.make_async_copy(w_ref.at[:, pl.ds(k * depth, depth)], w_here.at[k], arrived.at[k]) for k in range(pieces)
+    ]
+    for copy in copies:
+        copy.start()
+    total = None
+    for k, copy in enumerate(copies):
+        copy.wait()
+        term = lax.dot_general(
+            rows_ref[:, k * depth : (k + 1) * depth], w_here[k], (((1,), (1,)), ((), ())), preferred_element_type=F32
+        )
+        total = term if k == 0 else total + term
+    encode(total, out_ref)
+
+
 def pick_kernel(place_ref, own_ref, other_ref, out_ref):
     column = lax.broadcasted_iota(I32, (256, 256), 1)
     lane16, lane8 = lax.broadcasted_iota(I32, (16, 128), 1), lax.broadcasted_iota(I32, (8, 128), 1)
@@ -66,23 +83,33 @@
             out_ref[to] = packed.astype(I32).astype(I16)
 
 
-def decode_kernel(coefficient_ref, got_ref, out_ref):
+def decode_kernel(coefficient_ref, got_ref, out_ref, tail_ref, step_ref):
     rows, cands, width = out_ref.shape
-    lane = lax.broadcasted_iota(I32, (32, 128), 1)
-    totals = [None] * cands
+    lane = lax.broadcasted_iota(I32, (rows, 128), 1)
+    at = width % 128
     for source in range(16):
-        codes = got_ref[source].astype(I32).astype(F32)
-        fold, last = codes[96:112], codes[112:120]
+        codes = got_ref[source, 96:].astype(I32).astype(F32)
+        fold, last = codes[:16], codes[16:]
         folds = jnp.concatenate([fold, pltpu.roll(fold, 64, 1)], axis=0)
         lasts = jnp.concatenate([pltpu.roll(last, (64 - 32 * i) % 128, 1) for i in range(4)], axis=0)
         tail = jnp.where(lane < 64, folds, lasts)
-        at = width % 128
         step = tail[:, at : at + 1] * jnp.exp2(tail[:, at + 1 : at + 2]) * (1.0 / (8192.0 * TOP))
-        values = jnp.concatenate([codes[:32], codes[32:64], codes[64:96], tail], axis=1) * step
-        for c in range(cands):
-            term = coefficient_ref[c, source % 4 * 4 + source // 4] * values
-            totals[c] = term if source == 0 else totals[c] + term
-    out_ref[...] = jnp.stack([t[:, :width] for t in totals], axis=1).astype(BF16)
+        tail_ref[source] = tail * step
+        step_ref[source] = jnp.broadcast_to(step, (rows, 128))
+    for block in range(4):
+        totals = [None] * cands
+        for source in range(16):
+            if block < 3:
+                codes = got_ref[source, 32 * block : 32 * block + 32].astype(I32).astype(F32)
+                values = codes * step_ref[source]
+            else:
+                values = tail_ref[source]
+            for c in range(cands):
+                term = coefficient_ref[c, source % 4 * 4 + source // 4] * values
+                totals[c] = term if source == 0 else totals[c] + term
+        columns = slice(128 * block, min(128 * block + 128, width))
+        stacked = jnp.stack([t[:, : columns.stop - columns.start] for t in totals], axis=1)
+        out_ref[:, :, columns] = stacked.astype(BF16)
 
 
 def on_device(weights, calib_pool, cand_index, coef_table, row_ids):
@@ -99,19 +126,22 @@
     vmem = pl.BlockSpec(memory_space=pltpu.VMEM)
     params = pltpu.CompilerParams(vmem_limit_bytes=16 * 2**20)
 
-    def coded(w):
+    def coded(kernel, w, w_spec, scratch):
         return pl.pallas_call(
-            coded_kernel,
+            kernel,
             out_shape=jax.ShapeDtypeStruct((512, LANES), BF16),
-            in_specs=[vmem] * 2,
+            in_specs=[vmem, w_spec],
             out_specs=vmem,
+            scratch_shapes=scratch,
             compiler_params=params,
             cost_estimate=pl.CostEstimate(flops=2 * 256 * 4096 * width, bytes_accessed=6 * 2**20, transcendentals=0),
             name="coded",
         )(own, w)
 
-    from_other = lax.ppermute(coded(w_other), "c", swap)
-    mine = coded(w_piece)
+    from_other = lax.ppermute(coded(coded_kernel, w_other, vmem, []), "c", swap)
+    pieces = [pltpu.VMEM((4, width, 1024), BF16), pltpu.SemaphoreType.DMA((4,))]
+    here = pltpu.with_memory_space_constraint(w_piece, pltpu.HBM)
+    mine = coded(streamed_kernel, here, pl.BlockSpec(memory_space=pltpu.HBM), pieces)
 
     x, zh, y, zl, c = (row_ids >> 7) & 3, (row_ids >> 5) & 3, (row_ids >> 3) & 3, (row_ids >> 1) & 3, row_ids & 1
     place = jnp.where(c == 0, x * 4 + y, y * 4 + x) * 16 + zh * 4 + zl + jnp.where(c == core, 0, 256)
@@ -135,6 +165,7 @@
         in_specs=[pl.BlockSpec(memory_space=pltpu.SMEM), vmem],
         out_specs=vmem,
         compiler_params=params,
+        scratch_shapes=[pltpu.VMEM((16, 32, 128), F32)] * 2,
         name="decode",
     )(coefficient, got)
 

time: 114 us -> 113 us (level)
  local copies, waits for them, and re-layouts: 2.59 us -> 0.52 us
  Pallas kernels: 6.74 us -> 8.51 us
    unnamed x9 -> x7, local copies, waits for them, and re-layouts: 2.14 us -> 0.07 us
    pallas_call x2, Pallas kernels: 3.02 us -> 4.72 us  [coded(): pl.pallas_call(kernel, out_shape=jax.ShapeDtypeStruct((512, LANES), BF16)...]
  transfers between devices with their start and end apart: 3 -> 3, of which waited for: 1 -> 1; matrix products, arithmetic and copies ran while one was open for 0% -> 0% of each run, Pallas kernels for 1% -> 3%
where the time goes in v7:
time: 113 us
  blocking collectives  62.2 us (55%)
  waiting for transfers between devices  32.4 us (29%)
  Pallas kernels  8.51 us (8%)
  starting transfers between devices  8.12 us (7%)
    all_to_all x3, blocking collectives, spread(): return lax.all_to_all(copies, axes, 0, 0, axis_index_groups=groups)  62.2 us
    all_to_all x1, waiting for transfers between devices, on_device(): got = lax.all_to_all(sent, ('zh', 'x'), 0, 0)  32.4 us
    pallas_call x2, Pallas kernels, coded(): pl.pallas_call(kernel, out_shape=jax.ShapeDtypeStruct((512, LANES), BF16)...  4.72 us
    all_to_all x1, starting transfers between devices, on_device(): got = lax.all_to_all(sent, ('zh', 'x'), 0, 0)  4.29 us
  transfers between devices with their start and end apart: 3, of which 1 were waited for; matrix products, arithmetic and copies ran while one was open for 0% of the time, Pallas kernels for 3%

profile of v7, /device:TPU:32, one launch (start us, length us, event | category | flops | bytes accessed | tf_op | source)
XLA Modules:
  0.0 112.8 jit_solution(2860119875875288022)
XLA Ops:
  0.0 0.8 reduce
  0.8 29.2 %all_to_all.20 = bf16[16,32,128]{2,1,0:T(8,128)(2,1)S(1)} all-to-all(bf16[16,32,128]{2,1,0:T(8,128)(2,1)S(1)} %broadcast_in_dim.35), channel_id=1, replica_groups=mesh['x'=4,'zh'=4,'y'=4,'zl'=4,'c'=2] {'zh','zl'}, dimensions={0} | all-to-all | bytes 262144 | tf_op jit(solution)/shard_map/all_to_all | solution.py:16
  30.0 0.1 copy.10
  30.1 12.3 %all_to_all.21 = bf16[4,16,4096]{2,1,0:T(8,128)(2,1)S(1)} all-to-all(bf16[4,16,4096]{2,1,0:T(8,128)(2,1)S(1)} %broadcast_in_dim.37), channel_id=1, replica_groups={{0,8,16,24},{128,136,144,152},{256,264,272,280},{384,392,400,408},{1,12..., dimensions={0} | all-to-all | bytes 1048576 | tf_op jit(solution)/shard_map/all_to_all | solution.py:16
  42.5 1.9 %collective-permute-start = (bf16[464,4096]{1,0:T(8,128)(2,1)}, bf16[464,4096]{1,0:T(8,128)(2,1)S(1)}, u32[]{:S(2)}, u32[]{:S(2)}) collective-permute-start(bf16[464,4096]{1,0:T(8,128)(2,1)} %bitcast.13), channel_id=1, source_target_pairs={{0,1},{1,0},{2,3},{3,2},{4,5},{5,4},{6,7},{7,6},{8,9},{9,8},{10,11... | collective-permute-start | bytes 11403272 | tf_op jit(solution)/shard_map/ppermute | solution.py:122
  44.4 0.2 broadcast_in_dim.38
  44.6 20.6 %all_to_all.22 = bf16[4,64,4096]{2,1,0:T(8,128)(2,1)S(1)} all-to-all(bf16[4,64,4096]{2,1,0:T(8,128)(2,1)S(1)} %broadcast_in_dim.38), channel_id=1, replica_groups={{1,9,17,25},{129,137,145,153},{257,265,273,281},{385,393,401,409},{0,12..., dimensions={0} | all-to-all | bytes 4194304 | tf_op jit(solution)/shard_map/all_to_all | solution.py:16
  65.2 0.0 copy-start
  65.2 0.0 collective-permute-done.w_ref
  65.2 1.5 %coded.3 = bf16[512,512]{1,0:T(8,128)(2,1)S(1)} custom-call(bf16[256,4096]{1,0:T(8,128)(2,1)S(1)} %bitcast.11, bf16[464,4096]{1,0:T(8,128)(2,1)S(1)} %collective-permute-done.w_ref), custom_call_target="tpu_custom_call" | custom-call | flops 973078528 | bytes 6291456 | tf_op jit(solution)/shard_map/coded/pallas_call | solution.py:130
  66.8 1.9 %collective-permute-start.1 = (bf16[512,512]{1,0:T(8,128)(2,1)S(1)}, bf16[512,512]{1,0:T(8,128)(2,1)S(1)}, u32[]{:S(2)}, u32[]{:S(2)}) collective-permute-start(bf16[512,512]{1,0:T(8,128)(2,1)S(1)} %coded.3), channel_id=1, source_target_pairs={{0,1},{1,0},{2,3},{3,2},{4,5},{5,4},{6,7},{7,6},{8,9},{9,8},{10,11... | collective-permute-start | bytes 1572872 | tf_op jit(solution)/shard_map/ppermute | solution.py:141
  68.7 0.0 copy-done
  68.7 0.1 copy.7.place_ref
  68.9 0.0 copy-start.1
  68.9 0.0 copy-start.2
  68.9 3.2 %coded.2.own_ref = bf16[512,512]{1,0:T(8,128)(2,1)S(1)} custom-call(bf16[256,4096]{1,0:T(8,128)(2,1)S(1)} %bitcast.12, bf16[464,4096]{1,0:T(8,128)(2,1)} %bitcast.14), custom_call_target="tpu_custom_call" | custom-call | flops 973078528 | bytes 6291456 | tf_op jit(solution)/shard_map/coded/pallas_call | solution.py:130
  72.1 0.0 collective-permute-done.1.other_ref
  72.1 1.6 %pick.1 = s16[16,120,128]{2,1,0:T(8,128)(2,1)} custom-call(s32[512,1]{1,0:T(8,128)S(1)} %copy.7.place_ref, bf16[512,512]{1,0:T(8,128)(2,1)S(1)} %coded.2.own_ref, bf16[512,512]{1,0:T(8,128)(2,1)S(1)} %collective-permute-done.1.other_ref), custom_call_target="tpu_custom_call" | custom-call | flops 536870912 | bytes 2097152 | tf_op jit(solution)/shard_map/pick/pallas_call | solution.py:148
  73.7 4.3 %all-to-all-start.3 = ((s16[16,120,128]{2,1,0:T(8,128)(2,1)}), s16[16,120,128]{2,1,0:T(8,128)(2,1)S(1)}, u32[]{:S(2)}, u32[]{:S(2)}) async-start(s16[16,120,128]{2,1,0:T(8,128)(2,1)} %pick.1), calls=%async_computation.3 | async-start | bytes 983040 | tf_op jit(solution)/shard_map/all_to_all | solution.py:157
  78.0 0.0 copy-done.1
  78.0 0.0 copy-done.2
  78.1 0.2 select_reduce_fusion.coefficient_ref
  78.2 32.4 %all-to-all-done.3.got_ref = s16[16,120,128]{2,1,0:T(8,128)(2,1)S(1)} async-done(((s16[16,120,128]{2,1,0:T(8,128)(2,1)}), s16[16,120,128]{2,1,0:T(8,128)(2,1)S(1)}, u32[]{:S(2)}, u32[]{:S(2)}) %all-to-all-start.3) | async-done | bytes 491552 | tf_op jit(solution)/shard_map/all_to_all | solution.py:157
  110.6 2.2 %decode.1 = bf16[32,4,464]{2,1,0:T(4,128)(2,1)} custom-call(f32[4,16]{1,0:T(4,128)S(1)} %select_reduce_fusion.coefficient_ref, s16[16,120,128]{2,1,0:T(8,128)(2,1)S(1)} %all-to-all-done.3.got_ref), custom_call_target="tpu_custom_call" | custom-call | tf_op jit(solution)/shard_map/decode/pallas_call | solution.py:162
  (3 shorter events, 0.1 us)
Async XLA Ops:
  42.5 22.8 %collective-permute-start = (bf16[464,4096]{1,0:T(8,128)(2,1)}, bf16[464,4096]{1,0:T(8,128)(2,1)S(1)}, u32[]{:S(2)}, u32[]{:S(2)}) collective-permute-start(bf16[464,4096]{1,0:T(8,128)(2,1)} %bitcast.13), channel_id=1, source_target_pairs={{0,1},{1,0},{2,3},{3,2},{4,5},{5,4},{6,7},{7,6},{8,9},{9,8},{10,11... | collective-permute-start | bytes 11403272 | tf_op jit(solution)/shard_map/ppermute | solution.py:122
  65.2 3.5 %copy-start = (s32[512]{0:T(512)S(1)}, s32[512]{0:T(512)}, u32[]{:S(2)}) copy-start(s32[512]{0:T(512)} %param.9) | copy-start | bytes 6148
  66.8 5.4 %collective-permute-start.1 = (bf16[512,512]{1,0:T(8,128)(2,1)S(1)}, bf16[512,512]{1,0:T(8,128)(2,1)S(1)}, u32[]{:S(2)}, u32[]{:S(2)}) collective-permute-start(bf16[512,512]{1,0:T(8,128)(2,1)S(1)} %coded.3), channel_id=1, source_target_pairs={{0,1},{1,0},{2,3},{3,2},{4,5},{5,4},{6,7},{7,6},{8,9},{9,8},{10,11... | collective-permute-start | bytes 1572872 | tf_op jit(solution)/shard_map/ppermute | solution.py:141
  68.9 9.2 %copy-start.1 = (s32[4,16]{1,0:T(4,128)S(1)}, s32[4,16]{1,0:T(4,128)}, u32[]{:S(2)}) copy-start(s32[4,16]{1,0:T(4,128)} %param.7) | copy-start | bytes 772
  68.9 9.2 %copy-start.2 = (f32[16]{0:T(128)S(1)}, f32[16]{0:T(128)}, u32[]{:S(2)}) copy-start(f32[16]{0:T(128)} %param.8) | copy-start | bytes 196
  73.7 36.9 %all-to-all-start.3 = ((s16[16,120,128]{2,1,0:T(8,128)(2,1)}), s16[16,120,128]{2,1,0:T(8,128)(2,1)S(1)}, u32[]{:S(2)}, u32[]{:S(2)}) async-start(s16[16,120,128]{2,1,0:T(8,128)(2,1)} %pick.1), calls=%async_computation.3 | async-start | bytes 983040 | tf_op jit(solution)/shard_map/all_to_all | solution.py:157

commit v8 on v7

--- a/solution.py
+++ b/solution.py
@@ -11,15 +11,8 @@
 AXES = ("x", "zh", "y", "zl", "c")
 
 
-def spread(block, axes, count, groups=None):
-    copies = jnp.broadcast_to(block[None], (count,) + block.shape)
-    return lax.all_to_all(copies, axes, 0, 0, axis_index_groups=groups)
-
-
-def lines(along):
-    return [[(k * 4 + i) * 2 + along for i in range(4)] for k in range(4)] + [
-        [(i * 4 + k) * 2 + 1 - along for i in range(4)] for k in range(4)
-    ]
+def spread(block, axes):
+    return lax.all_to_all(jnp.broadcast_to(block[None], (16,) + block.shape), axes, 0, 0)
 
 
 def encode(partial, out_ref):
@@ -39,38 +32,43 @@
         out_ref[rows:, columns] = (codes - high * 256.0).astype(BF16)
 
 
-def coded_kernel(rows_ref, w_ref, out_ref):
-    encode(lax.dot_general(rows_ref[...], w_ref[...], (((1,), (1,)), ((), ())), preferred_element_type=F32), out_ref)
+def times(rows, weights):
+    return lax.dot_general(rows, weights, (((1,), (1,)), ((), ())), preferred_element_type=F32)
 
 
-def streamed_kernel(rows_ref, w_ref, out_ref, w_here, arrived):
-    pieces, _, depth = w_here.shape
-    copies = [
-        pltpu.make_async_copy(w_ref.at[:, pl.ds(k * depth, depth)], w_here.at[k], arrived.at[k]) for k in range(pieces)
-    ]
-    for copy in copies:
-        copy.start()
+def picked(place, half, bytes_ref):
+    found = place - half == lax.broadcasted_iota(I32, (place.shape[0], 256), 1)
+    pick = jnp.concatenate([jnp.where(found, 256.0, 0.0), jnp.where(found, 1.0, 0.0)], axis=1).astype(BF16)
+    return jnp.dot(pick, bytes_ref[...], preferred_element_type=F32)
+
+
+def product(rows_ref, w_ref, far_ref, near_ref, arrived):
+    pieces = arrived.shape[0]
+    depth = far_ref.shape[1] // pieces
+    copies = []
+    for k in range(pieces):
+        part = pl.ds(k * depth, depth)
+        copies.append(pltpu.make_async_copy(far_ref.at[:, part], near_ref.at[:, part], arrived.at[k]))
+        copies[k].start()
     total = None
     for k, copy in enumerate(copies):
         copy.wait()
-        term = lax.dot_general(
-            rows_ref[:, k * depth : (k + 1) * depth], w_here[k], (((1,), (1,)), ((), ())), preferred_element_type=F32
-        )
+        part = slice(k * depth, (k + 1) * depth)
+        term = times(rows_ref[:, part], w_ref[:, part])
         total = term if k == 0 else total + term
-    encode(total, out_ref)
+    return total
 
 
-def pick_kernel(place_ref, own_ref, other_ref, out_ref):
-    column = lax.broadcasted_iota(I32, (256, 256), 1)
+def own_kernel(place_ref, rows_ref, far_ref, out_ref, w_ref, bytes_ref, arrived):
+    encode(product(rows_ref, w_ref, far_ref, w_ref, arrived), bytes_ref)
+    out_ref[...] = picked(place_ref[...], 0, bytes_ref)
+
+
+def other_kernel(place_ref, far_ref, w_ref, own_ref, out_ref, rows_ref, bytes_ref, arrived):
+    encode(product(rows_ref, w_ref, far_ref, rows_ref, arrived), bytes_ref)
     lane16, lane8 = lax.broadcasted_iota(I32, (16, 128), 1), lax.broadcasted_iota(I32, (8, 128), 1)
     for at in range(0, 512, 256):
-        place = place_ref[at : at + 256]
-        picks = []
-        for half in (0, 256):
-            found = place - half == column
-            picks += [jnp.where(found, 256.0, 0.0).astype(BF16), jnp.where(found, 1.0, 0.0).astype(BF16)]
-        codes = jnp.dot(jnp.concatenate(picks[:2], axis=1), own_ref[...], preferred_element_type=F32)
-        codes += jnp.dot(jnp.concatenate(picks[2:], axis=1), other_ref[...], preferred_element_type=F32)
+        codes = own_ref[at : at + 256] + picked(place_ref[at : at + 256], 256, bytes_ref)
         for block in range(8):
             owner = at // 32 + block
             to = owner % 4 * 4 + owner // 4
@@ -114,46 +112,38 @@
 
 def on_device(weights, calib_pool, cand_index, coef_table, row_ids):
     core = lax.axis_index("c")
-    swap = [(0, 1), (1, 0)]
     w_piece = weights[0].T
-    own = spread(calib_pool.reshape(32, 128), ("zh", "zl"), 16).reshape(16, 4096)
-    own = spread(own, ("x", "y", "c"), 4, lines(0)).reshape(64, 4096)
-    own, w_mine = lax.optimization_barrier((own, w_piece))
-    w_other = lax.ppermute(w_mine, "c", swap)
-    own = spread(own, ("x", "y", "c"), 4, lines(1)).reshape(256, 4096)
+    own = spread(calib_pool.reshape(32, 128), ("zh", "zl")).reshape(16, 4096)
+    own = spread(own, ("x", "y")).reshape(256, 4096)
+    other = lax.ppermute(own, "c", [(0, 1), (1, 0)])
+
+    x, zh, y, zl, c = (row_ids >> 7) & 3, (row_ids >> 5) & 3, (row_ids >> 3) & 3, (row_ids >> 1) & 3, row_ids & 1
+    place = (((x * 4 + y) * 4 + zh) * 4 + zl + jnp.where(c == core, 0, 256))[:, None]
 
     width = w_piece.shape[0]
-    vmem = pl.BlockSpec(memory_space=pltpu.VMEM)
+    vmem, far = pl.BlockSpec(memory_space=pltpu.VMEM), pl.BlockSpec(memory_space=pltpu.HBM)
     params = pltpu.CompilerParams(vmem_limit_bytes=16 * 2**20)
-
-    def coded(kernel, w, w_spec, scratch):
-        return pl.pallas_call(
-            kernel,
-            out_shape=jax.ShapeDtypeStruct((512, LANES), BF16),
-            in_specs=[vmem, w_spec],
-            out_specs=vmem,
-            scratch_shapes=scratch,
-            compiler_params=params,
-            cost_estimate=pl.CostEstimate(flops=2 * 256 * 4096 * width, bytes_accessed=6 * 2**20, transcendentals=0),
-            name="coded",
-        )(own, w)
-
-    from_other = lax.ppermute(coded(coded_kernel, w_other, vmem, []), "c", swap)
-    pieces = [pltpu.VMEM((4, width, 1024), BF16), pltpu.SemaphoreType.DMA((4,))]
-    here = pltpu.with_memory_space_constraint(w_piece, pltpu.HBM)
-    mine = coded(streamed_kernel, here, pl.BlockSpec(memory_space=pltpu.HBM), pieces)
-
-    x, zh, y, zl, c = (row_ids >> 7) & 3, (row_ids >> 5) & 3, (row_ids >> 3) & 3, (row_ids >> 1) & 3, row_ids & 1
-    place = jnp.where(c == 0, x * 4 + y, y * 4 + x) * 16 + zh * 4 + zl + jnp.where(c == core, 0, 256)
+    cost = pl.CostEstimate(flops=2 * 256 * 4096 * width, bytes_accessed=6 * 2**20, transcendentals=0)
+    codes, w_here = pl.pallas_call(
+        own_kernel,
+        out_shape=(jax.ShapeDtypeStruct((512, LANES), F32), jax.ShapeDtypeStruct(w_piece.shape, BF16)),
+        in_specs=[vmem, vmem, far],
+        out_specs=(vmem, vmem),
+        scratch_shapes=[pltpu.VMEM((512, LANES), BF16), pltpu.SemaphoreType.DMA((4,))],
+        compiler_params=params,
+        cost_estimate=cost,
+        name="own",
+    )(place, own, pltpu.with_memory_space_constraint(w_piece, pltpu.HBM))
     sent = pl.pallas_call(
-        pick_kernel,
+        other_kernel,
         out_shape=jax.ShapeDtypeStruct((16, 120, 128), I16),
-        in_specs=[vmem] * 3,
+        in_specs=[vmem, far, vmem, vmem],
         out_specs=vmem,
+        scratch_shapes=[pltpu.VMEM((256, 4096), BF16), pltpu.VMEM((512, LANES), BF16), pltpu.SemaphoreType.DMA((4,))],
         compiler_params=params,
-        cost_estimate=pl.CostEstimate(flops=2**29, bytes_accessed=2**21, transcendentals=0),
-        name="pick",
-    )(place[:, None], mine, from_other)
+        cost_estimate=cost,
+        name="other",
+    )(place, pltpu.with_memory_space_constraint(other, pltpu.HBM), w_here, codes)
     got = lax.all_to_all(sent, ("zh", "x"), 0, 0)
 
     entries = jnp.arange(coef_table.shape[0], dtype=I32)

time: 113 us -> 113 us (level)
  the two profiles are of different devices: /device:TPU:32 before, /device:TPU:68 now
where the time goes in v8:
time: 113 us
  blocking collectives  58.8 us (52%)
  waiting for transfers between devices  32.2 us (28%)
  starting transfers between devices  10.3 us (9%)
  Pallas kernels  10 us (9%)
    all_to_all x2, blocking collectives, spread(): lax.all_to_all(jnp.broadcast_to(block[None], (16,) + block.shape), axes,...  58.8 us
    all_to_all x1, waiting for transfers between devices, on_device(): got = lax.all_to_all(sent, ('zh', 'x'), 0, 0)  31.7 us
    all_to_all x1, starting transfers between devices, on_device(): got = lax.all_to_all(sent, ('zh', 'x'), 0, 0)  8.36 us
    pallas_call x1, Pallas kernels, on_device(): pl.pallas_call(other_kernel, out_shape=jax.ShapeDtypeStruct((16, 120, 128...  4.23 us
    pallas_call x1, Pallas kernels, on_device(): pl.pallas_call(own_kernel, out_shape=(jax.ShapeDtypeStruct((512, LANES),...  3.62 us
  transfers between devices with their start and end apart: 2, of which 2 were waited for; matrix products, arithmetic and copies ran while one was open for 0% of the time, Pallas kernels for 3%

profile of v8, /device:TPU:68, one launch (start us, length us, event | category | flops | bytes accessed | tf_op | source)
XLA Modules:
  0.0 112.7 jit_solution(14287352663215738117)
XLA Ops:
  0.0 0.8 reduce
  0.8 28.0 %all_to_all.15 = bf16[16,32,128]{2,1,0:T(8,128)(2,1)S(1)} all-to-all(bf16[16,32,128]{2,1,0:T(8,128)(2,1)S(1)} %broadcast_in_dim.32), channel_id=1, replica_groups=mesh['x'=4,'zh'=4,'y'=4,'zl'=4,'c'=2] {'zh','zl'}, dimensions={0} | all-to-all | bytes 262144 | tf_op jit(solution)/shard_map/all_to_all | solution.py:15
  28.8 0.1 copy.12
  28.9 0.2 broadcast_in_dim.34
  29.1 0.0 copy-start
  29.1 30.8 %all_to_all.16 = bf16[16,16,4096]{2,1,0:T(8,128)(2,1)S(1)} all-to-all(bf16[16,16,4096]{2,1,0:T(8,128)(2,1)S(1)} %broadcast_in_dim.34), channel_id=1, replica_groups=mesh['x'=4,'zh'=4,'y'=4,'zl'=4,'c'=2] {'x','y'}, dimensions={0} | all-to-all | bytes 4194304 | tf_op jit(solution)/shard_map/all_to_all | solution.py:15
  59.9 1.9 %collective-permute-start = (bf16[256,4096]{1,0:T(8,128)(2,1)S(1)}, bf16[256,4096]{1,0:T(8,128)(2,1)}, u32[]{:S(2)}, u32[]{:S(2)}) collective-permute-start(bf16[256,4096]{1,0:T(8,128)(2,1)S(1)} %bitcast.10), channel_id=1, source_target_pairs={{0,1},{1,0},{2,3},{3,2},{4,5},{5,4},{6,7},{7,6},{8,9},{9,8},{10,11... | collective-permute-start | bytes 6291464 | tf_op jit(solution)/shard_map/ppermute | solution.py:118
  61.8 0.0 copy-done
  61.9 0.1 copy.9.place_ref
  62.0 3.6 %own.1 = (f32[512,512]{1,0:T(8,128)S(1)}, bf16[464,4096]{1,0:T(8,128)(2,1)S(1)}) custom-call(s32[512,1]{1,0:T(8,128)S(1)} %copy.9.place_ref, bf16[256,4096]{1,0:T(8,128)(2,1)S(1)} %bitcast.11, bf16[464,4096]{1,0:T(8,128)(2,1)} %bitcast.12), custom_call_target="tpu_custom_call" | custom-call | flops 973078528 | bytes 6291456 | tf_op jit(solution)/shard_map/own/pallas_call | solution.py:127
  65.6 0.4 collective-permute-done.far_ref
  66.1 0.0 copy-start.1
  66.1 0.0 copy-start.2
  66.1 4.2 %other.1 = s16[16,120,128]{2,1,0:T(8,128)(2,1)} custom-call(s32[512,1]{1,0:T(8,128)S(1)} %copy.9.place_ref, bf16[256,4096]{1,0:T(8,128)(2,1)} %collective-permute-done.far_ref, bf16[464,4096]{1,0:T(8,128)(2,1)S(1)} %get-tuple-element.7.w_ref, f32[512,512]{1,0:T(8,128)S(1)} %get-tuple-element.8.own_ref), custom_call_target="tpu_custom_call" | custom-call | flops 973078528 | bytes 6291456 | tf_op jit(solution)/shard_map/other/pallas_call | solution.py:137
  70.3 8.4 %all-to-all-start.2 = ((s16[16,120,128]{2,1,0:T(8,128)(2,1)}), s16[16,120,128]{2,1,0:T(8,128)(2,1)S(1)}, u32[]{:S(2)}, u32[]{:S(2)}) async-start(s16[16,120,128]{2,1,0:T(8,128)(2,1)} %other.1), calls=%async_computation.2 | async-start | bytes 983040 | tf_op jit(solution)/shard_map/all_to_all | solution.py:147
  78.7 0.0 copy-done.1
  78.7 0.0 copy-done.2
  78.7 0.2 select_reduce_fusion.coefficient_ref
  78.9 31.7 %all-to-all-done.2.got_ref = s16[16,120,128]{2,1,0:T(8,128)(2,1)S(1)} async-done(((s16[16,120,128]{2,1,0:T(8,128)(2,1)}), s16[16,120,128]{2,1,0:T(8,128)(2,1)S(1)}, u32[]{:S(2)}, u32[]{:S(2)}) %all-to-all-start.2) | async-done | bytes 491552 | tf_op jit(solution)/shard_map/all_to_all | solution.py:147
  110.6 2.2 %decode.1 = bf16[32,4,464]{2,1,0:T(4,128)(2,1)} custom-call(f32[4,16]{1,0:T(4,128)S(1)} %select_reduce_fusion.coefficient_ref, s16[16,120,128]{2,1,0:T(8,128)(2,1)S(1)} %all-to-all-done.2.got_ref), custom_call_target="tpu_custom_call" | custom-call | tf_op jit(solution)/shard_map/decode/pallas_call | solution.py:152
  (2 shorter events, 0.0 us)
Async XLA Ops:
  29.1 32.7 %copy-start = (s32[512]{0:T(512)S(1)}, s32[512]{0:T(512)}, u32[]{:S(2)}) copy-start(s32[512]{0:T(512)} %param.9) | copy-start | bytes 6148
  59.9 6.2 %collective-permute-start = (bf16[256,4096]{1,0:T(8,128)(2,1)S(1)}, bf16[256,4096]{1,0:T(8,128)(2,1)}, u32[]{:S(2)}, u32[]{:S(2)}) collective-permute-start(bf16[256,4096]{1,0:T(8,128)(2,1)S(1)} %bitcast.10), channel_id=1, source_target_pairs={{0,1},{1,0},{2,3},{3,2},{4,5},{5,4},{6,7},{7,6},{8,9},{9,8},{10,11... | collective-permute-start | bytes 6291464 | tf_op jit(solution)/shard_map/ppermute | solution.py:118
  66.1 12.6 %copy-start.1 = (s32[4,16]{1,0:T(4,128)S(1)}, s32[4,16]{1,0:T(4,128)}, u32[]{:S(2)}) copy-start(s32[4,16]{1,0:T(4,128)} %param.7) | copy-start | bytes 772
  66.1 12.6 %copy-start.2 = (f32[16]{0:T(128)S(1)}, f32[16]{0:T(128)}, u32[]{:S(2)}) copy-start(f32[16]{0:T(128)} %param.8) | copy-start | bytes 196
  70.3 40.2 %all-to-all-start.2 = ((s16[16,120,128]{2,1,0:T(8,128)(2,1)}), s16[16,120,128]{2,1,0:T(8,128)(2,1)S(1)}, u32[]{:S(2)}, u32[]{:S(2)}) async-start(s16[16,120,128]{2,1,0:T(8,128)(2,1)} %other.1), calls=%async_computation.2 | async-start | bytes 983040 | tf_op jit(solution)/shard_map/all_to_all | solution.py:147

commit v9 on v7

--- a/solution.py
+++ b/solution.py
@@ -11,15 +11,8 @@
 AXES = ("x", "zh", "y", "zl", "c")
 
 
-def spread(block, axes, count, groups=None):
-    copies = jnp.broadcast_to(block[None], (count,) + block.shape)
-    return lax.all_to_all(copies, axes, 0, 0, axis_index_groups=groups)
-
-
-def lines(along):
-    return [[(k * 4 + i) * 2 + along for i in range(4)] for k in range(4)] + [
-        [(i * 4 + k) * 2 + 1 - along for i in range(4)] for k in range(4)
-    ]
+def spread(block, axes):
+    return lax.all_to_all(jnp.broadcast_to(block[None], (16,) + block.shape), axes, 0, 0)
 
 
 def encode(partial, out_ref):
@@ -39,25 +32,12 @@
         out_ref[rows:, columns] = (codes - high * 256.0).astype(BF16)
 
 
-def coded_kernel(rows_ref, w_ref, out_ref):
-    encode(lax.dot_general(rows_ref[...], w_ref[...], (((1,), (1,)), ((), ())), preferred_element_type=F32), out_ref)
-
-
-def streamed_kernel(rows_ref, w_ref, out_ref, w_here, arrived):
-    pieces, _, depth = w_here.shape
-    copies = [
-        pltpu.make_async_copy(w_ref.at[:, pl.ds(k * depth, depth)], w_here.at[k], arrived.at[k]) for k in range(pieces)
+def coded_kernel(rows_ref, *refs):
+    *w_refs, out_ref = refs
+    parts = [
+        lax.dot_general(rows_ref[...], w[...], (((1,), (1,)), ((), ())), preferred_element_type=F32) for w in w_refs
     ]
-    for copy in copies:
-        copy.start()
-    total = None
-    for k, copy in enumerate(copies):
-        copy.wait()
-        term = lax.dot_general(
-            rows_ref[:, k * depth : (k + 1) * depth], w_here[k], (((1,), (1,)), ((), ())), preferred_element_type=F32
-        )
-        total = term if k == 0 else total + term
-    encode(total, out_ref)
+    encode(jnp.concatenate(parts, axis=1), out_ref)
 
 
 def pick_kernel(place_ref, own_ref, other_ref, out_ref):
@@ -114,37 +94,32 @@
 
 def on_device(weights, calib_pool, cand_index, coef_table, row_ids):
     core = lax.axis_index("c")
+    w_piece = weights[0].T
     swap = [(0, 1), (1, 0)]
-    w_piece = weights[0].T
-    own = spread(calib_pool.reshape(32, 128), ("zh", "zl"), 16).reshape(16, 4096)
-    own = spread(own, ("x", "y", "c"), 4, lines(0)).reshape(64, 4096)
-    own, w_mine = lax.optimization_barrier((own, w_piece))
-    w_other = lax.ppermute(w_mine, "c", swap)
-    own = spread(own, ("x", "y", "c"), 4, lines(1)).reshape(256, 4096)
-
     width = w_piece.shape[0]
     vmem = pl.BlockSpec(memory_space=pltpu.VMEM)
-    params = pltpu.CompilerParams(vmem_limit_bytes=16 * 2**20)
+    params = pltpu.CompilerParams(vmem_limit_bytes=12 * 2**20)
+    own = spread(calib_pool.reshape(32, 128), ("zh", "zl")).reshape(16, 4096)
+    own, w_mine = lax.optimization_barrier((own, w_piece))
+    w_other = [lax.ppermute(part, "c", swap) for part in (w_mine[:128], w_mine[128:256], w_mine[256:384], w_mine[384:])]
+    own = spread(own, ("x", "y")).reshape(256, 4096)
 
-    def coded(kernel, w, w_spec, scratch):
+    def coded(*w):
         return pl.pallas_call(
-            kernel,
+            coded_kernel,
             out_shape=jax.ShapeDtypeStruct((512, LANES), BF16),
-            in_specs=[vmem, w_spec],
+            in_specs=[vmem] * (1 + len(w)),
             out_specs=vmem,
-            scratch_shapes=scratch,
             compiler_params=params,
             cost_estimate=pl.CostEstimate(flops=2 * 256 * 4096 * width, bytes_accessed=6 * 2**20, transcendentals=0),
             name="coded",
-        )(own, w)
+        )(own, *w)
 
-    from_other = lax.ppermute(coded(coded_kernel, w_other, vmem, []), "c", swap)
-    pieces = [pltpu.VMEM((4, width, 1024), BF16), pltpu.SemaphoreType.DMA((4,))]
-    here = pltpu.with_memory_space_constraint(w_piece, pltpu.HBM)
-    mine = coded(streamed_kernel, here, pl.BlockSpec(memory_space=pltpu.HBM), pieces)
+    from_other = lax.ppermute(coded(*w_other), "c", swap)
+    mine = coded(w_piece)
 
     x, zh, y, zl, c = (row_ids >> 7) & 3, (row_ids >> 5) & 3, (row_ids >> 3) & 3, (row_ids >> 1) & 3, row_ids & 1
-    place = jnp.where(c == 0, x * 4 + y, y * 4 + x) * 16 + zh * 4 + zl + jnp.where(c == core, 0, 256)
+    place = ((x * 4 + y) * 4 + zh) * 4 + zl + jnp.where(c == core, 0, 256)
     sent = pl.pallas_call(
         pick_kernel,
         out_shape=jax.ShapeDtypeStruct((16, 120, 128), I16),

time: 113 us -> 120 us (1.062)
  the two profiles are of different devices: /device:TPU:32 before, /device:TPU:68 now
where the time goes in v9:
time: 120 us
  waiting for transfers between devices  41.7 us (35%)
  blocking collectives  28 us (23%)
  starting transfers between devices  26.7 us (22%)
  local copies, waits for them, and re-layouts  13.6 us (11%)
  Pallas kernels  8.66 us (7%)
    all_to_all x1, waiting for transfers between devices, on_device(): got = lax.all_to_all(sent, ('zh', 'x'), 0, 0)  32.3 us
    all_to_all x1, blocking collectives, spread(): lax.all_to_all(jnp.broadcast_to(block[None], (16,) + block.shape), axes,...  28 us
    all_to_all x1, starting transfers between devices, on_device(): got = lax.all_to_all(sent, ('zh', 'x'), 0, 0)  8.7 us
    ppermute x4, starting transfers between devices, on_device(): lax.ppermute(part, 'c', swap)  8.65 us
    unnamed x21, local copies, waits for them, and re-layouts  8.48 us
    all_to_all x1, waiting for transfers between devices, spread(): lax.all_to_all(jnp.broadcast_to(block[None], (16,) + block.shape), axes,...  7.7 us
    all_to_all x1, starting transfers between devices, spread(): lax.all_to_all(jnp.broadcast_to(block[None], (16,) + block.shape), axes,...  7.45 us
    pallas_call x2, Pallas kernels, coded(): pl.pallas_call(coded_kernel, out_shape=jax.ShapeDtypeStruct((512, LANES),...  4.86 us
  transfers between devices with their start and end apart: 7, of which 3 were waited for; matrix products, arithmetic and copies ran while one was open for 3% of the time, Pallas kernels for 1%

profile of v9, /device:TPU:68, one launch (start us, length us, event | category | flops | bytes accessed | tf_op | source)
XLA Modules:
  0.0 119.7 jit_solution(8632044845946750848)
XLA Ops:
  0.0 0.8 reduce
  0.8 28.0 %all_to_all.15 = bf16[16,32,128]{2,1,0:T(8,128)(2,1)S(1)} all-to-all(bf16[16,32,128]{2,1,0:T(8,128)(2,1)S(1)} %broadcast_in_dim.31), channel_id=1, replica_groups=mesh['x'=4,'zh'=4,'y'=4,'zl'=4,'c'=2] {'zh','zl'}, dimensions={0} | all-to-all | bytes 262144 | tf_op jit(solution)/shard_map/all_to_all | solution.py:15
  28.8 0.1 copy.10
  28.9 1.6 %broadcast_in_dim.32 = bf16[16,16,4096]{2,1,0:T(8,128)(2,1)} broadcast(bf16[16,4096]{1,0:T(8,128)(2,1)S(1)} %bitcast.15), dimensions={1,2} | broadcast | bytes 2228224 | tf_op jit(solution)/shard_map/broadcast_in_dim | solution.py:15
  30.4 7.5 %all-to-all-start.1 = ((bf16[16,16,4096]{2,1,0:T(8,128)(2,1)}), bf16[16,16,4096]{2,1,0:T(8,128)(2,1)S(1)}, u32[]{:S(2)}, u32[]{:S(2)}) async-start(bf16[16,16,4096]{2,1,0:T(8,128)(2,1)} %broadcast_in_dim.32), calls=%async_computation.1 | async-start | bytes 4194304 | tf_op jit(solution)/shard_map/all_to_all | solution.py:15
  37.9 2.2 %fusion = (bf16[128,4096]{1,0:T(8,128)(2,1)S(1)}, bf16[128,4096]{1,0:T(8,128)(2,1)S(1)}, bf16[128,4096]{1,0:T(8,128)(2,1)S(1)}) fusion(bf16[464,4096]{1,0:T(8,128)(2,1)} %bitcast.12), kind=kLoop, calls=%fused_computation.5 | loop fusion | bytes 6291456 | tf_op jit(solution)/shard_map/slice | solution.py:104
  40.1 1.9 %collective-permute-start = (bf16[128,4096]{1,0:T(8,128)(2,1)S(1)}, bf16[128,4096]{1,0:T(8,128)(2,1)S(1)}, u32[]{:S(2)}, u32[]{:S(2)}) collective-permute-start(bf16[128,4096]{1,0:T(8,128)(2,1)S(1)} %get-tuple-element.11), channel_id=1, source_target_pairs={{0,1},{1,0},{2,3},{3,2},{4,5},{5,4},{6,7},{7,6},{8,9},{9,8},{10,11... | collective-permute-start | bytes 3145736 | tf_op jit(solution)/shard_map/ppermute | solution.py:104
  42.0 2.4 %collective-permute-start.1 = (bf16[128,4096]{1,0:T(8,128)(2,1)S(1)}, bf16[128,4096]{1,0:T(8,128)(2,1)S(1)}, u32[]{:S(2)}, u32[]{:S(2)}) collective-permute-start(bf16[128,4096]{1,0:T(8,128)(2,1)S(1)} %get-tuple-element.10), channel_id=1, source_target_pairs={{0,1},{1,0},{2,3},{3,2},{4,5},{5,4},{6,7},{7,6},{8,9},{9,8},{10,11... | collective-permute-start | bytes 3145736 | tf_op jit(solution)/shard_map/ppermute | solution.py:104
  44.5 0.0 copy-start.7
  44.5 1.9 %collective-permute-start.2 = (bf16[128,4096]{1,0:T(8,128)(2,1)S(1)}, bf16[128,4096]{1,0:T(8,128)(2,1)S(1)}, u32[]{:S(2)}, u32[]{:S(2)}) collective-permute-start(bf16[128,4096]{1,0:T(8,128)(2,1)S(1)} %get-tuple-element.9), channel_id=1, source_target_pairs={{0,1},{1,0},{2,3},{3,2},{4,5},{5,4},{6,7},{7,6},{8,9},{9,8},{10,11... | collective-permute-start | bytes 3145736 | tf_op jit(solution)/shard_map/ppermute | solution.py:104
  46.4 1.1 slice.15
  47.5 2.4 %collective-permute-start.3 = (bf16[80,4096]{1,0:T(8,128)(2,1)S(1)}, bf16[80,4096]{1,0:T(8,128)(2,1)S(1)}, u32[]{:S(2)}, u32[]{:S(2)}) collective-permute-start(bf16[80,4096]{1,0:T(8,128)(2,1)S(1)} %slice.15), channel_id=1, source_target_pairs={{0,1},{1,0},{2,3},{3,2},{4,5},{5,4},{6,7},{7,6},{8,9},{9,8},{10,11... | collective-permute-start | bytes 1966088 | tf_op jit(solution)/shard_map/ppermute | solution.py:104
  49.9 1.7 %collective-permute-done.3.refs_3_ = bf16[80,4096]{1,0:T(8,128)(2,1)S(1)} collective-permute-done((bf16[80,4096]{1,0:T(8,128)(2,1)S(1)}, bf16[80,4096]{1,0:T(8,128)(2,1)S(1)}, u32[]{:S(2)}, u32[]{:S(2)}) %collective-permute-start.3) | collective-permute-done | bytes 655392 | tf_op jit(solution)/shard_map/ppermute | solution.py:104
  51.6 0.0 copy-start.5
  51.6 0.8 copy-done.5
  52.5 0.0 collective-permute-done.refs_0_
  52.5 0.0 collective-permute-done.1.refs_1_
  52.5 0.0 copy-start.1
  52.5 1.0 copy-done.1
  53.5 0.0 collective-permute-done.2.refs_2_
  53.5 0.0 copy-start.3
  53.5 1.0 copy-done.3
  54.5 7.7 %all-to-all-done.1 = bf16[16,16,4096]{2,1,0:T(8,128)(2,1)S(1)} async-done(((bf16[16,16,4096]{2,1,0:T(8,128)(2,1)}), bf16[16,16,4096]{2,1,0:T(8,128)(2,1)S(1)}, u32[]{:S(2)}, u32[]{:S(2)}) %all-to-all-start.1) | async-done | bytes 2097184 | tf_op jit(solution)/shard_map/all_to_all | solution.py:15
  62.2 0.0 copy-start.2
  62.2 1.2 %copy-done.2 = bf16[128,4096]{1,0:T(8,128)(2,1)S(1)} copy-done((bf16[128,4096]{1,0:T(8,128)(2,1)S(1)}, bf16[128,4096]{1,0:T(8,128)(2,1)}, u32[]{:S(2)}) %copy-start.2) | copy-done | bytes 1048600
  63.4 0.0 copy-start.4
  63.4 1.2 %copy-done.4 = bf16[128,4096]{1,0:T(8,128)(2,1)S(1)} copy-done((bf16[128,4096]{1,0:T(8,128)(2,1)S(1)}, bf16[128,4096]{1,0:T(8,128)(2,1)}, u32[]{:S(2)}) %copy-start.4) | copy-done | bytes 1048600
  64.6 0.0 copy-start.6
  64.6 1.1 copy-done.6
  65.7 3.4 %coded.3 = bf16[512,512]{1,0:T(8,128)(2,1)} custom-call(bf16[256,4096]{1,0:T(8,128)(2,1)S(1)} %bitcast.10, bf16[128,4096]{1,0:T(8,128)(2,1)S(1)} %collective-permute-done.refs_0_, bf16[128,4096]{1,0:T(8,128)(2,1)S(1)} %copy-done.2, bf16[128,4096]{1,0:T(8,128)(2,1)S(1)} %copy-done.4, bf16[80,4096]{1,0:T(8,128)(2,1)S(1)} %copy-done.6), custom_call_target="tpu_custom_call" | custom-call | flops 973078528 | bytes 6291456 | tf_op jit(solution)/shard_map/coded/pallas_call | solution.py:108
  69.1 1.9 %collective-permute-start.4 = (bf16[512,512]{1,0:T(8,128)(2,1)}, bf16[512,512]{1,0:T(8,128)(2,1)S(1)}, u32[]{:S(2)}, u32[]{:S(2)}) collective-permute-start(bf16[512,512]{1,0:T(8,128)(2,1)} %coded.3), channel_id=1, source_target_pairs={{0,1},{1,0},{2,3},{3,2},{4,5},{5,4},{6,7},{7,6},{8,9},{9,8},{10,11... | collective-permute-start | bytes 1572872 | tf_op jit(solution)/shard_map/ppermute | solution.py:118
  71.0 0.0 copy-done.7
  71.0 0.1 copy.7.place_ref
  71.2 0.0 copy-start
  71.2 2.1 %copy-done = bf16[1,4096,464]{1,2,0:T(8,128)(2,1)S(1)} copy-done((bf16[1,4096,464]{1,2,0:T(8,128)(2,1)S(1)}, bf16[1,4096,464]{1,2,0:T(8,128)(2,1)}, u32[]{:S(2)}) %copy-start) | copy-done | bytes 3801112
  73.2 0.0 copy-start.8
  73.2 0.0 copy-start.9
  73.2 1.5 %coded.2.own_ref = bf16[512,512]{1,0:T(8,128)(2,1)S(1)} custom-call(bf16[256,4096]{1,0:T(8,128)(2,1)S(1)} %bitcast.11, bf16[464,4096]{1,0:T(8,128)(2,1)S(1)} %bitcast.14), custom_call_target="tpu_custom_call" | custom-call | flops 973078528 | bytes 6291456 | tf_op jit(solution)/shard_map/coded/pallas_call | solution.py:108
  74.8 0.0 collective-permute-done.4.other_ref
  74.8 1.6 %pick.1 = s16[16,120,128]{2,1,0:T(8,128)(2,1)} custom-call(s32[512,1]{1,0:T(8,128)S(1)} %copy.7.place_ref, bf16[512,512]{1,0:T(8,128)(2,1)S(1)} %coded.2.own_ref, bf16[512,512]{1,0:T(8,128)(2,1)S(1)} %collective-permute-done.4.other_ref), custom_call_target="tpu_custom_call" | custom-call | flops 536870912 | bytes 2097152 | tf_op jit(solution)/shard_map/pick/pallas_call | solution.py:123
  76.4 8.7 %all-to-all-start.2 = ((s16[16,120,128]{2,1,0:T(8,128)(2,1)}), s16[16,120,128]{2,1,0:T(8,128)(2,1)S(1)}, u32[]{:S(2)}, u32[]{:S(2)}) async-start(s16[16,120,128]{2,1,0:T(8,128)(2,1)} %pick.1), calls=%async_computation.2 | async-start | bytes 983040 | tf_op jit(solution)/shard_map/all_to_all | solution.py:132
  85.1 0.0 copy-done.8
  85.1 0.0 copy-done.9
  85.1 0.2 select_reduce_fusion.coefficient_ref
  85.3 32.3 %all-to-all-done.2.got_ref = s16[16,120,128]{2,1,0:T(8,128)(2,1)S(1)} async-done(((s16[16,120,128]{2,1,0:T(8,128)(2,1)}), s16[16,120,128]{2,1,0:T(8,128)(2,1)S(1)}, u32[]{:S(2)}, u32[]{:S(2)}) %all-to-all-start.2) | async-done | bytes 491552 | tf_op jit(solution)/shard_map/all_to_all | solution.py:132
  117.5 2.2 %decode.1 = bf16[32,4,464]{2,1,0:T(4,128)(2,1)} custom-call(f32[4,16]{1,0:T(4,128)S(1)} %select_reduce_fusion.coefficient_ref, s16[16,120,128]{2,1,0:T(8,128)(2,1)S(1)} %all-to-all-done.2.got_ref), custom_call_target="tpu_custom_call" | custom-call | tf_op jit(solution)/shard_map/decode/pallas_call | solution.py:137
  (2 shorter events, 0.0 us)
Async XLA Ops:
  30.4 31.7 %all-to-all-start.1 = ((bf16[16,16,4096]{2,1,0:T(8,128)(2,1)}), bf16[16,16,4096]{2,1,0:T(8,128)(2,1)S(1)}, u32[]{:S(2)}, u32[]{:S(2)}) async-start(bf16[16,16,4096]{2,1,0:T(8,128)(2,1)} %broadcast_in_dim.32), calls=%async_computation.1 | async-start | bytes 4194304 | tf_op jit(solution)/shard_map/all_to_all | solution.py:15
  40.1 12.4 %collective-permute-start = (bf16[128,4096]{1,0:T(8,128)(2,1)S(1)}, bf16[128,4096]{1,0:T(8,128)(2,1)S(1)}, u32[]{:S(2)}, u32[]{:S(2)}) collective-permute-start(bf16[128,4096]{1,0:T(8,128)(2,1)S(1)} %get-tuple-element.11), channel_id=1, source_target_pairs={{0,1},{1,0},{2,3},{3,2},{4,5},{5,4},{6,7},{7,6},{8,9},{9,8},{10,11... | collective-permute-start | bytes 3145736 | tf_op jit(solution)/shard_map/ppermute | solution.py:104
  42.0 10.5 %collective-permute-start.1 = (bf16[128,4096]{1,0:T(8,128)(2,1)S(1)}, bf16[128,4096]{1,0:T(8,128)(2,1)S(1)}, u32[]{:S(2)}, u32[]{:S(2)}) collective-permute-start(bf16[128,4096]{1,0:T(8,128)(2,1)S(1)} %get-tuple-element.10), channel_id=1, source_target_pairs={{0,1},{1,0},{2,3},{3,2},{4,5},{5,4},{6,7},{7,6},{8,9},{9,8},{10,11... | collective-permute-start | bytes 3145736 | tf_op jit(solution)/shard_map/ppermute | solution.py:104
  44.5 26.5 %copy-start.7 = (s32[512]{0:T(512)S(1)}, s32[512]{0:T(512)}, u32[]{:S(2)}) copy-start(s32[512]{0:T(512)} %param.9) | copy-start | bytes 6148
  44.5 9.0 %collective-permute-start.2 = (bf16[128,4096]{1,0:T(8,128)(2,1)S(1)}, bf16[128,4096]{1,0:T(8,128)(2,1)S(1)}, u32[]{:S(2)}, u32[]{:S(2)}) collective-permute-start(bf16[128,4096]{1,0:T(8,128)(2,1)S(1)} %get-tuple-element.9), channel_id=1, source_target_pairs={{0,1},{1,0},{2,3},{3,2},{4,5},{5,4},{6,7},{7,6},{8,9},{9,8},{10,11... | collective-permute-start | bytes 3145736 | tf_op jit(solution)/shard_map/ppermute | solution.py:104
  47.5 4.1 %collective-permute-start.3 = (bf16[80,4096]{1,0:T(8,128)(2,1)S(1)}, bf16[80,4096]{1,0:T(8,128)(2,1)S(1)}, u32[]{:S(2)}, u32[]{:S(2)}) collective-permute-start(bf16[80,4096]{1,0:T(8,128)(2,1)S(1)} %slice.15), channel_id=1, source_target_pairs={{0,1},{1,0},{2,3},{3,2},{4,5},{5,4},{6,7},{7,6},{8,9},{9,8},{10,11... | collective-permute-start | bytes 1966088 | tf_op jit(solution)/shard_map/ppermute | solution.py:104
  51.6 0.8 copy-start.5
  52.5 1.0 copy-start.1
  53.5 1.0 copy-start.3
  62.2 1.2 %copy-start.2 = (bf16[128,4096]{1,0:T(8,128)(2,1)S(1)}, bf16[128,4096]{1,0:T(8,128)(2,1)}, u32[]{:S(2)}) copy-start(bf16[128,4096]{1,0:T(8,128)(2,1)} %copy-done.1) | copy-start | bytes 3145732
  63.4 1.2 %copy-start.4 = (bf16[128,4096]{1,0:T(8,128)(2,1)S(1)}, bf16[128,4096]{1,0:T(8,128)(2,1)}, u32[]{:S(2)}) copy-start(bf16[128,4096]{1,0:T(8,128)(2,1)} %copy-done.3) | copy-start | bytes 3145732
  64.6 1.1 copy-start.6
  69.1 5.7 %collective-permute-start.4 = (bf16[512,512]{1,0:T(8,128)(2,1)}, bf16[512,512]{1,0:T(8,128)(2,1)S(1)}, u32[]{:S(2)}, u32[]{:S(2)}) collective-permute-start(bf16[512,512]{1,0:T(8,128)(2,1)} %coded.3), channel_id=1, source_target_pairs={{0,1},{1,0},{2,3},{3,2},{4,5},{5,4},{6,7},{7,6},{8,9},{9,8},{10,11... | collective-permute-start | bytes 1572872 | tf_op jit(solution)/shard_map/ppermute | solution.py:118
  71.2 2.1 %copy-start = (bf16[1,4096,464]{1,2,0:T(8,128)(2,1)S(1)}, bf16[1,4096,464]{1,2,0:T(8,128)(2,1)}, u32[]{:S(2)}) copy-start(bf16[1,4096,464]{1,2,0:T(8,128)(2,1)} %param.5) | copy-start | bytes 11403268
  73.2 11.9 %copy-start.8 = (s32[4,16]{1,0:T(4,128)S(1)}, s32[4,16]{1,0:T(4,128)}, u32[]{:S(2)}) copy-start(s32[4,16]{1,0:T(4,128)} %param.7) | copy-start | bytes 772
  73.2 11.9 %copy-start.9 = (f32[16]{0:T(128)S(1)}, f32[16]{0:T(128)}, u32[]{:S(2)}) copy-start(f32[16]{0:T(128)} %param.8) | copy-start | bytes 196
  76.4 41.1 %all-to-all-start.2 = ((s16[16,120,128]{2,1,0:T(8,128)(2,1)}), s16[16,120,128]{2,1,0:T(8,128)(2,1)S(1)}, u32[]{:S(2)}, u32[]{:S(2)}) async-start(s16[16,120,128]{2,1,0:T(8,128)(2,1)} %pick.1), calls=%async_computation.2 | async-start | bytes 983040 | tf_op jit(solution)/shard_map/all_to_all | solution.py:132

commit v10 on v8

--- a/solution.py
+++ b/solution.py
@@ -13,6 +13,12 @@
 
 def spread(block, axes):
     return lax.all_to_all(jnp.broadcast_to(block[None], (16,) + block.shape), axes, 0, 0)
+
+
+def lines(first):
+    return [[(i * 4 + k) * 2 + first for i in range(4)] for k in range(4)] + [
+        [(k * 4 + i) * 2 + 1 - first for i in range(4)] for k in range(4)
+    ]
 
 
 def encode(partial, out_ref):
@@ -64,20 +70,20 @@
     out_ref[...] = picked(place_ref[...], 0, bytes_ref)
 
 
-def other_kernel(place_ref, far_ref, w_ref, own_ref, out_ref, rows_ref, bytes_ref, arrived):
-    encode(product(rows_ref, w_ref, far_ref, rows_ref, arrived), bytes_ref)
+def other_kernel(core_ref, place_ref, rows_ref, w_ref, own_ref, out_ref, bytes_ref):
+    encode(times(rows_ref[...], w_ref[...]), bytes_ref)
     lane16, lane8 = lax.broadcasted_iota(I32, (16, 128), 1), lax.broadcasted_iota(I32, (8, 128), 1)
     for at in range(0, 512, 256):
         codes = own_ref[at : at + 256] + picked(place_ref[at : at + 256], 256, bytes_ref)
         for block in range(8):
-            owner = at // 32 + block
-            to = owner % 4 * 4 + owner // 4
             rows = codes[block * 32 : block * 32 + 32]
             tail = rows[:, 384:]
             fold = jnp.where(lane16 < 64, tail[:16], pltpu.roll(tail[16:], 64, 1))
             a, b, c, d = (pltpu.roll(tail[8 * i : 8 * i + 8], (64 + 32 * i) % 128, 1) for i in range(4))
             last = jnp.where(lane8 < 64, jnp.where(lane8 < 32, a, b), jnp.where(lane8 < 96, c, d))
             packed = jnp.concatenate([rows[:, :128], rows[:, 128:256], rows[:, 256:384], fold, last], axis=0)
+            owner = at // 32 + block
+            to = jnp.where(core_ref[0] == 0, owner, owner % 4 * 4 + owner // 4)
             out_ref[to] = packed.astype(I32).astype(I16)
 
 
@@ -103,7 +109,7 @@
             else:
                 values = tail_ref[source]
             for c in range(cands):
-                term = coefficient_ref[c, source % 4 * 4 + source // 4] * values
+                term = coefficient_ref[c, source] * values
                 totals[c] = term if source == 0 else totals[c] + term
         columns = slice(128 * block, min(128 * block + 128, width))
         stacked = jnp.stack([t[:, : columns.stop - columns.start] for t in totals], axis=1)
@@ -137,18 +143,22 @@
     sent = pl.pallas_call(
         other_kernel,
         out_shape=jax.ShapeDtypeStruct((16, 120, 128), I16),
-        in_specs=[vmem, far, vmem, vmem],
+        in_specs=[pl.BlockSpec(memory_space=pltpu.SMEM)] + [vmem] * 4,
         out_specs=vmem,
-        scratch_shapes=[pltpu.VMEM((256, 4096), BF16), pltpu.VMEM((512, LANES), BF16), pltpu.SemaphoreType.DMA((4,))],
+        scratch_shapes=[pltpu.VMEM((512, LANES), BF16)],
         compiler_params=params,
         cost_estimate=cost,
         name="other",
-    )(place, pltpu.with_memory_space_constraint(other, pltpu.HBM), w_here, codes)
-    got = lax.all_to_all(sent, ("zh", "x"), 0, 0)
+    )(core.astype(I32)[None], place, other, w_here, codes)
+    got = lax.all_to_all(sent.reshape(4, 4, 120, 128), ("x", "zh", "c"), 0, 0, axis_index_groups=lines(0))
+    got = jnp.transpose(got, (1, 0, 2, 3))
+    got = lax.all_to_all(got, ("x", "zh", "c"), 0, 0, axis_index_groups=lines(1)).reshape(16, 120, 128)
 
     entries = jnp.arange(coef_table.shape[0], dtype=I32)
     onehot = (cand_index[:, :, None] == entries[None, None, :]).astype(F32)
     coefficient = jnp.sum(onehot * coef_table[None, None, :], axis=2)
+    turned = jnp.transpose(coefficient.reshape(4, 4, 4), (0, 2, 1)).reshape(4, 16)
+    coefficient = jnp.where(core == 0, turned, coefficient)
     return pl.pallas_call(
         decode_kernel,
         out_shape=jax.ShapeDtypeStruct((32, 4, width), BF16),

time: 113 us -> 113 us (level)
  the two profiles are of different devices: /device:TPU:68 before, /device:TPU:32 now
where the time goes in v10:
time: 113 us; the launch traced here: 111 us
  blocking collectives  71.9 us (64%)
  waiting for transfers between devices  19.3 us (17%)
  Pallas kernels  9.39 us (8%)
  starting transfers between devices  7.62 us (7%)
  local copies, waits for them, and re-layouts  1.57 us (1%)
    all_to_all x2, blocking collectives, spread(): lax.all_to_all(jnp.broadcast_to(block[None], (16,) + block.shape), axes,...  61.3 us
    all_to_all x1, waiting for transfers between devices, on_device(): lax.all_to_all(got, ('x', 'zh', 'c'), 0, 0, axis_index_groups=lines(1))  18.8 us
    all_to_all x1, blocking collectives, on_device(): lax.all_to_all(sent.reshape(4, 4, 120, 128), ('x', 'zh', 'c'), 0, 0, axis...  10.6 us
    all_to_all x1, starting transfers between devices, on_device(): lax.all_to_all(got, ('x', 'zh', 'c'), 0, 0, axis_index_groups=lines(1))  5.71 us
    pallas_call x1, Pallas kernels, on_device(): pl.pallas_call(own_kernel, out_shape=(jax.ShapeDtypeStruct((512, LANES),...  3.62 us
    pallas_call x1, Pallas kernels, on_device(): pl.pallas_call(other_kernel, out_shape=jax.ShapeDtypeStruct((16, 120, 128...  3.59 us
  transfers between devices with their start and end apart: 2, of which 2 were waited for; matrix products, arithmetic and copies ran while one was open for 1% of the time, Pallas kernels for 3%

profile of v10, /device:TPU:32, one launch (start us, length us, event | category | flops | bytes accessed | tf_op | source)
XLA Modules:
  0.0 110.8 jit_solution(3330878514182954261)
XLA Ops:
  0.0 0.8 reduce
  0.8 29.2 %all_to_all.20 = bf16[16,32,128]{2,1,0:T(8,128)(2,1)S(1)} all-to-all(bf16[16,32,128]{2,1,0:T(8,128)(2,1)S(1)} %broadcast_in_dim.36), channel_id=1, replica_groups=mesh['x'=4,'zh'=4,'y'=4,'zl'=4,'c'=2] {'zh','zl'}, dimensions={0} | all-to-all | bytes 262144 | tf_op jit(solution)/shard_map/all_to_all | solution.py:15
  30.0 0.1 copy.26
  30.1 0.2 broadcast_in_dim.38
  30.3 0.0 copy-start
  30.3 32.1 %all_to_all.21 = bf16[16,16,4096]{2,1,0:T(8,128)(2,1)S(1)} all-to-all(bf16[16,16,4096]{2,1,0:T(8,128)(2,1)S(1)} %broadcast_in_dim.38), channel_id=1, replica_groups=mesh['x'=4,'zh'=4,'y'=4,'zl'=4,'c'=2] {'x','y'}, dimensions={0} | all-to-all | bytes 4194304 | tf_op jit(solution)/shard_map/all_to_all | solution.py:15
  62.4 1.9 %collective-permute-start = (bf16[256,4096]{1,0:T(8,128)(2,1)S(1)}, bf16[256,4096]{1,0:T(8,128)(2,1)}, u32[]{:S(2)}, u32[]{:S(2)}) collective-permute-start(bf16[256,4096]{1,0:T(8,128)(2,1)S(1)} %bitcast.15), channel_id=1, source_target_pairs={{0,1},{1,0},{2,3},{3,2},{4,5},{5,4},{6,7},{7,6},{8,9},{9,8},{10,11... | collective-permute-start | bytes 6291464 | tf_op jit(solution)/shard_map/ppermute | solution.py:124
  64.4 0.0 copy-done
  64.4 0.1 copy.22.place_ref
  64.5 3.6 %own.1 = (f32[512,512]{1,0:T(8,128)S(1)}, bf16[464,4096]{1,0:T(8,128)(2,1)S(1)}) custom-call(s32[512,1]{1,0:T(8,128)S(1)} %copy.22.place_ref, bf16[256,4096]{1,0:T(8,128)(2,1)S(1)} %bitcast.16, bf16[464,4096]{1,0:T(8,128)(2,1)} %bitcast.19), custom_call_target="tpu_custom_call" | custom-call | flops 973078528 | bytes 6291456 | tf_op jit(solution)/shard_map/own/pallas_call | solution.py:133
  68.2 0.4 collective-permute-done.rows_ref
  68.6 3.6 %other.1 = s16[16,120,128]{2,1,0:T(8,128)(2,1)S(1)} custom-call(s32[1]{0:T(128)} %bitcast.1.core_ref, s32[512,1]{1,0:T(8,128)S(1)} %copy.22.place_ref, bf16[256,4096]{1,0:T(8,128)(2,1)} %collective-permute-done.rows_ref, bf16[464,4096]{1,0:T(8,128)(2,1)S(1)} %get-tuple-element.7.w_ref, f32[512,512]{1,0:T(8,128)S(1)} %get-tuple-element.8.own_ref), custom_call_target="tpu_custom_call" | custom-call | flops 973078528 | bytes 6291456 | tf_op jit(solution)/shard_map/other/pallas_call | solution.py:143
  72.2 0.0 copy-start.1
  72.2 0.0 copy-start.2
  72.2 10.6 %all_to_all.22 = s16[4,4,120,128]{3,2,1,0:T(8,128)(2,1)S(1)} all-to-all(s16[4,4,120,128]{3,2,1,0:T(8,128)(2,1)S(1)} %bitcast.18), channel_id=1, replica_groups={{0,128,256,384},{32,160,288,416},{64,192,320,448},{96,224,352,480},{1,3..., dimensions={0} | all-to-all | bytes 983040 | tf_op jit(solution)/shard_map/all_to_all | solution.py:153
  82.8 0.8 copy.23
  83.6 5.7 %all-to-all-start.3 = ((s16[4,4,120,128]{3,2,1,0:T(8,128)(2,1)}), s16[4,4,120,128]{3,2,1,0:T(8,128)(2,1)S(1)}, u32[]{:S(2)}, u32[]{:S(2)}) async-start(s16[4,4,120,128]{3,2,1,0:T(8,128)(2,1)} %copy.23), calls=%async_computation.3 | async-start | bytes 983040 | tf_op jit(solution)/shard_map/all_to_all | solution.py:155
  89.3 0.0 copy-done.1
  89.3 0.0 copy-done.2
  89.3 0.2 select_reduce_fusion
  89.5 0.1 reshape.19
  89.6 0.1 copy.20
  89.7 0.1 reshape.20
  89.8 18.8 %all-to-all-done.3 = s16[4,4,120,128]{3,2,1,0:T(8,128)(2,1)S(1)} async-done(((s16[4,4,120,128]{3,2,1,0:T(8,128)(2,1)}), s16[4,4,120,128]{3,2,1,0:T(8,128)(2,1)S(1)}, u32[]{:S(2)}, u32[]{:S(2)}) %all-to-all-start.3) | async-done | bytes 491552 | tf_op jit(solution)/shard_map/all_to_all | solution.py:155
  108.6 2.2 %decode.1 = bf16[32,4,464]{2,1,0:T(4,128)(2,1)} custom-call(f32[4,16]{1,0:T(4,128)S(1)} %broadcast_select_fusion.coefficient_ref, s16[16,120,128]{2,1,0:T(8,128)(2,1)S(1)} %bitcast.17), custom_call_target="tpu_custom_call" | custom-call | tf_op jit(solution)/shard_map/decode/pallas_call | solution.py:162
  (3 shorter events, 0.0 us)
Async XLA Ops:
  30.3 34.1 %copy-start = (s32[512]{0:T(512)S(1)}, s32[512]{0:T(512)}, u32[]{:S(2)}) copy-start(s32[512]{0:T(512)} %param.9) | copy-start | bytes 6148
  62.4 6.2 %collective-permute-start = (bf16[256,4096]{1,0:T(8,128)(2,1)S(1)}, bf16[256,4096]{1,0:T(8,128)(2,1)}, u32[]{:S(2)}, u32[]{:S(2)}) collective-permute-start(bf16[256,4096]{1,0:T(8,128)(2,1)S(1)} %bitcast.15), channel_id=1, source_target_pairs={{0,1},{1,0},{2,3},{3,2},{4,5},{5,4},{6,7},{7,6},{8,9},{9,8},{10,11... | collective-permute-start | bytes 6291464 | tf_op jit(solution)/shard_map/ppermute | solution.py:124
  72.2 17.1 %copy-start.1 = (s32[4,16]{1,0:T(4,128)S(1)}, s32[4,16]{1,0:T(4,128)}, u32[]{:S(2)}) copy-start(s32[4,16]{1,0:T(4,128)} %param.7) | copy-start | bytes 772
  72.2 17.1 %copy-start.2 = (f32[16]{0:T(128)S(1)}, f32[16]{0:T(128)}, u32[]{:S(2)}) copy-start(f32[16]{0:T(128)} %param.8) | copy-start | bytes 196
  83.6 25.0 %all-to-all-start.3 = ((s16[4,4,120,128]{3,2,1,0:T(8,128)(2,1)}), s16[4,4,120,128]{3,2,1,0:T(8,128)(2,1)S(1)}, u32[]{:S(2)}, u32[]{:S(2)}) async-start(s16[4,4,120,128]{3,2,1,0:T(8,128)(2,1)} %copy.23), calls=%async_computation.3 | async-start | bytes 983040 | tf_op jit(solution)/shard_map/all_to_all | solution.py:155

commit v11 on v10

--- a/solution.py
+++ b/solution.py
@@ -1,3 +1,5 @@
+import functools
+
 import jax
 import jax.numpy as jnp
 from jax import lax
@@ -42,13 +44,12 @@
     return lax.dot_general(rows, weights, (((1,), (1,)), ((), ())), preferred_element_type=F32)
 
 
-def picked(place, half, bytes_ref):
+def selection(place, half):
     found = place - half == lax.broadcasted_iota(I32, (place.shape[0], 256), 1)
-    pick = jnp.concatenate([jnp.where(found, 256.0, 0.0), jnp.where(found, 1.0, 0.0)], axis=1).astype(BF16)
-    return jnp.dot(pick, bytes_ref[...], preferred_element_type=F32)
-
-
-def product(rows_ref, w_ref, far_ref, near_ref, arrived):
+    return jnp.concatenate([jnp.where(found, 256.0, 0.0), jnp.where(found, 1.0, 0.0)], axis=1).astype(BF16)
+
+
+def product(rows_ref, w_ref, far_ref, near_ref, arrived, meanwhile=lambda: None):
     pieces = arrived.shape[0]
     depth = far_ref.shape[1] // pieces
     copies = []
@@ -56,6 +57,7 @@
         part = pl.ds(k * depth, depth)
         copies.append(pltpu.make_async_copy(far_ref.at[:, part], near_ref.at[:, part], arrived.at[k]))
         copies[k].start()
+    meanwhile()
     total = None
     for k, copy in enumerate(copies):
         copy.wait()
@@ -67,14 +69,21 @@
 
 def own_kernel(place_ref, rows_ref, far_ref, out_ref, w_ref, bytes_ref, arrived):
     encode(product(rows_ref, w_ref, far_ref, w_ref, arrived), bytes_ref)
-    out_ref[...] = picked(place_ref[...], 0, bytes_ref)
-
-
-def other_kernel(core_ref, place_ref, rows_ref, w_ref, own_ref, out_ref, bytes_ref):
-    encode(times(rows_ref[...], w_ref[...]), bytes_ref)
+    out_ref[...] = jnp.dot(selection(place_ref[...], 0), bytes_ref[...], preferred_element_type=F32)
+
+
+def store_selection(place_ref, pick_ref):
+    pick_ref[...] = selection(place_ref[...], 256)
+
+
+def other_kernel(core_ref, place_ref, far_ref, w_ref, own_ref, out_ref, rows_ref, bytes_ref, pick_ref, arrived):
+    meanwhile = functools.partial(store_selection, place_ref, pick_ref)
+    encode(product(rows_ref, w_ref, far_ref, rows_ref, arrived, meanwhile), bytes_ref)
     lane16, lane8 = lax.broadcasted_iota(I32, (16, 128), 1), lax.broadcasted_iota(I32, (8, 128), 1)
     for at in range(0, 512, 256):
-        codes = own_ref[at : at + 256] + picked(place_ref[at : at + 256], 256, bytes_ref)
+        codes = own_ref[at : at + 256] + jnp.dot(
+            pick_ref[at : at + 256], bytes_ref[...], preferred_element_type=F32
+        )
         for block in range(8):
             rows = codes[block * 32 : block * 32 + 32]
             tail = rows[:, 384:]
@@ -85,6 +94,12 @@
             owner = at // 32 + block
             to = jnp.where(core_ref[0] == 0, owner, owner % 4 * 4 + owner // 4)
             out_ref[to] = packed.astype(I32).astype(I16)
+
+
+def turn_kernel(in_ref, out_ref):
+    for a in range(4):
+        for b in range(4):
+            out_ref[b, a] = in_ref[a, b]
 
 
 def decode_kernel(coefficient_ref, got_ref, out_ref, tail_ref, step_ref):
@@ -100,6 +115,7 @@
         step = tail[:, at : at + 1] * jnp.exp2(tail[:, at + 1 : at + 2]) * (1.0 / (8192.0 * TOP))
         tail_ref[source] = tail * step
         step_ref[source] = jnp.broadcast_to(step, (rows, 128))
+    sums = []
     for block in range(4):
         totals = [None] * cands
         for source in range(16):
@@ -111,9 +127,11 @@
             for c in range(cands):
                 term = coefficient_ref[c, source] * values
                 totals[c] = term if source == 0 else totals[c] + term
-        columns = slice(128 * block, min(128 * block + 128, width))
-        stacked = jnp.stack([t[:, : columns.stop - columns.start] for t in totals], axis=1)
-        out_ref[:, :, columns] = stacked.astype(BF16)
+        sums.append(jnp.concatenate([t.astype(BF16) for t in totals], axis=0))
+    to, of = (lax.broadcasted_iota(I32, (rows * cands, rows * cands), d) for d in (0, 1))
+    order = jnp.where(to % cands * rows + to // cands == of, 1.0, 0.0).astype(BF16)
+    laid = jnp.dot(order, jnp.concatenate(sums, axis=1)[:, :width], preferred_element_type=F32)
+    out_ref[...] = laid.reshape(rows, cands, width).astype(BF16)
 
 
 def on_device(weights, calib_pool, cand_index, coef_table, row_ids):
@@ -143,15 +161,24 @@
     sent = pl.pallas_call(
         other_kernel,
         out_shape=jax.ShapeDtypeStruct((16, 120, 128), I16),
-        in_specs=[pl.BlockSpec(memory_space=pltpu.SMEM)] + [vmem] * 4,
+        in_specs=[pl.BlockSpec(memory_space=pltpu.SMEM), vmem, far, vmem, vmem],
         out_specs=vmem,
-        scratch_shapes=[pltpu.VMEM((512, LANES), BF16)],
+        scratch_shapes=[pltpu.VMEM((256, 4096), BF16)]
+        + [pltpu.VMEM((512, LANES), BF16)] * 2
+        + [pltpu.SemaphoreType.DMA((4,))],
         compiler_params=params,
         cost_estimate=cost,
         name="other",
-    )(core.astype(I32)[None], place, other, w_here, codes)
+    )(core.astype(I32)[None], place, pltpu.with_memory_space_constraint(other, pltpu.HBM), w_here, codes)
     got = lax.all_to_all(sent.reshape(4, 4, 120, 128), ("x", "zh", "c"), 0, 0, axis_index_groups=lines(0))
-    got = jnp.transpose(got, (1, 0, 2, 3))
+    got = pl.pallas_call(
+        turn_kernel,
+        out_shape=jax.ShapeDtypeStruct(got.shape, I16),
+        in_specs=[vmem],
+        out_specs=vmem,
+        compiler_params=params,
+        name="turn",
+    )(got)
     got = lax.all_to_all(got, ("x", "zh", "c"), 0, 0, axis_index_groups=lines(1)).reshape(16, 120, 128)
 
     entries = jnp.arange(coef_table.shape[0], dtype=I32)

time: 113 us -> 112 us (level)
  no operation moved by 1% of the time
where the time goes in v11:
time: 112 us; the launch traced here: 110 us
  blocking collectives  71.8 us (64%)
  waiting for transfers between devices  19.3 us (17%)
  Pallas kernels  9.83 us (9%)
  starting transfers between devices  7.62 us (7%)
    all_to_all x2, blocking collectives, spread(): lax.all_to_all(jnp.broadcast_to(block[None], (16,) + block.shape), axes,...  61.3 us
    all_to_all x1, waiting for transfers between devices, on_device(): lax.all_to_all(got, ('x', 'zh', 'c'), 0, 0, axis_index_groups=lines(1))  18.8 us
    all_to_all x1, blocking collectives, on_device(): lax.all_to_all(sent.reshape(4, 4, 120, 128), ('x', 'zh', 'c'), 0, 0, axis...  10.4 us
    all_to_all x1, starting transfers between devices, on_device(): lax.all_to_all(got, ('x', 'zh', 'c'), 0, 0, axis_index_groups=lines(1))  5.71 us
    pallas_call x1, Pallas kernels, on_device(): pl.pallas_call(own_kernel, out_shape=(jax.ShapeDtypeStruct((512, LANES),...  3.62 us
    pallas_call x1, Pallas kernels, on_device(): pl.pallas_call(other_kernel, out_shape=jax.ShapeDtypeStruct((16, 120, 128...  3.41 us
  transfers between devices with their start and end apart: 2, of which 2 were waited for; matrix products, arithmetic and copies ran while one was open for 1% of the time, Pallas kernels for 3%

profile of v11, /device:TPU:32, one launch (start us, length us, event | category | flops | bytes accessed | tf_op | source)
XLA Modules:
  0.0 110.3 jit_solution(521746677765624919)
XLA Ops:
  0.0 0.8 reduce
  0.8 29.2 %all_to_all.20 = bf16[16,32,128]{2,1,0:T(8,128)(2,1)S(1)} all-to-all(bf16[16,32,128]{2,1,0:T(8,128)(2,1)S(1)} %broadcast_in_dim.36), channel_id=1, replica_groups=mesh['x'=4,'zh'=4,'y'=4,'zl'=4,'c'=2] {'zh','zl'}, dimensions={0} | all-to-all | bytes 262144 | tf_op jit(solution)/shard_map/all_to_all | solution.py:17
  30.0 0.1 copy.15
  30.1 0.2 broadcast_in_dim.38
  30.3 0.0 copy-start
  30.3 32.1 %all_to_all.21 = bf16[16,16,4096]{2,1,0:T(8,128)(2,1)S(1)} all-to-all(bf16[16,16,4096]{2,1,0:T(8,128)(2,1)S(1)} %broadcast_in_dim.38), channel_id=1, replica_groups=mesh['x'=4,'zh'=4,'y'=4,'zl'=4,'c'=2] {'x','y'}, dimensions={0} | all-to-all | bytes 4194304 | tf_op jit(solution)/shard_map/all_to_all | solution.py:17
  62.4 1.9 %collective-permute-start = (bf16[256,4096]{1,0:T(8,128)(2,1)S(1)}, bf16[256,4096]{1,0:T(8,128)(2,1)}, u32[]{:S(2)}, u32[]{:S(2)}) collective-permute-start(bf16[256,4096]{1,0:T(8,128)(2,1)S(1)} %bitcast.14), channel_id=1, source_target_pairs={{0,1},{1,0},{2,3},{3,2},{4,5},{5,4},{6,7},{7,6},{8,9},{9,8},{10,11... | collective-permute-start | bytes 6291464 | tf_op jit(solution)/shard_map/ppermute | solution.py:142
  64.4 0.0 copy-done
  64.4 0.1 copy.12.place_ref
  64.5 3.6 %own.1 = (f32[512,512]{1,0:T(8,128)S(1)}, bf16[464,4096]{1,0:T(8,128)(2,1)S(1)}) custom-call(s32[512,1]{1,0:T(8,128)S(1)} %copy.12.place_ref, bf16[256,4096]{1,0:T(8,128)(2,1)S(1)} %bitcast.15, bf16[464,4096]{1,0:T(8,128)(2,1)} %bitcast.18), custom_call_target="tpu_custom_call" | custom-call | flops 973078528 | bytes 6291456 | tf_op jit(solution)/shard_map/own/pallas_call | solution.py:151
  68.2 0.4 collective-permute-done.far_ref
  68.6 3.4 %other.1 = s16[16,120,128]{2,1,0:T(8,128)(2,1)S(1)} custom-call(s32[1]{0:T(128)} %bitcast.1.core_ref, s32[512,1]{1,0:T(8,128)S(1)} %copy.12.place_ref, bf16[256,4096]{1,0:T(8,128)(2,1)} %collective-permute-done.far_ref, bf16[464,4096]{1,0:T(8,128)(2,1)S(1)} %get-tuple-element.7.w_ref, f32[512,512]{1,0:T(8,128)S(1)} %get-tuple-element.8.own_ref), custom_call_target="tpu_custom_call" | custom-call | flops 973078528 | bytes 6291456 | tf_op jit(solution)/shard_map/other/pallas_call | solution.py:161
  72.0 0.0 copy-start.1
  72.0 0.0 copy-start.2
  72.1 10.4 %all_to_all.22.in_ref = s16[4,4,120,128]{3,2,1,0:T(8,128)(2,1)S(1)} all-to-all(s16[4,4,120,128]{3,2,1,0:T(8,128)(2,1)S(1)} %bitcast.17), channel_id=1, replica_groups={{0,128,256,384},{32,160,288,416},{64,192,320,448},{96,224,352,480},{1,3..., dimensions={0} | all-to-all | bytes 983040 | tf_op jit(solution)/shard_map/all_to_all | solution.py:173
  82.5 0.8 turn.1
  83.3 5.7 %all-to-all-start.3 = ((s16[4,4,120,128]{3,2,1,0:T(8,128)(2,1)}), s16[4,4,120,128]{3,2,1,0:T(8,128)(2,1)S(1)}, u32[]{:S(2)}, u32[]{:S(2)}) async-start(s16[4,4,120,128]{3,2,1,0:T(8,128)(2,1)} %turn.1), calls=%async_computation.3 | async-start | bytes 983040 | tf_op jit(solution)/shard_map/all_to_all | solution.py:182
  89.0 0.0 copy-done.1
  89.0 0.0 copy-done.2
  89.0 0.2 select_reduce_fusion
  89.2 0.1 reshape.19
  89.3 0.1 copy.10
  89.4 0.1 reshape.20
  89.5 18.8 %all-to-all-done.3 = s16[4,4,120,128]{3,2,1,0:T(8,128)(2,1)S(1)} async-done(((s16[4,4,120,128]{3,2,1,0:T(8,128)(2,1)}), s16[4,4,120,128]{3,2,1,0:T(8,128)(2,1)S(1)}, u32[]{:S(2)}, u32[]{:S(2)}) %all-to-all-start.3) | async-done | bytes 491552 | tf_op jit(solution)/shard_map/all_to_all | solution.py:182
  108.3 2.0 %decode.1 = bf16[32,4,464]{2,1,0:T(4,128)(2,1)} custom-call(f32[4,16]{1,0:T(4,128)S(1)} %broadcast_select_fusion.coefficient_ref, s16[16,120,128]{2,1,0:T(8,128)(2,1)S(1)} %bitcast.16), custom_call_target="tpu_custom_call" | custom-call | tf_op jit(solution)/shard_map/decode/pallas_call | solution.py:189
  (3 shorter events, 0.0 us)
Async XLA Ops:
  30.3 34.1 %copy-start = (s32[512]{0:T(512)S(1)}, s32[512]{0:T(512)}, u32[]{:S(2)}) copy-start(s32[512]{0:T(512)} %param.9) | copy-start | bytes 6148
  62.4 6.2 %collective-permute-start = (bf16[256,4096]{1,0:T(8,128)(2,1)S(1)}, bf16[256,4096]{1,0:T(8,128)(2,1)}, u32[]{:S(2)}, u32[]{:S(2)}) collective-permute-start(bf16[256,4096]{1,0:T(8,128)(2,1)S(1)} %bitcast.14), channel_id=1, source_target_pairs={{0,1},{1,0},{2,3},{3,2},{4,5},{5,4},{6,7},{7,6},{8,9},{9,8},{10,11... | collective-permute-start | bytes 6291464 | tf_op jit(solution)/shard_map/ppermute | solution.py:142
  72.0 17.0 %copy-start.1 = (s32[4,16]{1,0:T(4,128)S(1)}, s32[4,16]{1,0:T(4,128)}, u32[]{:S(2)}) copy-start(s32[4,16]{1,0:T(4,128)} %param.7) | copy-start | bytes 772
  72.0 17.0 %copy-start.2 = (f32[16]{0:T(128)S(1)}, f32[16]{0:T(128)}, u32[]{:S(2)}) copy-start(f32[16]{0:T(128)} %param.8) | copy-start | bytes 196
  83.3 25.0 %all-to-all-start.3 = ((s16[4,4,120,128]{3,2,1,0:T(8,128)(2,1)}), s16[4,4,120,128]{3,2,1,0:T(8,128)(2,1)S(1)}, u32[]{:S(2)}, u32[]{:S(2)}) async-start(s16[4,4,120,128]{3,2,1,0:T(8,128)(2,1)} %turn.1), calls=%async_computation.3 | async-start | bytes 983040 | tf_op jit(solution)/shard_map/all_to_all | solution.py:182

commit v12 on v11

--- a/solution.py
+++ b/solution.py
@@ -13,8 +13,9 @@
 AXES = ("x", "zh", "y", "zl", "c")
 
 
-def spread(block, axes):
-    return lax.all_to_all(jnp.broadcast_to(block[None], (16,) + block.shape), axes, 0, 0)
+def spread(block, axes, count, groups=None):
+    copies = jnp.broadcast_to(block[None], (count,) + block.shape)
+    return lax.all_to_all(copies, axes, 0, 0, axis_index_groups=groups)
 
 
 def lines(first):
@@ -137,12 +138,14 @@
 def on_device(weights, calib_pool, cand_index, coef_table, row_ids):
     core = lax.axis_index("c")
     w_piece = weights[0].T
-    own = spread(calib_pool.reshape(32, 128), ("zh", "zl")).reshape(16, 4096)
-    own = spread(own, ("x", "y")).reshape(256, 4096)
+    own = spread(calib_pool.reshape(32, 128), ("zh", "zl"), 16).reshape(16, 4096)
+    own = spread(own, ("x", "y", "c"), 4, lines(1)).reshape(64, 4096)
+    own = spread(own, ("x", "y", "c"), 4, lines(0)).reshape(256, 4096)
     other = lax.ppermute(own, "c", [(0, 1), (1, 0)])
 
     x, zh, y, zl, c = (row_ids >> 7) & 3, (row_ids >> 5) & 3, (row_ids >> 3) & 3, (row_ids >> 1) & 3, row_ids & 1
-    place = (((x * 4 + y) * 4 + zh) * 4 + zl + jnp.where(c == core, 0, 256))[:, None]
+    line = jnp.where(c == 0, x * 4 + y, y * 4 + x)
+    place = ((line * 4 + zh) * 4 + zl + jnp.where(c == core, 0, 256))[:, None]
 
     width = w_piece.shape[0]
     vmem, far = pl.BlockSpec(memory_space=pltpu.VMEM), pl.BlockSpec(memory_space=pltpu.HBM)

time: 112 us -> 113 us (level)
  the two profiles are of different devices: /device:TPU:32 before, /device:TPU:2 now
where the time goes in v12:
time: 113 us; the launch traced here: 112 us
  blocking collectives  72 us (64%)
  waiting for transfers between devices  22.9 us (20%)
  Pallas kernels  9.83 us (9%)
  starting transfers between devices  5.63 us (5%)
    all_to_all x3, blocking collectives, spread(): return lax.all_to_all(copies, axes, 0, 0, axis_index_groups=groups)  61.7 us
    all_to_all x1, waiting for transfers between devices, on_device(): lax.all_to_all(got, ('x', 'zh', 'c'), 0, 0, axis_index_groups=lines(1))  22.4 us
    all_to_all x1, blocking collectives, on_device(): lax.all_to_all(sent.reshape(4, 4, 120, 128), ('x', 'zh', 'c'), 0, 0, axis...  10.3 us
    all_to_all x1, starting transfers between devices, on_device(): lax.all_to_all(got, ('x', 'zh', 'c'), 0, 0, axis_index_groups=lines(1))  3.72 us
    pallas_call x1, Pallas kernels, on_device(): pl.pallas_call(own_kernel, out_shape=(jax.ShapeDtypeStruct((512, LANES),...  3.62 us
    pallas_call x1, Pallas kernels, on_device(): pl.pallas_call(other_kernel, out_shape=jax.ShapeDtypeStruct((16, 120, 128...  3.42 us
  transfers between devices with their start and end apart: 2, of which 2 were waited for; matrix products, arithmetic and copies ran while one was open for 1% of the time, Pallas kernels for 3%

profile of v12, /device:TPU:2, one launch (start us, length us, event | category | flops | bytes accessed | tf_op | source)
XLA Modules:
  0.0 112.2 jit_solution(14542772027502163653)
XLA Ops:
  0.0 0.8 reduce
  0.8 29.7 %all_to_all.25 = bf16[16,32,128]{2,1,0:T(8,128)(2,1)S(1)} all-to-all(bf16[16,32,128]{2,1,0:T(8,128)(2,1)S(1)} %broadcast_in_dim.40), channel_id=1, replica_groups=mesh['x'=4,'zh'=4,'y'=4,'zl'=4,'c'=2] {'zh','zl'}, dimensions={0} | all-to-all | bytes 262144 | tf_op jit(solution)/shard_map/all_to_all | solution.py:18
  30.5 0.1 copy.15
  30.6 12.3 %all_to_all.26 = bf16[4,16,4096]{2,1,0:T(8,128)(2,1)S(1)} all-to-all(bf16[4,16,4096]{2,1,0:T(8,128)(2,1)S(1)} %broadcast_in_dim.42), channel_id=1, replica_groups={{1,129,257,385},{9,137,265,393},{17,145,273,401},{25,153,281,409},{0,8,..., dimensions={0} | all-to-all | bytes 1048576 | tf_op jit(solution)/shard_map/all_to_all | solution.py:18
  42.9 0.2 broadcast_in_dim.44
  43.2 0.0 copy-start
  43.2 19.7 %all_to_all.27 = bf16[4,64,4096]{2,1,0:T(8,128)(2,1)S(1)} all-to-all(bf16[4,64,4096]{2,1,0:T(8,128)(2,1)S(1)} %broadcast_in_dim.44), channel_id=1, replica_groups={{0,128,256,384},{8,136,264,392},{16,144,272,400},{24,152,280,408},{1,9,..., dimensions={0} | all-to-all | bytes 4194304 | tf_op jit(solution)/shard_map/all_to_all | solution.py:18
  62.9 1.9 %collective-permute-start = (bf16[256,4096]{1,0:T(8,128)(2,1)S(1)}, bf16[256,4096]{1,0:T(8,128)(2,1)}, u32[]{:S(2)}, u32[]{:S(2)}) collective-permute-start(bf16[256,4096]{1,0:T(8,128)(2,1)S(1)} %bitcast.15), channel_id=1, source_target_pairs={{0,1},{1,0},{2,3},{3,2},{4,5},{5,4},{6,7},{7,6},{8,9},{9,8},{10,11... | collective-permute-start | bytes 6291464 | tf_op jit(solution)/shard_map/ppermute | solution.py:144
  64.8 0.0 copy-done
  64.8 0.1 copy.12.place_ref
  65.0 3.6 %own.1 = (f32[512,512]{1,0:T(8,128)S(1)}, bf16[464,4096]{1,0:T(8,128)(2,1)S(1)}) custom-call(s32[512,1]{1,0:T(8,128)S(1)} %copy.12.place_ref, bf16[256,4096]{1,0:T(8,128)(2,1)S(1)} %bitcast.16, bf16[464,4096]{1,0:T(8,128)(2,1)} %bitcast.19), custom_call_target="tpu_custom_call" | custom-call | flops 973078528 | bytes 6291456 | tf_op jit(solution)/shard_map/own/pallas_call | solution.py:154
  68.6 0.4 collective-permute-done.far_ref
  69.1 3.4 %other.1 = s16[16,120,128]{2,1,0:T(8,128)(2,1)S(1)} custom-call(s32[1]{0:T(128)} %bitcast.1.core_ref, s32[512,1]{1,0:T(8,128)S(1)} %copy.12.place_ref, bf16[256,4096]{1,0:T(8,128)(2,1)} %collective-permute-done.far_ref, bf16[464,4096]{1,0:T(8,128)(2,1)S(1)} %get-tuple-element.7.w_ref, f32[512,512]{1,0:T(8,128)S(1)} %get-tuple-element.8.own_ref), custom_call_target="tpu_custom_call" | custom-call | flops 973078528 | bytes 6291456 | tf_op jit(solution)/shard_map/other/pallas_call | solution.py:164
  72.5 0.0 copy-start.1
  72.5 0.0 copy-start.2
  72.5 10.3 %all_to_all.28.in_ref = s16[4,4,120,128]{3,2,1,0:T(8,128)(2,1)S(1)} all-to-all(s16[4,4,120,128]{3,2,1,0:T(8,128)(2,1)S(1)} %bitcast.18), channel_id=1, replica_groups={{0,128,256,384},{32,160,288,416},{64,192,320,448},{96,224,352,480},{1,3..., dimensions={0} | all-to-all | bytes 983040 | tf_op jit(solution)/shard_map/all_to_all | solution.py:176
  82.8 0.8 turn.1
  83.6 3.7 %all-to-all-start.4 = ((s16[4,4,120,128]{3,2,1,0:T(8,128)(2,1)}), s16[4,4,120,128]{3,2,1,0:T(8,128)(2,1)S(1)}, u32[]{:S(2)}, u32[]{:S(2)}) async-start(s16[4,4,120,128]{3,2,1,0:T(8,128)(2,1)} %turn.1), calls=%async_computation.4 | async-start | bytes 983040 | tf_op jit(solution)/shard_map/all_to_all | solution.py:185
  87.3 0.0 copy-done.1
  87.3 0.0 copy-done.2
  87.3 0.2 select_reduce_fusion
  87.5 0.1 reshape.20
  87.6 0.1 copy.10
  87.7 0.1 reshape.21
  87.8 22.4 %all-to-all-done.4 = s16[4,4,120,128]{3,2,1,0:T(8,128)(2,1)S(1)} async-done(((s16[4,4,120,128]{3,2,1,0:T(8,128)(2,1)}), s16[4,4,120,128]{3,2,1,0:T(8,128)(2,1)S(1)}, u32[]{:S(2)}, u32[]{:S(2)}) %all-to-all-start.4) | async-done | bytes 491552 | tf_op jit(solution)/shard_map/all_to_all | solution.py:185
  110.2 2.0 %decode.1 = bf16[32,4,464]{2,1,0:T(4,128)(2,1)} custom-call(f32[4,16]{1,0:T(4,128)S(1)} %broadcast_select_fusion.coefficient_ref, s16[16,120,128]{2,1,0:T(8,128)(2,1)S(1)} %bitcast.17), custom_call_target="tpu_custom_call" | custom-call | tf_op jit(solution)/shard_map/decode/pallas_call | solution.py:192
  (4 shorter events, 0.1 us)
Async XLA Ops:
  43.2 21.6 %copy-start = (s32[512]{0:T(512)S(1)}, s32[512]{0:T(512)}, u32[]{:S(2)}) copy-start(s32[512]{0:T(512)} %param.9) | copy-start | bytes 6148
  62.9 6.2 %collective-permute-start = (bf16[256,4096]{1,0:T(8,128)(2,1)S(1)}, bf16[256,4096]{1,0:T(8,128)(2,1)}, u32[]{:S(2)}, u32[]{:S(2)}) collective-permute-start(bf16[256,4096]{1,0:T(8,128)(2,1)S(1)} %bitcast.15), channel_id=1, source_target_pairs={{0,1},{1,0},{2,3},{3,2},{4,5},{5,4},{6,7},{7,6},{8,9},{9,8},{10,11... | collective-permute-start | bytes 6291464 | tf_op jit(solution)/shard_map/ppermute | solution.py:144
  72.5 14.9 %copy-start.1 = (s32[4,16]{1,0:T(4,128)S(1)}, s32[4,16]{1,0:T(4,128)}, u32[]{:S(2)}) copy-start(s32[4,16]{1,0:T(4,128)} %param.7) | copy-start | bytes 772
  72.5 14.9 %copy-start.2 = (f32[16]{0:T(128)S(1)}, f32[16]{0:T(128)}, u32[]{:S(2)}) copy-start(f32[16]{0:T(128)} %param.8) | copy-start | bytes 196
  83.6 26.6 %all-to-all-start.4 = ((s16[4,4,120,128]{3,2,1,0:T(8,128)(2,1)}), s16[4,4,120,128]{3,2,1,0:T(8,128)(2,1)S(1)}, u32[]{:S(2)}, u32[]{:S(2)}) async-start(s16[4,4,120,128]{3,2,1,0:T(8,128)(2,1)} %turn.1), calls=%async_computation.4 | async-start | bytes 983040 | tf_op jit(solution)/shard_map/all_to_all | solution.py:185

commit v13 on v11

--- a/solution.py
+++ b/solution.py
@@ -92,7 +92,7 @@
             last = jnp.where(lane8 < 64, jnp.where(lane8 < 32, a, b), jnp.where(lane8 < 96, c, d))
             packed = jnp.concatenate([rows[:, :128], rows[:, 128:256], rows[:, 256:384], fold, last], axis=0)
             owner = at // 32 + block
-            to = jnp.where(core_ref[0] == 0, owner, owner % 4 * 4 + owner // 4)
+            to = jnp.where(core_ref[0] == 1, owner, owner % 4 * 4 + owner // 4)
             out_ref[to] = packed.astype(I32).astype(I16)
 
 
@@ -170,7 +170,7 @@
         cost_estimate=cost,
         name="other",
     )(core.astype(I32)[None], place, pltpu.with_memory_space_constraint(other, pltpu.HBM), w_here, codes)
-    got = lax.all_to_all(sent.reshape(4, 4, 120, 128), ("x", "zh", "c"), 0, 0, axis_index_groups=lines(0))
+    got = lax.all_to_all(sent.reshape(4, 4, 120, 128), ("x", "zh", "c"), 0, 0, axis_index_groups=lines(1))
     got = pl.pallas_call(
         turn_kernel,
         out_shape=jax.ShapeDtypeStruct(got.shape, I16),
@@ -179,13 +179,13 @@
         compiler_params=params,
         name="turn",
     )(got)
-    got = lax.all_to_all(got, ("x", "zh", "c"), 0, 0, axis_index_groups=lines(1)).reshape(16, 120, 128)
+    got = lax.all_to_all(got, ("x", "zh", "c"), 0, 0, axis_index_groups=lines(0)).reshape(16, 120, 128)
 
     entries = jnp.arange(coef_table.shape[0], dtype=I32)
     onehot = (cand_index[:, :, None] == entries[None, None, :]).astype(F32)
     coefficient = jnp.sum(onehot * coef_table[None, None, :], axis=2)
     turned = jnp.transpose(coefficient.reshape(4, 4, 4), (0, 2, 1)).reshape(4, 16)
-    coefficient = jnp.where(core == 0, turned, coefficient)
+    coefficient = jnp.where(core == 1, turned, coefficient)
     return pl.pallas_call(
         decode_kernel,
         out_shape=jax.ShapeDtypeStruct((32, 4, width), BF16),

time: 112 us -> 116 us (1.036)
  blocking collectives: 71.8 us -> 90.3 us
  waiting for transfers between devices: 19.3 us -> 7.85 us
  starting transfers between devices: 7.62 us -> 5.38 us
    all_to_all x1, blocking collectives: 10.4 us -> 29 us  [on_device(): lax.all_to_all(sent.reshape(4, 4, 120, 128), ('x', 'zh', 'c'), 0, 0, axis...]
    all_to_all x1, waiting for transfers between devices: 18.8 us -> 7.4 us  [on_device(): lax.all_to_all(got, ('x', 'zh', 'c'), 0, 0, axis_index_groups=lines(0))]
    all_to_all x1, starting transfers between devices: 5.71 us -> 3.47 us  [on_device(): lax.all_to_all(got, ('x', 'zh', 'c'), 0, 0, axis_index_groups=lines(0))]
where the time goes in v13:
time: 116 us; the launch traced here: 115 us
  blocking collectives  90.3 us (78%)
  Pallas kernels  9.83 us (8%)
  waiting for transfers between devices  7.85 us (7%)
  starting transfers between devices  5.38 us (5%)
    all_to_all x2, blocking collectives, spread(): lax.all_to_all(jnp.broadcast_to(block[None], (16,) + block.shape), axes,...  61.3 us
    all_to_all x1, blocking collectives, on_device(): lax.all_to_all(sent.reshape(4, 4, 120, 128), ('x', 'zh', 'c'), 0, 0, axis...  29 us
    all_to_all x1, waiting for transfers between devices, on_device(): lax.all_to_all(got, ('x', 'zh', 'c'), 0, 0, axis_index_groups=lines(0))  7.4 us
    pallas_call x1, Pallas kernels, on_device(): pl.pallas_call(own_kernel, out_shape=(jax.ShapeDtypeStruct((512, LANES),...  3.62 us
    all_to_all x1, starting transfers between devices, on_device(): lax.all_to_all(got, ('x', 'zh', 'c'), 0, 0, axis_index_groups=lines(0))  3.47 us
    pallas_call x1, Pallas kernels, on_device(): pl.pallas_call(other_kernel, out_shape=jax.ShapeDtypeStruct((16, 120, 128...  3.41 us
  transfers between devices with their start and end apart: 2, of which 2 were waited for; matrix products, arithmetic and copies ran while one was open for 1% of the time, Pallas kernels for 3%

profile of v13, /device:TPU:32, one launch (start us, length us, event | category | flops | bytes accessed | tf_op | source)
XLA Modules:
  0.0 115.2 jit_solution(4386521245692705565)
XLA Ops:
  0.0 0.8 reduce
  0.8 29.2 %all_to_all.20 = bf16[16,32,128]{2,1,0:T(8,128)(2,1)S(1)} all-to-all(bf16[16,32,128]{2,1,0:T(8,128)(2,1)S(1)} %broadcast_in_dim.36), channel_id=1, replica_groups=mesh['x'=4,'zh'=4,'y'=4,'zl'=4,'c'=2] {'zh','zl'}, dimensions={0} | all-to-all | bytes 262144 | tf_op jit(solution)/shard_map/all_to_all | solution.py:17
  30.0 0.1 copy.15
  30.1 0.2 broadcast_in_dim.38
  30.3 0.0 copy-start
  30.3 32.1 %all_to_all.21 = bf16[16,16,4096]{2,1,0:T(8,128)(2,1)S(1)} all-to-all(bf16[16,16,4096]{2,1,0:T(8,128)(2,1)S(1)} %broadcast_in_dim.38), channel_id=1, replica_groups=mesh['x'=4,'zh'=4,'y'=4,'zl'=4,'c'=2] {'x','y'}, dimensions={0} | all-to-all | bytes 4194304 | tf_op jit(solution)/shard_map/all_to_all | solution.py:17
  62.4 1.9 %collective-permute-start = (bf16[256,4096]{1,0:T(8,128)(2,1)S(1)}, bf16[256,4096]{1,0:T(8,128)(2,1)}, u32[]{:S(2)}, u32[]{:S(2)}) collective-permute-start(bf16[256,4096]{1,0:T(8,128)(2,1)S(1)} %bitcast.14), channel_id=1, source_target_pairs={{0,1},{1,0},{2,3},{3,2},{4,5},{5,4},{6,7},{7,6},{8,9},{9,8},{10,11... | collective-permute-start | bytes 6291464 | tf_op jit(solution)/shard_map/ppermute | solution.py:142
  64.4 0.0 copy-done
  64.4 0.1 copy.12.place_ref
  64.5 3.6 %own.1 = (f32[512,512]{1,0:T(8,128)S(1)}, bf16[464,4096]{1,0:T(8,128)(2,1)S(1)}) custom-call(s32[512,1]{1,0:T(8,128)S(1)} %copy.12.place_ref, bf16[256,4096]{1,0:T(8,128)(2,1)S(1)} %bitcast.15, bf16[464,4096]{1,0:T(8,128)(2,1)} %bitcast.18), custom_call_target="tpu_custom_call" | custom-call | flops 973078528 | bytes 6291456 | tf_op jit(solution)/shard_map/own/pallas_call | solution.py:151
  68.2 0.4 collective-permute-done.far_ref
  68.6 3.4 %other.1 = s16[16,120,128]{2,1,0:T(8,128)(2,1)S(1)} custom-call(s32[1]{0:T(128)} %bitcast.1.core_ref, s32[512,1]{1,0:T(8,128)S(1)} %copy.12.place_ref, bf16[256,4096]{1,0:T(8,128)(2,1)} %collective-permute-done.far_ref, bf16[464,4096]{1,0:T(8,128)(2,1)S(1)} %get-tuple-element.7.w_ref, f32[512,512]{1,0:T(8,128)S(1)} %get-tuple-element.8.own_ref), custom_call_target="tpu_custom_call" | custom-call | flops 973078528 | bytes 6291456 | tf_op jit(solution)/shard_map/other/pallas_call | solution.py:161
  72.0 0.0 copy-start.1
  72.0 0.0 copy-start.2
  72.1 29.0 %all_to_all.22.in_ref = s16[4,4,120,128]{3,2,1,0:T(8,128)(2,1)S(1)} all-to-all(s16[4,4,120,128]{3,2,1,0:T(8,128)(2,1)S(1)} %bitcast.17), channel_id=1, replica_groups={{1,129,257,385},{33,161,289,417},{65,193,321,449},{97,225,353,481},{0,3..., dimensions={0} | all-to-all | bytes 983040 | tf_op jit(solution)/shard_map/all_to_all | solution.py:173
  101.0 0.8 turn.1
  101.8 3.5 %all-to-all-start.3 = ((s16[4,4,120,128]{3,2,1,0:T(8,128)(2,1)}), s16[4,4,120,128]{3,2,1,0:T(8,128)(2,1)S(1)}, u32[]{:S(2)}, u32[]{:S(2)}) async-start(s16[4,4,120,128]{3,2,1,0:T(8,128)(2,1)} %turn.1), calls=%async_computation.3 | async-start | bytes 983040 | tf_op jit(solution)/shard_map/all_to_all | solution.py:182
  105.3 0.0 copy-done.1
  105.3 0.0 copy-done.2
  105.3 0.2 select_reduce_fusion
  105.5 0.1 reshape.19
  105.6 0.1 copy.10
  105.7 0.1 reshape.20
  105.8 7.4 %all-to-all-done.3 = s16[4,4,120,128]{3,2,1,0:T(8,128)(2,1)S(1)} async-done(((s16[4,4,120,128]{3,2,1,0:T(8,128)(2,1)}), s16[4,4,120,128]{3,2,1,0:T(8,128)(2,1)S(1)}, u32[]{:S(2)}, u32[]{:S(2)}) %all-to-all-start.3) | async-done | bytes 491552 | tf_op jit(solution)/shard_map/all_to_all | solution.py:182
  113.2 2.0 %decode.1 = bf16[32,4,464]{2,1,0:T(4,128)(2,1)} custom-call(f32[4,16]{1,0:T(4,128)S(1)} %broadcast_select_fusion.coefficient_ref, s16[16,120,128]{2,1,0:T(8,128)(2,1)S(1)} %bitcast.16), custom_call_target="tpu_custom_call" | custom-call | tf_op jit(solution)/shard_map/decode/pallas_call | solution.py:189
  (3 shorter events, 0.0 us)
Async XLA Ops:
  30.3 34.1 %copy-start = (s32[512]{0:T(512)S(1)}, s32[512]{0:T(512)}, u32[]{:S(2)}) copy-start(s32[512]{0:T(512)} %param.9) | copy-start | bytes 6148
  62.4 6.2 %collective-permute-start = (bf16[256,4096]{1,0:T(8,128)(2,1)S(1)}, bf16[256,4096]{1,0:T(8,128)(2,1)}, u32[]{:S(2)}, u32[]{:S(2)}) collective-permute-start(bf16[256,4096]{1,0:T(8,128)(2,1)S(1)} %bitcast.14), channel_id=1, source_target_pairs={{0,1},{1,0},{2,3},{3,2},{4,5},{5,4},{6,7},{7,6},{8,9},{9,8},{10,11... | collective-permute-start | bytes 6291464 | tf_op jit(solution)/shard_map/ppermute | solution.py:142
  72.0 33.3 %copy-start.1 = (s32[4,16]{1,0:T(4,128)S(1)}, s32[4,16]{1,0:T(4,128)}, u32[]{:S(2)}) copy-start(s32[4,16]{1,0:T(4,128)} %param.7) | copy-start | bytes 772
  72.0 33.3 %copy-start.2 = (f32[16]{0:T(128)S(1)}, f32[16]{0:T(128)}, u32[]{:S(2)}) copy-start(f32[16]{0:T(128)} %param.8) | copy-start | bytes 196
  101.8 11.3 %all-to-all-start.3 = ((s16[4,4,120,128]{3,2,1,0:T(8,128)(2,1)}), s16[4,4,120,128]{3,2,1,0:T(8,128)(2,1)S(1)}, u32[]{:S(2)}, u32[]{:S(2)}) async-start(s16[4,4,120,128]{3,2,1,0:T(8,128)(2,1)} %turn.1), calls=%async_computation.3 | async-start | bytes 983040 | tf_op jit(solution)/shard_map/all_to_all | solution.py:182

commit v14 on v12

--- a/solution.py
+++ b/solution.py
@@ -139,12 +139,12 @@
     core = lax.axis_index("c")
     w_piece = weights[0].T
     own = spread(calib_pool.reshape(32, 128), ("zh", "zl"), 16).reshape(16, 4096)
-    own = spread(own, ("x", "y", "c"), 4, lines(1)).reshape(64, 4096)
-    own = spread(own, ("x", "y", "c"), 4, lines(0)).reshape(256, 4096)
+    own = spread(own, ("x", "y", "c"), 4, lines(0)).reshape(64, 4096)
+    own = spread(own, ("x", "y", "c"), 4, lines(1)).reshape(256, 4096)
     other = lax.ppermute(own, "c", [(0, 1), (1, 0)])
 
     x, zh, y, zl, c = (row_ids >> 7) & 3, (row_ids >> 5) & 3, (row_ids >> 3) & 3, (row_ids >> 1) & 3, row_ids & 1
-    line = jnp.where(c == 0, x * 4 + y, y * 4 + x)
+    line = jnp.where(c == 1, x * 4 + y, y * 4 + x)
     place = ((line * 4 + zh) * 4 + zl + jnp.where(c == core, 0, 256))[:, None]
 
     width = w_piece.shape[0]

time: 113 us -> 113 us (level)
  no operation moved by 1% of the time
where the time goes in v14:
time: 113 us; the launch traced here: 112 us
  blocking collectives  72 us (64%)
  waiting for transfers between devices  22.9 us (20%)
  Pallas kernels  9.83 us (9%)
  starting transfers between devices  5.63 us (5%)
    all_to_all x3, blocking collectives, spread(): return lax.all_to_all(copies, axes, 0, 0, axis_index_groups=groups)  61.7 us
    all_to_all x1, waiting for transfers between devices, on_device(): lax.all_to_all(got, ('x', 'zh', 'c'), 0, 0, axis_index_groups=lines(1))  22.4 us
    all_to_all x1, blocking collectives, on_device(): lax.all_to_all(sent.reshape(4, 4, 120, 128), ('x', 'zh', 'c'), 0, 0, axis...  10.3 us
    all_to_all x1, starting transfers between devices, on_device(): lax.all_to_all(got, ('x', 'zh', 'c'), 0, 0, axis_index_groups=lines(1))  3.72 us
    pallas_call x1, Pallas kernels, on_device(): pl.pallas_call(own_kernel, out_shape=(jax.ShapeDtypeStruct((512, LANES),...  3.62 us
    pallas_call x1, Pallas kernels, on_device(): pl.pallas_call(other_kernel, out_shape=jax.ShapeDtypeStruct((16, 120, 128...  3.42 us
  transfers between devices with their start and end apart: 2, of which 2 were waited for; matrix products, arithmetic and copies ran while one was open for 1% of the time, Pallas kernels for 3%

profile of v14, /device:TPU:2, one launch (start us, length us, event | category | flops | bytes accessed | tf_op | source)
XLA Modules:
  0.0 112.2 jit_solution(7166431143529733476)
XLA Ops:
  0.0 0.8 reduce
  0.8 29.7 %all_to_all.25 = bf16[16,32,128]{2,1,0:T(8,128)(2,1)S(1)} all-to-all(bf16[16,32,128]{2,1,0:T(8,128)(2,1)S(1)} %broadcast_in_dim.43), channel_id=1, replica_groups=mesh['x'=4,'zh'=4,'y'=4,'zl'=4,'c'=2] {'zh','zl'}, dimensions={0} | all-to-all | bytes 262144 | tf_op jit(solution)/shard_map/all_to_all | solution.py:18
  30.5 0.1 copy.15
  30.6 11.3 %all_to_all.26 = bf16[4,16,4096]{2,1,0:T(8,128)(2,1)S(1)} all-to-all(bf16[4,16,4096]{2,1,0:T(8,128)(2,1)S(1)} %broadcast_in_dim.45), channel_id=1, replica_groups={{0,128,256,384},{8,136,264,392},{16,144,272,400},{24,152,280,408},{1,9,..., dimensions={0} | all-to-all | bytes 1048576 | tf_op jit(solution)/shard_map/all_to_all | solution.py:18
  41.8 0.2 broadcast_in_dim.47
  42.1 0.0 copy-start
  42.1 20.8 %all_to_all.27 = bf16[4,64,4096]{2,1,0:T(8,128)(2,1)S(1)} all-to-all(bf16[4,64,4096]{2,1,0:T(8,128)(2,1)S(1)} %broadcast_in_dim.47), channel_id=1, replica_groups={{1,129,257,385},{9,137,265,393},{17,145,273,401},{25,153,281,409},{0,8,..., dimensions={0} | all-to-all | bytes 4194304 | tf_op jit(solution)/shard_map/all_to_all | solution.py:18
  62.9 1.9 %collective-permute-start = (bf16[256,4096]{1,0:T(8,128)(2,1)S(1)}, bf16[256,4096]{1,0:T(8,128)(2,1)}, u32[]{:S(2)}, u32[]{:S(2)}) collective-permute-start(bf16[256,4096]{1,0:T(8,128)(2,1)S(1)} %bitcast.15), channel_id=1, source_target_pairs={{0,1},{1,0},{2,3},{3,2},{4,5},{5,4},{6,7},{7,6},{8,9},{9,8},{10,11... | collective-permute-start | bytes 6291464 | tf_op jit(solution)/shard_map/ppermute | solution.py:144
  64.8 0.0 copy-done
  64.8 0.1 copy.12.place_ref
  65.0 3.6 %own.1 = (f32[512,512]{1,0:T(8,128)S(1)}, bf16[464,4096]{1,0:T(8,128)(2,1)S(1)}) custom-call(s32[512,1]{1,0:T(8,128)S(1)} %copy.12.place_ref, bf16[256,4096]{1,0:T(8,128)(2,1)S(1)} %bitcast.16, bf16[464,4096]{1,0:T(8,128)(2,1)} %bitcast.19), custom_call_target="tpu_custom_call" | custom-call | flops 973078528 | bytes 6291456 | tf_op jit(solution)/shard_map/own/pallas_call | solution.py:154
  68.6 0.4 collective-permute-done.far_ref
  69.1 3.4 %other.1 = s16[16,120,128]{2,1,0:T(8,128)(2,1)S(1)} custom-call(s32[1]{0:T(128)} %bitcast.1.core_ref, s32[512,1]{1,0:T(8,128)S(1)} %copy.12.place_ref, bf16[256,4096]{1,0:T(8,128)(2,1)} %collective-permute-done.far_ref, bf16[464,4096]{1,0:T(8,128)(2,1)S(1)} %get-tuple-element.7.w_ref, f32[512,512]{1,0:T(8,128)S(1)} %get-tuple-element.8.own_ref), custom_call_target="tpu_custom_call" | custom-call | flops 973078528 | bytes 6291456 | tf_op jit(solution)/shard_map/other/pallas_call | solution.py:164
  72.5 0.0 copy-start.1
  72.5 0.0 copy-start.2
  72.5 10.3 %all_to_all.28.in_ref = s16[4,4,120,128]{3,2,1,0:T(8,128)(2,1)S(1)} all-to-all(s16[4,4,120,128]{3,2,1,0:T(8,128)(2,1)S(1)} %bitcast.18), channel_id=1, replica_groups={{0,128,256,384},{32,160,288,416},{64,192,320,448},{96,224,352,480},{1,3..., dimensions={0} | all-to-all | bytes 983040 | tf_op jit(solution)/shard_map/all_to_all | solution.py:176
  82.8 0.8 turn.1
  83.6 3.7 %all-to-all-start.4 = ((s16[4,4,120,128]{3,2,1,0:T(8,128)(2,1)}), s16[4,4,120,128]{3,2,1,0:T(8,128)(2,1)S(1)}, u32[]{:S(2)}, u32[]{:S(2)}) async-start(s16[4,4,120,128]{3,2,1,0:T(8,128)(2,1)} %turn.1), calls=%async_computation.4 | async-start | bytes 983040 | tf_op jit(solution)/shard_map/all_to_all | solution.py:185
  87.3 0.0 copy-done.1
  87.3 0.0 copy-done.2
  87.3 0.2 select_reduce_fusion
  87.5 0.1 reshape.20
  87.6 0.1 copy.10
  87.7 0.1 reshape.21
  87.8 22.4 %all-to-all-done.4 = s16[4,4,120,128]{3,2,1,0:T(8,128)(2,1)S(1)} async-done(((s16[4,4,120,128]{3,2,1,0:T(8,128)(2,1)}), s16[4,4,120,128]{3,2,1,0:T(8,128)(2,1)S(1)}, u32[]{:S(2)}, u32[]{:S(2)}) %all-to-all-start.4) | async-done | bytes 491552 | tf_op jit(solution)/shard_map/all_to_all | solution.py:185
  110.2 2.0 %decode.1 = bf16[32,4,464]{2,1,0:T(4,128)(2,1)} custom-call(f32[4,16]{1,0:T(4,128)S(1)} %broadcast_select_fusion.coefficient_ref, s16[16,120,128]{2,1,0:T(8,128)(2,1)S(1)} %bitcast.17), custom_call_target="tpu_custom_call" | custom-call | tf_op jit(solution)/shard_map/decode/pallas_call | solution.py:192
  (4 shorter events, 0.1 us)
Async XLA Ops:
  42.1 22.7 %copy-start = (s32[512]{0:T(512)S(1)}, s32[512]{0:T(512)}, u32[]{:S(2)}) copy-start(s32[512]{0:T(512)} %param.9) | copy-start | bytes 6148
  62.9 6.2 %collective-permute-start = (bf16[256,4096]{1,0:T(8,128)(2,1)S(1)}, bf16[256,4096]{1,0:T(8,128)(2,1)}, u32[]{:S(2)}, u32[]{:S(2)}) collective-permute-start(bf16[256,4096]{1,0:T(8,128)(2,1)S(1)} %bitcast.15), channel_id=1, source_target_pairs={{0,1},{1,0},{2,3},{3,2},{4,5},{5,4},{6,7},{7,6},{8,9},{9,8},{10,11... | collective-permute-start | bytes 6291464 | tf_op jit(solution)/shard_map/ppermute | solution.py:144
  72.5 14.9 %copy-start.1 = (s32[4,16]{1,0:T(4,128)S(1)}, s32[4,16]{1,0:T(4,128)}, u32[]{:S(2)}) copy-start(s32[4,16]{1,0:T(4,128)} %param.7) | copy-start | bytes 772
  72.5 14.9 %copy-start.2 = (f32[16]{0:T(128)S(1)}, f32[16]{0:T(128)}, u32[]{:S(2)}) copy-start(f32[16]{0:T(128)} %param.8) | copy-start | bytes 196
  83.6 26.6 %all-to-all-start.4 = ((s16[4,4,120,128]{3,2,1,0:T(8,128)(2,1)}), s16[4,4,120,128]{3,2,1,0:T(8,128)(2,1)S(1)}, u32[]{:S(2)}, u32[]{:S(2)}) async-start(s16[4,4,120,128]{3,2,1,0:T(8,128)(2,1)} %turn.1), calls=%async_computation.4 | async-start | bytes 983040 | tf_op jit(solution)/shard_map/all_to_all | solution.py:185
